TPU v7x, 128 devices: a whole 4x4x4 slice. The times are simulated.
128 devices in a mesh: dp: 32 (over y, x_lo, z), rep: 4 (over x_hi, core).
Axes of the slice: x: 4 (x_hi: 2, x_lo: 2; x = x_hi * 2 + x_lo), y: 4, z: 4, core: 2. Of those that a mesh axis runs over, the one named last changes fastest.
Arguments:
- images: bfloat16 [65536, 1152], P(('dp', 'rep')), may hold values from -1 to 1
- texts: bfloat16 [65536, 1152], P(('dp', 'rep')), may hold values from -1 to 1
- partner: int32 [65536], P(('dp', 'rep')), may hold values from 0 to 65535, as said below
- scale: float32 [1], replicated, may hold values from 1 to 3
- offset: float32 [1], replicated, may hold values from -2 to 0
Outputs:
- row_loss: float32 [65536], P(('dp', 'rep'))
- grad_images: bfloat16 [65536, 1152], P(('dp', 'rep'))
- grad_texts: bfloat16 [65536, 1152], P(('dp', 'rep'))
Inputs may be any that keep to these rules, and one draw needn't show every extreme that they name: partner[i] lies in the block of i or in the block before it, (k - 1) mod 32; index 0 has partner 65536 - 1 and index 1 has partner 0.
All inputs are finite; a program needn't handle non-finite values.
Results may differ from a plain program's by a relative error of at most 0.0041.
Values may be sent and summed in bfloat16 or wider, within the bound.
No kernel may reach another device: no remote copies, remote signals or barrier semaphores. Data moves between devices by JAX's collectives and lax.ppermute only.
A program may use at most 128 MiB of HBM per device.

v0:
```python
import jax
import jax.numpy as jnp
from jax import lax
from jax.sharding import PartitionSpec as P


def from_behind(block, axis, distance):
    devices = range(lax.axis_size(axis))
    route = [((i - distance) % len(devices), i) for i in devices]
    return lax.ppermute(block, axis, route)


def block_terms(image_rows, text_rows, partner_rows, start, temper, shift_bias):
    logits = (
        temper * jnp.dot(image_rows, text_rows.T, preferred_element_type=jnp.float32) + shift_bias
    )
    columns = start + jnp.arange(text_rows.shape[0], dtype=jnp.int32)
    sign = jnp.where(partner_rows[:, None] == columns[None, :], 1.0, -1.0).astype(jnp.float32)
    loss_sum = jnp.sum(jax.nn.softplus(-sign * logits), axis=1)
    coef = (-temper * sign * jax.nn.sigmoid(-sign * logits)).astype(jnp.bfloat16)
    grad_img = jnp.dot(coef, text_rows, preferred_element_type=jnp.float32)
    grad_txt = lax.dot_general(
        coef, image_rows, (((0,), (0,)), ((), ())), preferred_element_type=jnp.float32
    )
    return (loss_sum, grad_img, grad_txt)


def body(images, texts, partner, scale, offset):
    temper = scale[0]
    shift_bias = offset[0]
    n_cycle = lax.axis_size("dp")
    n_group = lax.axis_size("rep")
    block_len = texts.shape[0] * n_group
    position = lax.axis_index("dp")
    own_block = lax.all_gather(texts, "rep", axis=0, tiled=True)
    prev_block = from_behind(own_block, "dp", 1)
    own_start = position * block_len
    prev_start = (position + n_cycle - 1) % n_cycle * block_len
    loss_own, gimg_own, acc_own = block_terms(
        images, own_block, partner, own_start, temper, shift_bias
    )
    loss_prev, gimg_prev, acc_prev = block_terms(
        images, prev_block, partner, prev_start, temper, shift_bias
    )
    row_loss = (loss_own + loss_prev) / jnp.float32(2 * block_len)
    grad_images = (gimg_own + gimg_prev).astype(jnp.bfloat16)
    returned = from_behind(acc_prev, "dp", -1)
    grad_rows = lax.psum_scatter(acc_own + returned, "rep", scatter_dimension=0, tiled=True)
    return (row_loss, grad_images, grad_rows.astype(jnp.bfloat16))


def solution(mesh):
    in_specs = (P(("dp", "rep"), None), P(("dp", "rep"), None), P(("dp", "rep")), P(), P())
    out_specs = (P(("dp", "rep")), P(("dp", "rep"), None), P(("dp", "rep"), None))
    return jax.shard_map(body, mesh=mesh, in_specs=in_specs, out_specs=out_specs, check_vma=False)
```

profile of v0, /device:TPU:0, one launch (start us, length us, event | category | flops | bytes accessed | tf_op | source)
XLA Modules:
  0.0 481.6 jit_solution(14889163961158298494)
XLA Ops:
  7.2 0.0 copy-start
  7.2 0.0 all-gather.2.cloned.1.call-start
  7.2 0.7 all-gather.2.cloned.1.call-update
  7.9 0.0 reduce-scatter.2.cloned.1.call-start
  8.0 45.7 %all-gather.2.cloned.1.call-done = bf16[2048,1152]{1,0:T(8,128)(2,1)} async-done(((bf16[512,1152]{1,0:T(8,128)(2,1)}), bf16[2048,1152]{1,0:T(8,128)(2,1)}) %all-gather.2.cloned.1.call-update) | async-done | bytes 4718608 | tf_op jit(solution)/shard_map/all_gather | solution.py:35
  53.7 1.6 collective-permute-start
  56.5 105.6 %collective-permute-done = bf16[2048,1152]{1,0:T(8,128)(2,1)} collective-permute-done((bf16[2048,1152]{1,0:T(8,128)(2,1)}, bf16[2048,1152]{1,0:T(8,128)(2,1)}, u32[]{:S(2)}, u32[]{:S(2)}) %collective-permute-start) | collective-permute-done | bytes 4718624 | tf_op jit(solution)/shard_map/ppermute | solution.py:10
  162.2 0.0 copy-done
  162.2 0.0 copy-start.1
  162.2 7.0 %fusion.7 = (f32[512]{0:T(512)S(1)}, f32[512,2048]{1,0:T(8,128)S(1)}) fusion(f32[]{:T(128)} %bitcast.14, bf16[512,1152]{1,0:T(8,128)(2,1)S(1)} %copy-done, bf16[2048,1152]{1,0:T(8,128)(2,1)} %collective-permute-done, f32[]{:T(128)} %bitcast.12, s32[2048]{0:T(1024)S(1)} %iota_add_fusion, s32[512]{0:T(512)} %param.7), kind=kOutput, calls=%fused_computation.14 | convolution fusion | flops 2429550080 | bytes 10104840 | tf_op jit(solution)/shard_map/dot_general | solution.py:15
  169.2 0.0 copy-start.3
  169.2 0.0 copy-done.1
  169.2 5.7 %fusion.9 = f32[2048,1152]{1,0:T(8,128)} fusion(bf16[512,1152]{1,0:T(8,128)(2,1)S(1)} %copy-done, f32[512,2048]{1,0:T(8,128)S(1)} %get-tuple-element.6, f32[]{:T(128)S(6)} %neg.29, s32[2048]{0:T(1024)S(1)} %iota_add_fusion, s32[512]{0:T(512)S(1)} %copy-done.1), kind=kOutput, calls=%fused_computation.20 | convolution fusion | flops 2424307712 | bytes 14821380 | tf_op jit(solution)/shard_map/dot_general | solution.py:22
  174.9 0.0 copy-done.3
  174.9 0.9 collective-permute-start.1
  175.8 6.8 %fusion.6 = (f32[512]{0:T(512)S(1)}, f32[512,2048]{1,0:T(8,128)S(1)}) fusion(f32[]{:T(128)} %bitcast.13, bf16[512,1152]{1,0:T(8,128)(2,1)S(1)} %copy-done, bf16[2048,1152]{1,0:T(8,128)(2,1)} %all-gather.2.cloned.1.call-done, f32[]{:T(128)} %bitcast.10, s32[2048]{0:T(1024)S(1)} %iota_add_fusion.1, s32[512]{0:T(512)S(1)} %copy-done.1), kind=kOutput, calls=%fused_computation.13 | convolution fusion | flops 2429550080 | bytes 10104840 | tf_op jit(solution)/shard_map/dot_general | solution.py:15
  182.7 0.0 copy-start.2
  182.7 196.8 %collective-permute-done.1 = f32[2048,1152]{1,0:T(8,128)} collective-permute-done((f32[2048,1152]{1,0:T(8,128)}, f32[2048,1152]{1,0:T(8,128)}, u32[]{:S(2)}, u32[]{:S(2)}) %collective-permute-start.1) | collective-permute-done | bytes 9437216 | tf_op jit(solution)/shard_map/ppermute | solution.py:10
  379.5 0.0 copy-done.2
  379.5 8.0 %convolution_add_fusion = f32[2048,1152]{1,0:T(8,128)} fusion(f32[2048,1152]{1,0:T(8,128)} %collective-permute-done.1, bf16[512,1152]{1,0:T(8,128)(2,1)S(1)} %copy-done, f32[512,2048]{1,0:T(8,128)S(1)} %get-tuple-element.4, f32[]{:T(128)S(6)} %neg.29, s32[2048]{0:T(1024)S(1)} %iota_add_fusion.1, s32[512]{0:T(512)S(1)} %copy-done.1), kind=kOutput, calls=%fused_computation.2 | convolution fusion | flops 2426667008 | bytes 24258564 | tf_op jit(solution)/shard_map/dot_general | solution.py:22
  387.5 0.0 reduce-scatter.2.cloned.1.call-update
  387.5 0.0 copy-start.4
  387.5 6.4 %fusion.13 = f32[512,1152]{1,0:T(8,128)S(1)} fusion(bf16[2048,1152]{1,0:T(8,128)(2,1)} %all-gather.2.cloned.1.call-done, f32[512,2048]{1,0:T(8,128)} %copy-done.2, f32[]{:T(128)S(6)} %neg.29, s32[2048]{0:T(1024)S(1)} %iota_add_fusion.1, s32[512]{0:T(512)S(1)} %copy-done.1), kind=kOutput, calls=%fused_computation.21 | convolution fusion | flops 2424307712 | bytes 11282436 | tf_op jit(solution)/shard_map/dot_general | solution.py:21
  394.0 0.6 add_multiply_fusion
  394.5 0.0 copy-done.4
  394.6 6.6 %fusion.8 = bf16[512,1152]{1,0:T(8,128)(2,1)} fusion(f32[512,1152]{1,0:T(8,128)S(1)} %fusion.13, bf16[2048,1152]{1,0:T(8,128)(2,1)} %collective-permute-done, f32[512,2048]{1,0:T(8,128)S(1)} %copy-done.4, f32[]{:T(128)S(6)} %neg.29, s32[2048]{0:T(1024)S(1)} %iota_add_fusion, s32[512]{0:T(512)S(1)} %copy-done.1), kind=kOutput, calls=%fused_computation.16 | convolution fusion | flops 2425487360 | bytes 12462084 | tf_op jit(solution)/shard_map/dot_general | solution.py:21
  401.1 70.8 %reduce-scatter.2.cloned.1.call-done = f32[512,1152]{1,0:T(8,128)} async-done(((f32[2048,1152]{1,0:T(8,128)}), f32[512,1152]{1,0:T(8,128)}) %reduce-scatter.2.cloned.1.call-update) | async-done | bytes 2359312 | tf_op jit(solution)/shard_map/reduce_scatter | solution.py:48
  472.0 2.8 convert_element_type.15
  (2 shorter events, 0.0 us)
Async XLA Ops:
  7.2 155.0 %copy-start = (bf16[512,1152]{1,0:T(8,128)(2,1)S(1)}, bf16[512,1152]{1,0:T(8,128)(2,1)}, u32[]{:S(2)}) copy-start(bf16[512,1152]{1,0:T(8,128)(2,1)} %param.5) | copy-start | bytes 3538948
  7.2 46.5 %all-gather.2.cloned.1.call-start = ((), (), s32[]{:S(2)}) async-start(), calls=%async_computation.1 | async-start | bytes 5898240 | tf_op jit(solution)/shard_map/all_gather | solution.py:35
  7.9 464.1 %reduce-scatter.2.cloned.1.call-start = ((), (), s32[]{:S(2)}) async-start(), calls=%async_computation.2 | async-start | bytes 11796480 | tf_op jit(solution)/shard_map/reduce_scatter | solution.py:48
  53.7 108.5 %collective-permute-start = (bf16[2048,1152]{1,0:T(8,128)(2,1)}, bf16[2048,1152]{1,0:T(8,128)(2,1)}, u32[]{:S(2)}, u32[]{:S(2)}) collective-permute-start(bf16[2048,1152]{1,0:T(8,128)(2,1)} %all-gather.2.cloned.1.call-done), channel_id=1, source_target_pairs={{124,0},{0,4},{4,8},{8,12},{12,16},{16,20},{20,24},{24,28},{28,32}... | collective-permute-start | bytes 14155784 | tf_op jit(solution)/shard_map/ppermute | solution.py:10
  162.2 7.0 %copy-start.1 = (s32[512]{0:T(512)S(1)}, s32[512]{0:T(512)}, u32[]{:S(2)}) copy-start(s32[512]{0:T(512)} %param.7) | copy-start | bytes 6148
  169.2 5.7 %copy-start.3 = (f32[512,2048]{1,0:T(8,128)}, f32[512,2048]{1,0:T(8,128)S(1)}, u32[]{:S(2)}) copy-start(f32[512,2048]{1,0:T(8,128)S(1)} %get-tuple-element.6) | copy-start | bytes 12582916
  174.9 204.6 %collective-permute-start.1 = (f32[2048,1152]{1,0:T(8,128)}, f32[2048,1152]{1,0:T(8,128)}, u32[]{:S(2)}, u32[]{:S(2)}) collective-permute-start(f32[2048,1152]{1,0:T(8,128)} %fusion.9), channel_id=1, source_target_pairs={{4,0},{8,4},{12,8},{16,12},{20,16},{24,20},{28,24},{32,28},{36,32}... | collective-permute-start | bytes 28311560 | tf_op jit(solution)/shard_map/ppermute | solution.py:10
  182.7 196.8 %copy-start.2 = (f32[512,2048]{1,0:T(8,128)}, f32[512,2048]{1,0:T(8,128)S(1)}, u32[]{:S(2)}) copy-start(f32[512,2048]{1,0:T(8,128)S(1)} %get-tuple-element.4) | copy-start | bytes 12582916
  387.5 7.0 %copy-start.4 = (f32[512,2048]{1,0:T(8,128)S(1)}, f32[512,2048]{1,0:T(8,128)}, u32[]{:S(2)}) copy-start(f32[512,2048]{1,0:T(8,128)} %copy-done.3) | copy-start | bytes 12582916
Sparse Core Ops, SparseCore 0:
  9.7 43.9 all-gather.1
  387.6 84.2 reduce-scatter.1
where the time goes:
time: 483 us; the launch traced here: 482 us
  waiting for transfers between devices  420 us (87%)
  matrix products  40.6 us (8%)
  between operations  15.4 us (3%)
    ppermute x2, waiting for transfers between devices, from_behind(): return lax.ppermute(block, axis, route)  302 us
    reduce_scatter x1, waiting for transfers between devices, body(): lax.psum_scatter(acc_own + returned, 'rep', scatter_dimension=0, tiled=True)  70.8 us
    all_gather x1, waiting for transfers between devices, body(): own_block = lax.all_gather(texts, 'rep', axis=0, tiled=True)  45.7 us
    dot_general x2, matrix products, block_terms(): jnp.dot(image_rows, text_rows.T, preferred_element_type=jnp.float32)  13.9 us
    dot_general x2, matrix products, block_terms(): lax.dot_general(coef, image_rows, (((0,), (0,)), ((), ())), preferred_ele...  13.7 us
    dot_general x2, matrix products, block_terms(): grad_img = jnp.dot(coef, text_rows, preferred_element_type=jnp.float32)  13 us
  transfers between devices with their start and end apart: 4, of which 4 were waited for; matrix products, arithmetic and copies ran while one was open for 4% of the time, Pallas kernels for 0%

commit v1 on v0

v1 whole, which is shorter than its diff:
```python
import functools
import jax
import jax.numpy as jnp
from jax import lax
from jax.experimental import pallas as pl
from jax.experimental.pallas import tpu as pltpu
from jax.sharding import PartitionSpec as P

AXES = ("dp", "rep")
NT = (((1,), (1,)), ((), ()))
TN = (((0,), (0,)), ((), ()))


def place(flat):
    dp, rep = divmod(flat, 4)
    return dp // 8, (rep // 2) * 2 + (dp // 4) % 2, dp % 4, rep % 2


def flat_of(y, x, z, core):
    return (y * 8 + (x % 2) * 4 + z) * 4 + (x // 2) * 2 + core


def moved(x=0, z=0, core=0):
    route = []
    for source in range(128):
        sy, sx, sz, sc = place(source)
        route.append((source, flat_of(sy, (sx + x) % 4, (sz + z) % 4, (sc + core) % 2)))
    return route


def along_loop(step):
    return [(source, (source + 4 * step) % 128) for source in range(128)]


def send(block, route):
    return lax.ppermute(block, AXES, route)


def shifted(block, step, head):
    along_z = dict(moved(z=step))
    turn = 3 if step > 0 else 0
    hop = [(along_z[s], d) for s, d in along_loop(step) if place(s)[2] == turn]
    first = send(block[:head], moved(z=step))
    rest = send(block[head:], along_loop(step))
    turned = send(first, hop)
    here = lax.axis_index("dp") % 4 == (turn + step) % 4
    return jnp.concatenate([jnp.where(here, turned, first), rest])


def terms(dots, positive, temper, shift):
    logit = temper * dots + shift
    z = jnp.where(positive, -logit, logit)
    e = jnp.exp(-jnp.abs(z))
    log_term = jnp.where(e < 1e-4, e, jnp.log(1.0 + e))
    loss = jnp.maximum(z, 0.0) + log_term
    sigmoid = jnp.exp(jnp.minimum(z, 0.0) - log_term)
    coef = (jnp.where(positive, -temper, temper) * sigmoid).astype(jnp.bfloat16)
    return loss, coef


def pair_body(n, has_gi, has_gt, tile, start_ref, scale_ref, offset_ref, *refs):
    imgs, parts, txt, refs = refs[:n], refs[n : 2 * n], refs[2 * n], refs[2 * n + 1 :]
    if has_gi:
        gi_in, loss_in, refs = refs[:n], refs[n : 2 * n], refs[2 * n :]
    if has_gt:
        gt_in, refs = refs[0], refs[1:]
    gi, loss, gt = refs[:n], refs[n : 2 * n], refs[2 * n]
    step = pl.program_id(0)
    temper, shift = scale_ref[0], offset_ref[0]

    @pl.when(step == 0)
    def _():
        for m in range(n):
            if has_gi:
                gi[m][...] = gi_in[m][...]
                loss[m][...] = loss_in[m][...]
            else:
                gi[m][...] = jnp.zeros_like(gi[m])
                loss[m][...] = jnp.zeros_like(loss[m])

    t = txt[...]
    rows = imgs[0].shape[0]
    col = start_ref[0] + step * tile + lax.broadcasted_iota(jnp.int32, (tile, rows), 0)
    acc = gt_in[...].astype(jnp.float32) if has_gt else None
    for m in range(n):
        a = imgs[m][...]
        dots = lax.dot_general(t, a, NT, preferred_element_type=jnp.float32)
        ls, coef = terms(dots, parts[m][...] == col, temper, shift)
        loss[m][...] += jnp.sum(ls, axis=0, keepdims=True)
        gi[m][...] += lax.dot_general(coef, t, TN, preferred_element_type=jnp.float32)
        g = jnp.dot(coef, a, preferred_element_type=jnp.float32)
        acc = g if acc is None else acc + g
    gt[...] = acc.astype(gt.dtype)


def pairs(imgs, parts, txt, start, scale, offset, gi=None, loss=None, gt=None, gt_dtype=jnp.float32, tile=512):
    n, (rows, d), nt = len(imgs), imgs[0].shape, txt.shape[0]
    smem = pl.BlockSpec(memory_space=pltpu.SMEM)
    tiled = pl.BlockSpec((tile, d), lambda i: (i, 0))

    def whole(r, c):
        return pl.BlockSpec((r, c), lambda i: (0, 0))

    in_specs = [smem] * 3 + [whole(rows, d)] * n + [whole(1, rows)] * n + [tiled]
    args = [start.astype(jnp.int32)[None], scale, offset, *imgs, *parts, txt]
    if gi is not None:
        in_specs += [whole(rows, d)] * n + [whole(1, rows)] * n
        args += [*gi, *loss]
    if gt is not None:
        in_specs += [tiled]
        args += [gt]
    outs = pl.pallas_call(
        functools.partial(pair_body, n, gi is not None, gt is not None, tile),
        grid=(nt // tile,),
        in_specs=in_specs,
        out_specs=[whole(rows, d)] * n + [whole(1, rows)] * n + [tiled],
        out_shape=[jax.ShapeDtypeStruct((rows, d), jnp.float32)] * n
        + [jax.ShapeDtypeStruct((1, rows), jnp.float32)] * n
        + [jax.ShapeDtypeStruct((nt, d), gt_dtype)],
        compiler_params=pltpu.CompilerParams(vmem_limit_bytes=48 << 20),
        cost_estimate=pl.CostEstimate(
            flops=6 * n * rows * nt * d, bytes_accessed=nt * d * 8 + n * rows * d * 8, transcendentals=3 * n * rows * nt
        ),
    )(*args)
    return outs[:n], outs[n : 2 * n], outs[2 * n]


def body(images, texts, partner, scale, offset):
    dp, rep = lax.axis_index("dp"), lax.axis_index("rep")
    rows = texts.shape[0]

    def start(other_chip, other_core):
        c, b = rep // 2, rep % 2
        return (dp * 4 + (c ^ other_chip) * 2 + (b ^ other_core)) * rows

    swap = moved(core=1)
    across = moved(x=2)
    near_far = send(texts, swap)
    visitor = shifted(images, -1, 256)
    far = send(texts, across)
    visitor_partner = send(partner, along_loop(-1))
    far_far = send(far, swap)
    pa, pb = partner[None, :], visitor_partner[None, :]
    (ga,), (la,), gs = pairs([images], [pa], texts, start(0, 0), scale, offset)
    (ga,), (la,), gs_far = pairs([images], [pa], near_far, start(0, 1), scale, offset, [ga], [la])
    (gb,), (lb,), gs = pairs([visitor], [pb], texts, start(0, 0), scale, offset, gt=gs)
    (gb,), (lb,), gs_far = pairs([visitor], [pb], near_far, start(0, 1), scale, offset, [gb], [lb], gt=gs_far)
    (ga, gb), (la, lb), gu_far = pairs(
        [images, visitor], [pa, pb], far_far, start(1, 1), scale, offset, [ga, gb], [la, lb], gt_dtype=jnp.bfloat16
    )
    gu_got = send(gu_far, swap)
    (ga, gb), (la, lb), gu = pairs(
        [images, visitor], [pa, pb], far, start(1, 0), scale, offset, [ga, gb], [la, lb], gt=gu_got
    )
    back = shifted(gb.astype(jnp.bfloat16), 1, 256)
    back_loss = send(lb[0], along_loop(1))
    gu_back = send(gu.astype(jnp.bfloat16), across)
    gs_got = send(gs_far, swap)
    row_loss = (la[0] + back_loss) / jnp.float32(8 * rows)
    grad_images = (ga + back.astype(jnp.float32)).astype(jnp.bfloat16)
    grad_texts = (gs + gs_got + gu_back.astype(jnp.float32)).astype(jnp.bfloat16)
    return row_loss, grad_images, grad_texts


def solution(mesh):
    in_specs = (P(AXES, None), P(AXES, None), P(AXES), P(), P())
    out_specs = (P(AXES), P(AXES, None), P(AXES, None))
    return jax.shard_map(body, mesh=mesh, in_specs=in_specs, out_specs=out_specs, check_vma=False)
```

time: 483 us -> 163 us (0.34)
  waiting for transfers between devices: 420 us -> 74.2 us
  Pallas kernels: 0 us -> 45.3 us
  matrix products: 40.6 us -> 0 us
  starting transfers between devices: 2.54 us -> 22.5 us
  between operations: 15.4 us -> 2.08 us
  local copies, waits for them, and re-layouts: 0.03 us -> 9.45 us
  other arithmetic: 3.39 us -> 9.22 us
    ppermute x2 -> x14, waiting for transfers between devices: 302 us -> 74.2 us  [send(): return lax.ppermute(block, AXES, route)]
    reduce_scatter x1 -> x0, waiting for transfers between devices: 70.8 us -> none  [body(): lax.psum_scatter(acc_own + returned, 'rep', scatter_dimension=0, tiled=True)]
    all_gather x1 -> x0, waiting for transfers between devices: 45.7 us -> none  [body(): own_block = lax.all_gather(texts, 'rep', axis=0, tiled=True)]
    pallas_call x0 -> x6, Pallas kernels: none -> 45.3 us  [pairs(): pl.pallas_call(functools.partial(pair_body, n, gi is not None, gt is not...]
    dot_general x6 -> x0, matrix products: 40.6 us -> none  [the longest x2 13.9 us: block_terms(): jnp.dot(image_rows, text_rows.T, preferred_element_type=jnp.float32)]
    ppermute x2 -> x14, starting transfers between devices: 2.47 us -> 22.5 us  [send(): return lax.ppermute(block, AXES, route)]
    unnamed x10 -> x22, local copies, waits for them, and re-layouts: 0.03 us -> 8.03 us
  transfers between devices with their start and end apart: 4 -> 14, of which waited for: 4 -> 8; matrix products, arithmetic and copies ran while one was open for 4% -> 5% of each run, Pallas kernels for 0% -> 22%
where the time goes in v1:
time: 163 us
  waiting for transfers between devices  74.2 us (46%)
  Pallas kernels  45.3 us (28%)
  starting transfers between devices  22.5 us (14%)
  local copies, waits for them, and re-layouts  9.45 us (6%)
  other arithmetic  9.22 us (6%)
  between operations  2.08 us (1%)
    ppermute x14, waiting for transfers between devices, send(): return lax.ppermute(block, AXES, route)  74.2 us
    pallas_call x6, Pallas kernels, pairs(): pl.pallas_call(functools.partial(pair_body, n, gi is not None, gt is not...  45.3 us
    ppermute x14, starting transfers between devices, send(): return lax.ppermute(block, AXES, route)  22.5 us
    unnamed x22, local copies, waits for them, and re-layouts  8.03 us
  transfers between devices with their start and end apart: 14, of which 8 were waited for; matrix products, arithmetic and copies ran while one was open for 5% of the time, Pallas kernels for 22%

profile of v1, /device:TPU:0, one launch (start us, length us, event | category | flops | bytes accessed | tf_op | source)
XLA Modules:
  0.0 162.7 jit_solution(13763586783501248941)
XLA Ops:
  0.6 3.2 %collective-permute-start.4 = (bf16[512,1152]{1,0:T(8,128)(2,1)}, bf16[512,1152]{1,0:T(8,128)(2,1)}, u32[]{:S(2)}, u32[]{:S(2)}) collective-permute-start(bf16[512,1152]{1,0:T(8,128)(2,1)} %refs_2_.3), channel_id=1, source_target_pairs={{0,2},{1,3},{2,0},{3,1},{4,6},{5,7},{6,4},{7,5},{8,10},{9,11},{10,... | collective-permute-start | bytes 3538952 | tf_op jit(solution)/shard_map/ppermute | solution.py:36
  3.8 1.3 fusion.1
  5.2 4.1 %collective-permute-start = (bf16[256,1152]{1,0:T(8,128)(2,1)S(1)}, bf16[256,1152]{1,0:T(8,128)(2,1)S(1)}, u32[]{:S(2)}, u32[]{:S(2)}) collective-permute-start(bf16[256,1152]{1,0:T(8,128)(2,1)S(1)} %get-tuple-element.49), channel_id=1, source_target_pairs={{0,12},{1,13},{2,14},{3,15},{4,0},{5,1},{6,2},{7,3},{8,4},{9,5},{1... | collective-permute-start | bytes 1769480 | tf_op jit(solution)/shard_map/ppermute | solution.py:36
  9.3 12.3 %collective-permute-done = bf16[256,1152]{1,0:T(8,128)(2,1)S(1)} collective-permute-done((bf16[256,1152]{1,0:T(8,128)(2,1)S(1)}, bf16[256,1152]{1,0:T(8,128)(2,1)S(1)}, u32[]{:S(2)}, u32[]{:S(2)}) %collective-permute-start) | collective-permute-done | bytes 589856 | tf_op jit(solution)/shard_map/ppermute | solution.py:36
  21.6 1.5 collective-permute-start.1
  23.1 0.0 collective-permute-start.6
  23.1 8.2 %collective-permute-start.3 = (s32[512]{0:T(512)S(1)}, s32[512]{0:T(512)S(1)}, u32[]{:S(2)}, u32[]{:S(2)}) collective-permute-start(s32[512]{0:T(512)S(1)} %copy-done.5), channel_id=1, source_target_pairs={{0,124},{1,125},{2,126},{3,127},{4,0},{5,1},{6,2},{7,3},{8,4},{9,5... | collective-permute-start | bytes 6152 | tf_op jit(solution)/shard_map/ppermute | solution.py:36
  31.3 0.1 collective-permute-start.2
  32.7 5.8 %shard_map.76 = (f32[512,1152]{1,0:T(8,128)S(1)}, f32[1,512]{1,0:T(1,128)S(1)}, f32[512,1152]{1,0:T(8,128)}) custom-call(s32[1]{0:T(128)} %bitcast.5.start_ref, f32[1]{0:T(128)S(6)} %copy.8.scale_ref, f32[1]{0:T(128)S(6)} %copy.9.offset_ref, bf16[512,1152]{1,0:T(8,128)(2,1)S(1)} %copy-done.1, s32[1,512]{1,0:T(1,128)S(1)} %bitcast.13, bf16[512,1152]{1,0:T(8,128)(2,1)} %refs_2_.3), custom_call_target="tpu_custom_call" | custom-call | flops 1811939328 | bytes 9437184 | tf_op jit(solution)/shard_map/pallas_call | solution.py:112
  38.5 1.4 copy-done.6
  39.9 0.0 collective-permute-done.4.refs_4_
  39.9 0.1 collective-permute-start.5
  40.0 0.0 collective-permute-done.1
  40.0 0.1 broadcast_select_fusion.1
  40.1 6.7 %collective-permute-done.2 = bf16[256,1152]{1,0:T(8,128)(2,1)} collective-permute-done((bf16[256,1152]{1,0:T(8,128)(2,1)S(1)}, bf16[256,1152]{1,0:T(8,128)(2,1)}, u32[]{:S(2)}, u32[]{:S(2)}) %collective-permute-start.2) | collective-permute-done | bytes 589856 | tf_op jit(solution)/shard_map/ppermute | solution.py:36
  46.8 1.2 pad_maximum_fusion.refs_0_.refs_1_
  47.9 0.0 collective-permute-done.3
  47.9 6.4 %shard_map.78 = (f32[512,1152]{1,0:T(8,128)S(1)}, f32[1,512]{1,0:T(1,128)S(1)}, f32[512,1152]{1,0:T(8,128)}) custom-call(s32[1]{0:T(128)} %bitcast.5.start_ref, f32[1]{0:T(128)S(6)} %copy.8.scale_ref, f32[1]{0:T(128)S(6)} %copy.9.offset_ref, bf16[512,1152]{1,0:T(8,128)(2,1)S(1)} %pad_maximum_fusion.refs_0_.refs_1_, s32[1,512]{1,0:T(1,128)S(1)} %bitcast.8, ...), custom_call_target="tpu_custom_call" | custom-call | flops 1811939328 | bytes 9437184 | tf_op jit(solution)/shard_map/pallas_call | solution.py:112
  54.4 1.4 copy-done
  55.8 0.0 collective-permute-done.6.refs_2_
  55.8 6.2 %shard_map.77 = (f32[512,1152]{1,0:T(8,128)S(1)}, f32[1,512]{1,0:T(1,128)S(1)}, f32[512,1152]{1,0:T(8,128)}) custom-call(s32[1]{0:T(128)} %bitcast.4.start_ref, f32[1]{0:T(128)S(6)} %copy.8.scale_ref, f32[1]{0:T(128)S(6)} %copy.9.offset_ref, bf16[512,1152]{1,0:T(8,128)(2,1)S(1)} %copy-done.1, s32[1,512]{1,0:T(1,128)S(1)} %bitcast.14, ...), custom_call_target="tpu_custom_call" | custom-call | flops 1811939328 | bytes 9437184 | tf_op jit(solution)/shard_map/pallas_call | solution.py:112
  61.9 1.4 copy-done.7
  63.4 6.8 %shard_map.79 = (f32[512,1152]{1,0:T(8,128)S(1)}, f32[1,512]{1,0:T(1,128)S(1)}, f32[512,1152]{1,0:T(8,128)}) custom-call(s32[1]{0:T(128)} %bitcast.4.start_ref, f32[1]{0:T(128)S(6)} %copy.8.scale_ref, f32[1]{0:T(128)S(6)} %copy.9.offset_ref, bf16[512,1152]{1,0:T(8,128)(2,1)S(1)} %pad_maximum_fusion.refs_0_.refs_1_, s32[1,512]{1,0:T(1,128)S(1)} %bitcast.9, ...), custom_call_target="tpu_custom_call" | custom-call | flops 1811939328 | bytes 9437184 | tf_op jit(solution)/shard_map/pallas_call | solution.py:112
  70.2 1.5 copy-done.2
  71.7 10.2 %shard_map.80 = (f32[512,1152]{1,0:T(8,128)}, f32[512,1152]{1,0:T(8,128)}, f32[1,512]{1,0:T(1,128)S(1)}, f32[1,512]{1,0:T(1,128)S(1)}, bf16[512,1152]{1,0:T(8,128)(2,1)}) custom-call(s32[1]{0:T(128)} %bitcast.3.start_ref, f32[1]{0:T(128)S(6)} %copy.8.scale_ref, f32[1]{0:T(128)S(6)} %copy.9.offset_ref, bf16[512,1152]{1,0:T(8,128)(2,1)S(1)} %copy-done.1, ...), custom_call_target="tpu_custom_call" | custom-call | flops 3623878656 | bytes 14155776 | tf_op jit(solution)/shard_map/pallas_call | solution.py:112
  81.8 0.5 collective-permute-start.12
  82.3 4.2 %collective-permute-done.7.refs_9_ = bf16[512,1152]{1,0:T(8,128)(2,1)S(1)} collective-permute-done((bf16[512,1152]{1,0:T(8,128)(2,1)}, bf16[512,1152]{1,0:T(8,128)(2,1)S(1)}, u32[]{:S(2)}, u32[]{:S(2)}) %collective-permute-start.7) | collective-permute-done | bytes 1179680 | tf_op jit(solution)/shard_map/ppermute | solution.py:36
  86.6 1.0 copy-done.3
  87.6 1.3 copy-done.4
  88.8 9.9 %shard_map.81 = (f32[512,1152]{1,0:T(8,128)}, f32[512,1152]{1,0:T(8,128)}, f32[1,512]{1,0:T(1,128)S(1)}, f32[1,512]{1,0:T(1,128)S(1)}, f32[512,1152]{1,0:T(8,128)}) custom-call(s32[1]{0:T(128)} %bitcast.start_ref, f32[1]{0:T(128)S(6)} %copy.8.scale_ref, f32[1]{0:T(128)S(6)} %copy.9.offset_ref, bf16[512,1152]{1,0:T(8,128)(2,1)S(1)} %copy-done.1, ...), custom_call_target="tpu_custom_call" | custom-call | flops 3623878656 | bytes 14155776 | tf_op jit(solution)/shard_map/pallas_call | solution.py:112
  98.8 1.9 %convert_element_type.18 = bf16[512,1152]{1,0:T(8,128)(2,1)S(1)} convert(f32[512,1152]{1,0:T(8,128)} %get-tuple-element.43) | non-fusion elementwise | flops 589824 | bytes 3538944 | tf_op jit(solution)/shard_map/convert_element_type | solution.py:155
  100.7 0.1 fusion
  100.8 0.1 collective-permute-start.9
  100.9 16.6 %collective-permute-done.9 = bf16[256,1152]{1,0:T(8,128)(2,1)S(1)} collective-permute-done((bf16[256,1152]{1,0:T(8,128)(2,1)S(1)}, bf16[256,1152]{1,0:T(8,128)(2,1)S(1)}, u32[]{:S(2)}, u32[]{:S(2)}) %collective-permute-start.9) | collective-permute-done | bytes 589856 | tf_op jit(solution)/shard_map/ppermute | solution.py:36
  117.5 2.9 %collective-permute-start.10 = (bf16[256,1152]{1,0:T(8,128)(2,1)S(1)}, bf16[256,1152]{1,0:T(8,128)(2,1)}, u32[]{:S(2)}, u32[]{:S(2)}) collective-permute-start(bf16[256,1152]{1,0:T(8,128)(2,1)S(1)} %collective-permute-done.9), channel_id=1, source_target_pairs={{0,16},{1,17},{2,18},{3,19},{16,32},{17,33},{18,34},{19,35},{32,48... | collective-permute-start | bytes 1769480 | tf_op jit(solution)/shard_map/ppermute | solution.py:36
  120.4 0.1 collective-permute-start.8
  120.5 0.1 collective-permute-start.11
  120.6 0.1 convert_element_type.21
  120.7 1.7 %collective-permute-start.13 = (bf16[512,1152]{1,0:T(8,128)(2,1)S(1)}, bf16[512,1152]{1,0:T(8,128)(2,1)S(1)}, u32[]{:S(2)}, u32[]{:S(2)}) collective-permute-start(bf16[512,1152]{1,0:T(8,128)(2,1)S(1)} %convert_element_type.21), channel_id=1, source_target_pairs={{0,2},{1,3},{2,0},{3,1},{4,6},{5,7},{6,4},{7,5},{8,10},{9,11},{10,... | collective-permute-start | bytes 3538952 | tf_op jit(solution)/shard_map/ppermute | solution.py:36
  122.4 5.9 %collective-permute-done.8 = f32[512]{0:T(512)S(1)} collective-permute-done((f32[512]{0:T(512)S(1)}, f32[512]{0:T(512)S(1)}, u32[]{:S(2)}, u32[]{:S(2)}) %collective-permute-start.8) | collective-permute-done | bytes 2080 | tf_op jit(solution)/shard_map/ppermute | solution.py:36
  128.3 0.6 add_multiply_fusion
  128.9 8.9 %collective-permute-done.10 = bf16[256,1152]{1,0:T(8,128)(2,1)} collective-permute-done((bf16[256,1152]{1,0:T(8,128)(2,1)S(1)}, bf16[256,1152]{1,0:T(8,128)(2,1)}, u32[]{:S(2)}, u32[]{:S(2)}) %collective-permute-start.10) | collective-permute-done | bytes 589856 | tf_op jit(solution)/shard_map/ppermute | solution.py:36
  137.8 1.1 broadcast_select_fusion
  139.0 2.0 %collective-permute-done.11 = bf16[256,1152]{1,0:T(8,128)(2,1)S(1)} collective-permute-done((bf16[256,1152]{1,0:T(8,128)(2,1)S(1)}, bf16[256,1152]{1,0:T(8,128)(2,1)S(1)}, u32[]{:S(2)}, u32[]{:S(2)}) %collective-permute-start.11) | collective-permute-done | bytes 589856 | tf_op jit(solution)/shard_map/ppermute | solution.py:36
  141.0 1.3 add_convert_fusion.1
  142.2 0.0 collective-permute-done.12
  142.2 17.5 %collective-permute-done.13 = bf16[512,1152]{1,0:T(8,128)(2,1)S(1)} collective-permute-done((bf16[512,1152]{1,0:T(8,128)(2,1)S(1)}, bf16[512,1152]{1,0:T(8,128)(2,1)S(1)}, u32[]{:S(2)}, u32[]{:S(2)}) %collective-permute-start.13) | collective-permute-done | bytes 1179680 | tf_op jit(solution)/shard_map/ppermute | solution.py:36
  159.8 3.0 %add_convert_fusion = bf16[512,1152]{1,0:T(8,128)(2,1)} fusion(bf16[512,1152]{1,0:T(8,128)(2,1)S(1)} %collective-permute-done.13, f32[512,1152]{1,0:T(8,128)S(1)} %copy-done.8, f32[512,1152]{1,0:T(8,128)} %collective-permute-done.12), kind=kLoop, calls=%fused_computation | loop fusion | flops 2359296 | bytes 7077888 | tf_op jit(solution)/shard_map/convert_element_type | solution.py:161
  (18 shorter events, 0.0 us)
Async XLA Ops:
  0.6 32.0 %copy-start.1 = (bf16[512,1152]{1,0:T(8,128)(2,1)S(1)}, bf16[512,1152]{1,0:T(8,128)(2,1)}, u32[]{:S(2)}) copy-start(bf16[512,1152]{1,0:T(8,128)(2,1)} %refs_0_.7) | copy-start | bytes 3538948
  0.6 22.4 %copy-start.5 = (s32[512]{0:T(512)S(1)}, s32[512]{0:T(512)}, u32[]{:S(2)}) copy-start(s32[512]{0:T(512)} %param.7) | copy-start | bytes 6148
  0.6 39.3 %collective-permute-start.4 = (bf16[512,1152]{1,0:T(8,128)(2,1)}, bf16[512,1152]{1,0:T(8,128)(2,1)}, u32[]{:S(2)}, u32[]{:S(2)}) collective-permute-start(bf16[512,1152]{1,0:T(8,128)(2,1)} %refs_2_.3), channel_id=1, source_target_pairs={{0,2},{1,3},{2,0},{3,1},{4,6},{5,7},{6,4},{7,5},{8,10},{9,11},{10,... | collective-permute-start | bytes 3538952 | tf_op jit(solution)/shard_map/ppermute | solution.py:36
  5.2 16.4 %collective-permute-start = (bf16[256,1152]{1,0:T(8,128)(2,1)S(1)}, bf16[256,1152]{1,0:T(8,128)(2,1)S(1)}, u32[]{:S(2)}, u32[]{:S(2)}) collective-permute-start(bf16[256,1152]{1,0:T(8,128)(2,1)S(1)} %get-tuple-element.49), channel_id=1, source_target_pairs={{0,12},{1,13},{2,14},{3,15},{4,0},{5,1},{6,2},{7,3},{8,4},{9,5},{1... | collective-permute-start | bytes 1769480 | tf_op jit(solution)/shard_map/ppermute | solution.py:36
  21.6 18.4 %collective-permute-start.1 = (bf16[256,1152]{1,0:T(8,128)(2,1)S(1)}, bf16[256,1152]{1,0:T(8,128)(2,1)}, u32[]{:S(2)}, u32[]{:S(2)}) collective-permute-start(bf16[256,1152]{1,0:T(8,128)(2,1)S(1)} %collective-permute-done), channel_id=1, source_target_pairs={{12,124},{13,125},{14,126},{15,127},{28,12},{29,13},{30,14},{31,15... | collective-permute-start | bytes 1769480 | tf_op jit(solution)/shard_map/ppermute | solution.py:36
  23.1 32.7 %collective-permute-start.6 = (bf16[512,1152]{1,0:T(8,128)(2,1)}, bf16[512,1152]{1,0:T(8,128)(2,1)S(1)}, u32[]{:S(2)}, u32[]{:S(2)}) collective-permute-start(bf16[512,1152]{1,0:T(8,128)(2,1)} %refs_2_.3), channel_id=1, source_target_pairs={{0,1},{1,0},{2,3},{3,2},{4,5},{5,4},{6,7},{7,6},{8,9},{9,8},{10,11... | collective-permute-start | bytes 3538952 | tf_op jit(solution)/shard_map/ppermute | solution.py:36
  23.1 24.8 %collective-permute-start.3 = (s32[512]{0:T(512)S(1)}, s32[512]{0:T(512)S(1)}, u32[]{:S(2)}, u32[]{:S(2)}) collective-permute-start(s32[512]{0:T(512)S(1)} %copy-done.5), channel_id=1, source_target_pairs={{0,124},{1,125},{2,126},{3,127},{4,0},{5,1},{6,2},{7,3},{8,4},{9,5... | collective-permute-start | bytes 6152 | tf_op jit(solution)/shard_map/ppermute | solution.py:36
  31.3 15.5 %collective-permute-start.2 = (bf16[256,1152]{1,0:T(8,128)(2,1)S(1)}, bf16[256,1152]{1,0:T(8,128)(2,1)}, u32[]{:S(2)}, u32[]{:S(2)}) collective-permute-start(bf16[256,1152]{1,0:T(8,128)(2,1)S(1)} %get-tuple-element.50), channel_id=1, source_target_pairs={{0,124},{1,125},{2,126},{3,127},{4,0},{5,1},{6,2},{7,3},{8,4},{9,5... | collective-permute-start | bytes 1769480 | tf_op jit(solution)/shard_map/ppermute | solution.py:36
  38.5 1.4 copy-start.6
  39.9 31.8 %collective-permute-start.5 = (bf16[512,1152]{1,0:T(8,128)(2,1)}, bf16[512,1152]{1,0:T(8,128)(2,1)S(1)}, u32[]{:S(2)}, u32[]{:S(2)}) collective-permute-start(bf16[512,1152]{1,0:T(8,128)(2,1)} %collective-permute-done.4.refs_4_), channel_id=1, source_target_pairs={{0,1},{1,0},{2,3},{3,2},{4,5},{5,4},{6,7},{7,6},{8,9},{9,8},{10,11... | collective-permute-start | bytes 3538952 | tf_op jit(solution)/shard_map/ppermute | solution.py:36
  54.4 1.4 copy-start
  61.9 1.4 copy-start.7
  70.2 1.5 copy-start.2
  81.8 4.7 %collective-permute-start.7 = (bf16[512,1152]{1,0:T(8,128)(2,1)}, bf16[512,1152]{1,0:T(8,128)(2,1)S(1)}, u32[]{:S(2)}, u32[]{:S(2)}) collective-permute-start(bf16[512,1152]{1,0:T(8,128)(2,1)} %get-tuple-element.39), channel_id=1, source_target_pairs={{0,1},{1,0},{2,3},{3,2},{4,5},{5,4},{6,7},{7,6},{8,9},{9,8},{10,11... | collective-permute-start | bytes 3538952 | tf_op jit(solution)/shard_map/ppermute | solution.py:36
  81.8 60.4 %collective-permute-start.12 = (f32[512,1152]{1,0:T(8,128)}, f32[512,1152]{1,0:T(8,128)}, u32[]{:S(2)}, u32[]{:S(2)}) collective-permute-start(f32[512,1152]{1,0:T(8,128)} %get-tuple-element.45), channel_id=1, source_target_pairs={{0,1},{1,0},{2,3},{3,2},{4,5},{5,4},{6,7},{7,6},{8,9},{9,8},{10,11... | collective-permute-start | bytes 7077896 | tf_op jit(solution)/shard_map/ppermute | solution.py:36
  86.5 1.0 copy-start.3
  87.6 1.3 copy-start.4
  98.8 21.8 %copy-start.10 = (f32[512,1152]{1,0:T(8,128)S(1)}, f32[512,1152]{1,0:T(8,128)}, u32[]{:S(2)}) copy-start(f32[512,1152]{1,0:T(8,128)} %get-tuple-element.46) | copy-start | bytes 7077892
  100.8 16.7 %collective-permute-start.9 = (bf16[256,1152]{1,0:T(8,128)(2,1)S(1)}, bf16[256,1152]{1,0:T(8,128)(2,1)S(1)}, u32[]{:S(2)}, u32[]{:S(2)}) collective-permute-start(bf16[256,1152]{1,0:T(8,128)(2,1)S(1)} %get-tuple-element.47), channel_id=1, source_target_pairs={{0,4},{1,5},{2,6},{3,7},{4,8},{5,9},{6,10},{7,11},{8,12},{9,13},{1... | collective-permute-start | bytes 1769480 | tf_op jit(solution)/shard_map/ppermute | solution.py:36
  117.5 20.4 %collective-permute-start.10 = (bf16[256,1152]{1,0:T(8,128)(2,1)S(1)}, bf16[256,1152]{1,0:T(8,128)(2,1)}, u32[]{:S(2)}, u32[]{:S(2)}) collective-permute-start(bf16[256,1152]{1,0:T(8,128)(2,1)S(1)} %collective-permute-done.9), channel_id=1, source_target_pairs={{0,16},{1,17},{2,18},{3,19},{16,32},{17,33},{18,34},{19,35},{32,48... | collective-permute-start | bytes 1769480 | tf_op jit(solution)/shard_map/ppermute | solution.py:36
  120.4 8.0 %collective-permute-start.8 = (f32[512]{0:T(512)S(1)}, f32[512]{0:T(512)S(1)}, u32[]{:S(2)}, u32[]{:S(2)}) collective-permute-start(f32[512]{0:T(512)S(1)} %bitcast.17), channel_id=1, source_target_pairs={{0,4},{1,5},{2,6},{3,7},{4,8},{5,9},{6,10},{7,11},{8,12},{9,13},{1... | collective-permute-start | bytes 6152 | tf_op jit(solution)/shard_map/ppermute | solution.py:36
  120.5 20.5 %collective-permute-start.11 = (bf16[256,1152]{1,0:T(8,128)(2,1)S(1)}, bf16[256,1152]{1,0:T(8,128)(2,1)S(1)}, u32[]{:S(2)}, u32[]{:S(2)}) collective-permute-start(bf16[256,1152]{1,0:T(8,128)(2,1)S(1)} %get-tuple-element.48), channel_id=1, source_target_pairs={{0,4},{1,5},{2,6},{3,7},{4,8},{5,9},{6,10},{7,11},{8,12},{9,13},{1... | collective-permute-start | bytes 1769480 | tf_op jit(solution)/shard_map/ppermute | solution.py:36
  120.5 20.4 %copy-start.9 = (f32[512,1152]{1,0:T(8,128)S(1)}, f32[512,1152]{1,0:T(8,128)}, u32[]{:S(2)}) copy-start(f32[512,1152]{1,0:T(8,128)} %get-tuple-element.42) | copy-start | bytes 7077892
  120.7 39.1 %collective-permute-start.13 = (bf16[512,1152]{1,0:T(8,128)(2,1)S(1)}, bf16[512,1152]{1,0:T(8,128)(2,1)S(1)}, u32[]{:S(2)}, u32[]{:S(2)}) collective-permute-start(bf16[512,1152]{1,0:T(8,128)(2,1)S(1)} %convert_element_type.21), channel_id=1, source_target_pairs={{0,2},{1,3},{2,0},{3,1},{4,6},{5,7},{6,4},{7,5},{8,10},{9,11},{10,... | collective-permute-start | bytes 3538952 | tf_op jit(solution)/shard_map/ppermute | solution.py:36
  141.0 18.8 %copy-start.8 = (f32[512,1152]{1,0:T(8,128)S(1)}, f32[512,1152]{1,0:T(8,128)}, u32[]{:S(2)}) copy-start(f32[512,1152]{1,0:T(8,128)} %get-tuple-element.44) | copy-start | bytes 7077892

commit v2 on v0

v2 whole, which is shorter than its diff:
```python
import functools
import jax
import jax.numpy as jnp
from jax import lax
from jax.experimental import pallas as pl
from jax.experimental.pallas import tpu as pltpu
from jax.sharding import PartitionSpec as P

AXES = ("dp", "rep")
NT = (((1,), (1,)), ((), ()))
TN = (((0,), (0,)), ((), ()))
F32, BF16 = jnp.float32, jnp.bfloat16


def place(flat):
    dp, rep = divmod(flat, 4)
    return dp // 8, (rep // 2) * 2 + (dp // 4) % 2, dp % 4, rep % 2


def flat_of(y, x, z, core):
    return (y * 8 + (x % 2) * 4 + z) * 4 + (x // 2) * 2 + core


def moved(x=0, z=0, core=0):
    route = []
    for source in range(128):
        sy, sx, sz, sc = place(source)
        route.append((source, flat_of(sy, (sx + x) % 4, (sz + z) % 4, (sc + core) % 2)))
    return route


def along_loop(step, core=0):
    return [(source, ((source + 4 * step) % 128) ^ core) for source in range(128)]


def last_hop(step):
    along_z = dict(moved(z=step))
    turn = 3 if step > 0 else 0
    return [(along_z[s], d) for s, d in along_loop(step) if place(s)[2] == turn]


def send(block, route):
    return lax.ppermute(block, AXES, route)


def after(block, *others):
    return lax.optimization_barrier((block, *others))[0]


def terms(dots, positive, temper, shift):
    logit = temper * dots + shift
    z = jnp.where(positive, -logit, logit)
    e = jnp.exp(-jnp.abs(z))
    log_term = jnp.where(e < 1e-4, e, jnp.log(1.0 + e))
    loss = jnp.maximum(z, 0.0) + log_term
    sigmoid = jnp.exp(jnp.minimum(z, 0.0) - log_term)
    coef = (jnp.where(positive, -temper, temper) * sigmoid).astype(BF16)
    return loss, coef


SMEM = pl.BlockSpec(memory_space=pltpu.SMEM)
VMEM = pl.BlockSpec(memory_space=pltpu.VMEM)
ROWS, WIDTH, HALF = 512, 1152, 256
CARRY = 16


def near(array):
    return pltpu.with_memory_space_constraint(array, pltpu.VMEM)


def call(kernel, smalls, arrays, outs, alias=None, cells=0):
    return pl.pallas_call(
        kernel,
        in_specs=[SMEM] * len(smalls) + [VMEM] * len(arrays),
        out_specs=[VMEM] * len(outs),
        out_shape=outs,
        input_output_aliases=alias or {},
        compiler_params=pltpu.CompilerParams(vmem_limit_bytes=16 << 20),
        cost_estimate=pl.CostEstimate(flops=1000, bytes_accessed=1000, transcendentals=0),
    )(*smalls, *map(near, arrays))


def split3(value):
    high = value.astype(BF16)
    middle = (value - high.astype(F32)).astype(BF16)
    low = (value - high.astype(F32) - middle.astype(F32)).astype(BF16)
    return high, middle, low


def put_loss(ref, at, loss):
    if ref.dtype == F32:
        ref[pl.ds(at, 8), :ROWS] = jnp.broadcast_to(loss, (8, ROWS))
        return
    row = lax.broadcasted_iota(jnp.int32, (CARRY, ROWS), 0)
    parts = [part.astype(F32) for part in split3(loss)]
    block = jnp.where(row == 0, parts[0], jnp.where(row == 1, parts[1], jnp.where(row == 2, parts[2], 0.0)))
    ref[pl.ds(at, CARRY), :ROWS] = block.astype(BF16)


def get_loss(ref, at):
    if ref.dtype == F32:
        return ref[pl.ds(at, 8), :ROWS][0:1]
    parts = ref[pl.ds(at, CARRY), :ROWS].astype(F32)
    return parts[0:1] + parts[1:2] + parts[2:3]


def pair_body(gi_has, gt_has, start_ref, scale_ref, offset_ref, *refs):
    refs = list(refs)

    def take(count):
        out = refs[:count]
        del refs[:count]
        return out

    imgs, txt = take(2), take(1)[0]
    gi_in = take(2) if gi_has else None
    gt_in = take(1)[0] if gt_has else None
    gi, gt = take(2), take(1)[0]
    temper, shift = scale_ref[0], offset_ref[0]
    t = txt[...]
    col = start_ref[0] + lax.broadcasted_iota(jnp.int32, (ROWS, ROWS), 0).astype(F32)
    t_sum = gt_in[...] if gt_has else None
    for m in range(2):
        a = imgs[m][:ROWS, :]
        code = imgs[m][pl.ds(ROWS, CARRY), :ROWS].astype(F32)
        partner = code[0:1] * 256.0 + code[1:2]
        dots = lax.dot_general(t, a, NT, preferred_element_type=F32)
        ls, coef = terms(dots, partner == col, temper, shift)
        loss = jnp.sum(ls, axis=0, keepdims=True)
        g = lax.dot_general(coef, t, TN, preferred_element_type=F32)
        d = jnp.dot(coef, a, preferred_element_type=F32)
        if gi_has:
            loss = loss + get_loss(gi_in[m], ROWS)
            g = g + gi_in[m][:ROWS, :]
        gi[m][:ROWS, :] = g.astype(gi[m].dtype)
        put_loss(gi[m], ROWS, loss)
        t_sum = d if t_sum is None else t_sum + d
    gt[...] = t_sum.astype(gt.dtype)


def grad_shape(ty):
    return pltpu.VMEM((ROWS + (8 if ty == F32 else CARRY), WIDTH), ty)


def pairs(imgs, txt, start, scale, offset, gi=None, gt=None, gi_types=(F32, F32), gt_type=F32):
    arrays = [*imgs, txt, *(gi or []), *([gt] if gt is not None else [])]
    alias = {}
    if gi is not None:
        alias.update({6 + m: m for m in range(2) if gi_types[m] == F32})
    if gt is not None and gt_type == F32:
        alias[5 + len(arrays) - 3] = 2
    outs = [grad_shape(ty) for ty in gi_types] + [pltpu.VMEM((ROWS, WIDTH), gt_type)]
    got = call(
        functools.partial(pair_body, gi is not None, gt is not None), (start, scale, offset), arrays, outs, alias
    )
    return got[:2], got[2]


def assemble_body(flag_ref, first, turned, rest, out):
    out[:HALF, :] = jnp.where(flag_ref[0] == 1, turned[...], first[...])
    out[HALF:, :] = rest[...]


def fold_body(mine, other, top, rest):
    top[...] = (mine[:HALF, :] + other[:HALF, :].astype(F32)).astype(BF16)
    rest[:HALF, :] = (mine[HALF:ROWS, :] + other[HALF:ROWS, :].astype(F32)).astype(BF16)
    put_loss(rest, HALF, get_loss(mine, ROWS) + get_loss(other, ROWS))


def image_body(flag_ref, mine, other, first, turned, rest, grad, row_loss):
    top = jnp.where(flag_ref[0] == 1, turned[...], first[...]).astype(F32)
    grad[:HALF, :] = (mine[:HALF, :] + other[:HALF, :] + top).astype(BF16)
    below = rest[:HALF, :].astype(F32)
    grad[HALF:, :] = (mine[HALF:ROWS, :] + other[HALF:ROWS, :] + below).astype(BF16)
    loss = get_loss(mine, ROWS) + get_loss(other, ROWS) + get_loss(rest, HALF)
    row_loss[...] = loss / (8.0 * ROWS)


def add_body(one, two, out):
    out[...] = one[...] + two[...]


def text_body(mine, back, grad):
    grad[...] = (mine[...] + back[...].astype(F32)).astype(BF16)


def body(images, texts, partner, scale, offset):
    dp, rep = lax.axis_index("dp"), lax.axis_index("rep")
    start = ((dp * 4 + rep) * ROWS).astype(F32)[None]
    far_start = ((dp * 4 + (rep ^ 2)) * ROWS).astype(F32)[None]
    swap = moved(core=1)
    across = moved(x=2)

    def flag(z):
        return (dp % 4 == z).astype(jnp.int32)[None]

    code = jnp.stack([partner // 256, partner % 256]).astype(BF16)
    own = jnp.concatenate([images, jnp.pad(code, ((0, CARRY - 2), (0, WIDTH - ROWS)))])
    far = send(texts, across)
    first = send(images[:HALF], moved(z=-1))
    own2 = send(own, swap)
    (ga, ga2), gs = pairs([own, own2], texts, start, scale, offset)
    turned = send(after(first, gs), last_hop(-1))
    rest = send(after(own[HALF:], far, gs), along_loop(-1))
    (ga, ga2), gu = pairs([own, own2], far, far_start, scale, offset, [ga, ga2])
    visitor = call(
        assemble_body, (flag(3),), (after(first, gu), turned, rest), [pltpu.VMEM((ROWS + CARRY, WIDTH), BF16)]
    )[0]
    visitor2 = send(visitor, swap)
    (gb, gb2), gs2 = pairs([visitor, visitor2], texts, start, scale, offset)
    (gb, gb2), gu = pairs([visitor, visitor2], far, far_start, scale, offset, [gb, gb2], gu, (F32, BF16), BF16)
    gu_back = send(gu, across)
    gb_got = send(gb2, swap)
    top, bottom = call(
        fold_body, (), (gb, gb_got),
        [pltpu.VMEM((HALF, WIDTH), BF16), pltpu.VMEM((HALF + CARRY, WIDTH), BF16)],
    )
    back_first = send(top, moved(z=1))
    back_rest = send(after(bottom, back_first), along_loop(1))
    gs = call(add_body, (), (after(gs, top), gs2), [pltpu.VMEM((ROWS, WIDTH), F32)], {0: 0})[0]
    back_turned = send(back_first, last_hop(1))
    ga_got = send(after(ga2, top), swap)
    grad_texts = call(text_body, (), (gs, gu_back), [jax.ShapeDtypeStruct((ROWS, WIDTH), BF16)])[0]
    grad_images, row_loss = call(
        image_body, (flag(0),), (ga, ga_got, back_first, back_turned, back_rest),
        [jax.ShapeDtypeStruct((ROWS, WIDTH), BF16), jax.ShapeDtypeStruct((1, ROWS), F32)],
    )
    return row_loss[0], grad_images, grad_texts


def solution(mesh):
    in_specs = (P(AXES, None), P(AXES, None), P(AXES), P(), P())
    out_specs = (P(AXES), P(AXES, None), P(AXES, None))
    return jax.shard_map(body, mesh=mesh, in_specs=in_specs, out_specs=out_specs, check_vma=False)
```

time: 483 us -> 132 us (0.27)
  waiting for transfers between devices: 420 us -> 56.1 us
  matrix products: 40.6 us -> 0 us
  Pallas kernels: 0 us -> 38 us
  starting transfers between devices: 2.54 us -> 22.1 us
  between operations: 15.4 us -> 2.06 us
  local copies, waits for them, and re-layouts: 0.03 us -> 8.52 us
    ppermute x2 -> x12, waiting for transfers between devices: 302 us -> 56.1 us  [send(): return lax.ppermute(block, AXES, route)]
    reduce_scatter x1 -> x0, waiting for transfers between devices: 70.8 us -> none  [body(): lax.psum_scatter(acc_own + returned, 'rep', scatter_dimension=0, tiled=True)]
    all_gather x1 -> x0, waiting for transfers between devices: 45.7 us -> none  [body(): own_block = lax.all_gather(texts, 'rep', axis=0, tiled=True)]
    dot_general x6 -> x0, matrix products: 40.6 us -> none  [the longest x2 13.9 us: block_terms(): jnp.dot(image_rows, text_rows.T, preferred_element_type=jnp.float32)]
    pallas_call x0 -> x9, Pallas kernels: none -> 38 us  [call(): pl.pallas_call(kernel, in_specs=[SMEM] * len(smalls) + [VMEM] * len(array...]
    ppermute x2 -> x12, starting transfers between devices: 2.47 us -> 22.1 us  [send(): return lax.ppermute(block, AXES, route)]
    unnamed x10 -> x18, local copies, waits for them, and re-layouts: 0.03 us -> 7.65 us
  transfers between devices with their start and end apart: 4 -> 12, of which waited for: 4 -> 8; matrix products, arithmetic and copies ran while one was open for 4% -> 2% of each run, Pallas kernels for 0% -> 13%
where the time goes in v2:
time: 132 us; the launch traced here: 131 us
  waiting for transfers between devices  56.1 us (42%)
  Pallas kernels  38 us (29%)
  starting transfers between devices  22.1 us (17%)
  local copies, waits for them, and re-layouts  8.52 us (6%)
  other arithmetic  4.11 us (3%)
  between operations  2.06 us (2%)
    ppermute x12, waiting for transfers between devices, send(): return lax.ppermute(block, AXES, route)  56.1 us
    pallas_call x9, Pallas kernels, call(): pl.pallas_call(kernel, in_specs=[SMEM] * len(smalls) + [VMEM] * len(array...  38 us
    ppermute x12, starting transfers between devices, send(): return lax.ppermute(block, AXES, route)  22.1 us
    unnamed x18, local copies, waits for them, and re-layouts  7.65 us
    concatenate x2, other arithmetic, body(): jnp.concatenate([images, jnp.pad(code, ((0, CARRY - 2), (0, WIDTH - ROWS)...  3.4 us
  transfers between devices with their start and end apart: 12, of which 8 were waited for; matrix products, arithmetic and copies ran while one was open for 2% of the time, Pallas kernels for 13%

profile of v2, /device:TPU:0, one launch (start us, length us, event | category | flops | bytes accessed | tf_op | source)
XLA Modules:
  0.0 130.9 jit_solution(11368384633799581583)
XLA Ops:
  0.6 0.7 fusion.7
  1.4 0.0 copy-start.8
  1.4 1.5 %pad_maximum_fusion.refs_0_ = bf16[528,1152]{1,0:T(8,128)(2,1)S(1)} fusion(bf16[16,1152]{1,0:T(8,128)(2,1)S(1)} %fusion.6, bf16[512,1152]{1,0:T(8,128)(2,1)} %param.5), kind=kLoop, calls=%fused_computation.1 | loop fusion | flops 2433024 | bytes 2433024 | tf_op jit(solution)/shard_map/concatenate | solution.py:198
  2.8 0.1 collective-permute-start
  2.9 3.2 %collective-permute-start.1 = (bf16[512,1152]{1,0:T(8,128)(2,1)}, bf16[512,1152]{1,0:T(8,128)(2,1)}, u32[]{:S(2)}, u32[]{:S(2)}) collective-permute-start(bf16[512,1152]{1,0:T(8,128)(2,1)} %refs_2_.3), channel_id=1, source_target_pairs={{0,2},{1,3},{2,0},{3,1},{4,6},{5,7},{6,4},{7,5},{8,10},{9,11},{10,... | collective-permute-start | bytes 3538952 | tf_op jit(solution)/shard_map/ppermute | solution.py:43
  6.1 0.0 copy-done.8
  6.1 0.9 slice.6
  7.0 4.0 %collective-permute-start.2 = (bf16[256,1152]{1,0:T(8,128)(2,1)}, bf16[256,1152]{1,0:T(8,128)(2,1)}, u32[]{:S(2)}, u32[]{:S(2)}) collective-permute-start(bf16[256,1152]{1,0:T(8,128)(2,1)} %slice.6), channel_id=1, source_target_pairs={{0,12},{1,13},{2,14},{3,15},{4,0},{5,1},{6,2},{7,3},{8,4},{9,5},{1... | collective-permute-start | bytes 1769480 | tf_op jit(solution)/shard_map/ppermute | solution.py:43
  12.3 1.9 %fusion = bf16[272,1152]{1,0:T(8,128)(2,1)} fusion(bf16[512,1152]{1,0:T(8,128)(2,1)} %param.5, bf16[16,1152]{1,0:T(8,128)(2,1)S(1)} %fusion.6), kind=kLoop, calls=%fused_computation.3 | loop fusion | flops 1253376 | bytes 1843200 | tf_op jit(solution)/shard_map/concatenate | solution.py:198
  14.3 0.0 collective-permute-done.refs_1_
  14.3 7.2 %shard_map.76 = (f32[520,1152]{1,0:T(8,128)S(1)}, f32[520,1152]{1,0:T(8,128)}, f32[512,1152]{1,0:T(8,128)S(1)}) custom-call(f32[1]{0:T(128)} %bitcast.2.start_ref, f32[1]{0:T(128)S(6)} %copy.16.scale_ref, f32[1]{0:T(128)S(6)} %copy.17.offset_ref, bf16[528,1152]{1,0:T(8,128)(2,1)S(1)} %pad_maximum_fusion.refs_0_, ...), custom_call_target="tpu_custom_call" | custom-call | flops 1000 | bytes 1000 | tf_op jit(solution)/shard_map/pallas_call | solution.py:72
  21.5 1.4 %copy-done = f32[520,1152]{1,0:T(8,128)} copy-done((f32[520,1152]{1,0:T(8,128)}, f32[520,1152]{1,0:T(8,128)S(1)}, u32[]{:S(2)}) %copy-start) | copy-done | bytes 2396184
  22.9 1.5 %copy-done.4 = f32[512,1152]{1,0:T(8,128)} copy-done((f32[512,1152]{1,0:T(8,128)}, f32[512,1152]{1,0:T(8,128)S(1)}, u32[]{:S(2)}) %copy-start.4) | copy-done | bytes 2359320
  24.4 8.7 %collective-permute-done.1.refs_2_ = bf16[512,1152]{1,0:T(8,128)(2,1)} collective-permute-done((bf16[512,1152]{1,0:T(8,128)(2,1)}, bf16[512,1152]{1,0:T(8,128)(2,1)}, u32[]{:S(2)}, u32[]{:S(2)}) %collective-permute-start.1) | collective-permute-done | bytes 1179680 | tf_op jit(solution)/shard_map/ppermute | solution.py:43
  33.1 7.5 %collective-permute-start.4 = (bf16[272,1152]{1,0:T(8,128)(2,1)}, bf16[272,1152]{1,0:T(8,128)(2,1)S(1)}, u32[]{:S(2)}, u32[]{:S(2)}) collective-permute-start(bf16[272,1152]{1,0:T(8,128)(2,1)} %fusion), channel_id=1, source_target_pairs={{0,124},{1,125},{2,126},{3,127},{4,0},{5,1},{6,2},{7,3},{8,4},{9,5... | collective-permute-start | bytes 1880072 | tf_op jit(solution)/shard_map/ppermute | solution.py:43
  40.6 0.0 collective-permute-done.2.first
  40.6 1.5 %collective-permute-start.3 = (bf16[256,1152]{1,0:T(8,128)(2,1)}, bf16[256,1152]{1,0:T(8,128)(2,1)}, u32[]{:S(2)}, u32[]{:S(2)}) collective-permute-start(bf16[256,1152]{1,0:T(8,128)(2,1)} %collective-permute-done.2.first), channel_id=1, source_target_pairs={{12,124},{13,125},{14,126},{15,127},{28,12},{29,13},{30,14},{31,15... | collective-permute-start | bytes 1769480 | tf_op jit(solution)/shard_map/ppermute | solution.py:43
  42.1 1.7 %copy-done.1 = f32[520,1152]{1,0:T(8,128)S(1)} copy-done((f32[520,1152]{1,0:T(8,128)S(1)}, f32[520,1152]{1,0:T(8,128)}, u32[]{:S(2)}) %copy-start.1) | copy-done | bytes 2396184
  43.8 8.7 %shard_map.77 = (f32[520,1152]{1,0:T(8,128)S(1)}, f32[520,1152]{1,0:T(8,128)}, f32[512,1152]{1,0:T(8,128)S(1)}) custom-call(f32[1]{0:T(128)} %bitcast.1.start_ref, f32[1]{0:T(128)S(6)} %copy.16.scale_ref, f32[1]{0:T(128)S(6)} %copy.17.offset_ref, bf16[528,1152]{1,0:T(8,128)(2,1)S(1)} %pad_maximum_fusion.refs_0_, ...), custom_call_target="tpu_custom_call", output_to_operand_aliasing={{0}: (6, {}), {1}: (7, {})} | custom-call | flops 1000 | bytes 1000 | tf_op jit(solution)/shard_map/pallas_call | solution.py:72
  52.5 0.0 collective-permute-done.3.turned
  52.5 1.6 %collective-permute-done.4.rest = bf16[272,1152]{1,0:T(8,128)(2,1)S(1)} collective-permute-done((bf16[272,1152]{1,0:T(8,128)(2,1)}, bf16[272,1152]{1,0:T(8,128)(2,1)S(1)}, u32[]{:S(2)}, u32[]{:S(2)}) %collective-permute-start.4) | collective-permute-done | bytes 626720 | tf_op jit(solution)/shard_map/ppermute | solution.py:43
  54.1 1.4 %shard_map.78.refs_0_ = bf16[528,1152]{1,0:T(8,128)(2,1)S(1)} custom-call(s32[1]{0:T(128)} %bitcast.3.flag_ref, bf16[256,1152]{1,0:T(8,128)(2,1)} %collective-permute-done.2.first, bf16[256,1152]{1,0:T(8,128)(2,1)} %collective-permute-done.3.turned, bf16[272,1152]{1,0:T(8,128)(2,1)S(1)} %collective-permute-done.4.rest), custom_call_target="tpu_custom_call" | custom-call | flops 1000 | bytes 1000 | tf_op jit(solution)/shard_map/pallas_call | solution.py:72
  55.5 0.0 copy-done.2
  55.5 0.3 collective-permute-start.5
  55.8 2.9 %collective-permute-done.5.refs_1_ = bf16[528,1152]{1,0:T(8,128)(2,1)S(1)} collective-permute-done((bf16[528,1152]{1,0:T(8,128)(2,1)S(1)}, bf16[528,1152]{1,0:T(8,128)(2,1)S(1)}, u32[]{:S(2)}, u32[]{:S(2)}) %collective-permute-start.5) | collective-permute-done | bytes 1216544 | tf_op jit(solution)/shard_map/ppermute | solution.py:43
  58.7 7.1 %shard_map.79 = (f32[520,1152]{1,0:T(8,128)S(1)}, f32[520,1152]{1,0:T(8,128)S(1)}, f32[512,1152]{1,0:T(8,128)S(1)}) custom-call(f32[1]{0:T(128)} %bitcast.2.start_ref, f32[1]{0:T(128)S(6)} %copy.16.scale_ref, f32[1]{0:T(128)S(6)} %copy.17.offset_ref, bf16[528,1152]{1,0:T(8,128)(2,1)S(1)} %shard_map.78.refs_0_, ...), custom_call_target="tpu_custom_call" | custom-call | flops 1000 | bytes 1000 | tf_op jit(solution)/shard_map/pallas_call | solution.py:72
  65.8 0.0 copy-start.6
  65.8 1.4 %copy-done.6 = f32[512,1152]{1,0:T(8,128)} copy-done((f32[512,1152]{1,0:T(8,128)}, f32[512,1152]{1,0:T(8,128)S(1)}, u32[]{:S(2)}) %copy-start.6) | copy-done | bytes 2359320
  67.2 7.5 %shard_map.80 = (f32[520,1152]{1,0:T(8,128)S(1)}, bf16[528,1152]{1,0:T(8,128)(2,1)S(1)}, bf16[512,1152]{1,0:T(8,128)(2,1)}) custom-call(f32[1]{0:T(128)} %bitcast.1.start_ref, f32[1]{0:T(128)S(6)} %copy.16.scale_ref, f32[1]{0:T(128)S(6)} %copy.17.offset_ref, bf16[528,1152]{1,0:T(8,128)(2,1)S(1)} %shard_map.78.refs_0_, ...), custom_call_target="tpu_custom_call", output_to_operand_aliasing={{0}: (6, {})} | custom-call | flops 1000 | bytes 1000 | tf_op jit(solution)/shard_map/pallas_call | solution.py:72
  74.7 0.1 collective-permute-start.6
  74.8 2.8 %collective-permute-done.6.other = bf16[528,1152]{1,0:T(8,128)(2,1)S(1)} collective-permute-done((bf16[528,1152]{1,0:T(8,128)(2,1)S(1)}, bf16[528,1152]{1,0:T(8,128)(2,1)S(1)}, u32[]{:S(2)}, u32[]{:S(2)}) %collective-permute-start.6) | collective-permute-done | bytes 1216544 | tf_op jit(solution)/shard_map/ppermute | solution.py:43
  77.6 1.0 shard_map.81
  78.6 0.1 collective-permute-start.7
  78.7 0.0 collective-permute-start.8
  78.7 2.7 %collective-permute-start.11 = (bf16[512,1152]{1,0:T(8,128)(2,1)}, bf16[512,1152]{1,0:T(8,128)(2,1)S(1)}, u32[]{:S(2)}, u32[]{:S(2)}) collective-permute-start(bf16[512,1152]{1,0:T(8,128)(2,1)} %get-tuple-element.46), channel_id=1, source_target_pairs={{0,2},{1,3},{2,0},{3,1},{4,6},{5,7},{6,4},{7,5},{8,10},{9,11},{10,... | collective-permute-start | bytes 3538952 | tf_op jit(solution)/shard_map/ppermute | solution.py:43
  81.5 14.2 %collective-permute-done.8.first = bf16[256,1152]{1,0:T(8,128)(2,1)} collective-permute-done((bf16[256,1152]{1,0:T(8,128)(2,1)S(1)}, bf16[256,1152]{1,0:T(8,128)(2,1)}, u32[]{:S(2)}, u32[]{:S(2)}) %collective-permute-start.8) | collective-permute-done | bytes 589856 | tf_op jit(solution)/shard_map/ppermute | solution.py:43
  95.6 0.0 collective-permute-start.10
  95.6 2.4 %collective-permute-start.9 = (bf16[256,1152]{1,0:T(8,128)(2,1)}, bf16[256,1152]{1,0:T(8,128)(2,1)}, u32[]{:S(2)}, u32[]{:S(2)}) collective-permute-start(bf16[256,1152]{1,0:T(8,128)(2,1)} %collective-permute-done.8.first), channel_id=1, source_target_pairs={{0,16},{1,17},{2,18},{3,19},{16,32},{17,33},{18,34},{19,35},{32,48... | collective-permute-start | bytes 1769480 | tf_op jit(solution)/shard_map/ppermute | solution.py:43
  98.1 0.0 copy-done.5
  98.1 0.0 copy-start.7
  98.1 1.7 %copy-done.7 = f32[512,1152]{1,0:T(8,128)S(1)} copy-done((f32[512,1152]{1,0:T(8,128)S(1)}, f32[512,1152]{1,0:T(8,128)}, u32[]{:S(2)}) %copy-start.7) | copy-done | bytes 2359320
  99.8 0.4 shard_map.83.mine
  100.2 9.0 %collective-permute-done.11.back = bf16[512,1152]{1,0:T(8,128)(2,1)S(1)} collective-permute-done((bf16[512,1152]{1,0:T(8,128)(2,1)}, bf16[512,1152]{1,0:T(8,128)(2,1)S(1)}, u32[]{:S(2)}, u32[]{:S(2)}) %collective-permute-start.11) | collective-permute-done | bytes 1179680 | tf_op jit(solution)/shard_map/ppermute | solution.py:43
  109.2 1.2 shard_map.84
  110.5 10.4 %collective-permute-done.9.turned = bf16[256,1152]{1,0:T(8,128)(2,1)} collective-permute-done((bf16[256,1152]{1,0:T(8,128)(2,1)}, bf16[256,1152]{1,0:T(8,128)(2,1)}, u32[]{:S(2)}, u32[]{:S(2)}) %collective-permute-start.9) | collective-permute-done | bytes 589856 | tf_op jit(solution)/shard_map/ppermute | solution.py:43
  120.8 6.6 %collective-permute-done.10.rest = bf16[272,1152]{1,0:T(8,128)(2,1)} collective-permute-done((bf16[272,1152]{1,0:T(8,128)(2,1)}, bf16[272,1152]{1,0:T(8,128)(2,1)}, u32[]{:S(2)}, u32[]{:S(2)}) %collective-permute-start.10) | collective-permute-done | bytes 626720 | tf_op jit(solution)/shard_map/ppermute | solution.py:43
  127.4 0.0 collective-permute-done.7.other
  127.4 3.5 %shard_map.82 = (bf16[512,1152]{1,0:T(8,128)(2,1)}, f32[1,512]{1,0:T(1,128)}) custom-call(s32[1]{0:T(128)} %bitcast.flag_ref, f32[520,1152]{1,0:T(8,128)S(1)} %copy-done.3, f32[520,1152]{1,0:T(8,128)} %collective-permute-done.7.other, bf16[256,1152]{1,0:T(8,128)(2,1)} %collective-permute-done.8.first, bf16[256,1152]{1,0:T(8,128)(2,1)} %collective-permute-done.9.turned, ...), custom_call_target="tpu_custom_call" | custom-call | flops 1000 | bytes 1000 | tf_op jit(solution)/shard_map/pallas_call | solution.py:72
  (10 shorter events, 0.0 us)
Async XLA Ops:
  1.4 4.8 %copy-start.8 = (bf16[512,1152]{1,0:T(8,128)(2,1)S(1)}, bf16[512,1152]{1,0:T(8,128)(2,1)}, u32[]{:S(2)}) copy-start(bf16[512,1152]{1,0:T(8,128)(2,1)} %param.5) | copy-start | bytes 3538948
  2.8 11.4 %collective-permute-start = (bf16[528,1152]{1,0:T(8,128)(2,1)S(1)}, bf16[528,1152]{1,0:T(8,128)(2,1)S(1)}, u32[]{:S(2)}, u32[]{:S(2)}) collective-permute-start(bf16[528,1152]{1,0:T(8,128)(2,1)S(1)} %pad_maximum_fusion.refs_0_), channel_id=1, source_target_pairs={{0,1},{1,0},{2,3},{3,2},{4,5},{5,4},{6,7},{7,6},{8,9},{9,8},{10,11... | collective-permute-start | bytes 3649544 | tf_op jit(solution)/shard_map/ppermute | solution.py:43
  2.9 30.2 %collective-permute-start.1 = (bf16[512,1152]{1,0:T(8,128)(2,1)}, bf16[512,1152]{1,0:T(8,128)(2,1)}, u32[]{:S(2)}, u32[]{:S(2)}) collective-permute-start(bf16[512,1152]{1,0:T(8,128)(2,1)} %refs_2_.3), channel_id=1, source_target_pairs={{0,2},{1,3},{2,0},{3,1},{4,6},{5,7},{6,4},{7,5},{8,10},{9,11},{10,... | collective-permute-start | bytes 3538952 | tf_op jit(solution)/shard_map/ppermute | solution.py:43
  7.0 33.7 %collective-permute-start.2 = (bf16[256,1152]{1,0:T(8,128)(2,1)}, bf16[256,1152]{1,0:T(8,128)(2,1)}, u32[]{:S(2)}, u32[]{:S(2)}) collective-permute-start(bf16[256,1152]{1,0:T(8,128)(2,1)} %slice.6), channel_id=1, source_target_pairs={{0,12},{1,13},{2,14},{3,15},{4,0},{5,1},{6,2},{7,3},{8,4},{9,5},{1... | collective-permute-start | bytes 1769480 | tf_op jit(solution)/shard_map/ppermute | solution.py:43
  21.5 1.4 %copy-start = (f32[520,1152]{1,0:T(8,128)}, f32[520,1152]{1,0:T(8,128)S(1)}, u32[]{:S(2)}) copy-start(f32[520,1152]{1,0:T(8,128)S(1)} %get-tuple-element.25.refs_3_) | copy-start | bytes 7188484
  22.9 1.5 %copy-start.4 = (f32[512,1152]{1,0:T(8,128)}, f32[512,1152]{1,0:T(8,128)S(1)}, u32[]{:S(2)}) copy-start(f32[512,1152]{1,0:T(8,128)S(1)} %get-tuple-element.44.one) | copy-start | bytes 7077892
  33.1 21.0 %collective-permute-start.4 = (bf16[272,1152]{1,0:T(8,128)(2,1)}, bf16[272,1152]{1,0:T(8,128)(2,1)S(1)}, u32[]{:S(2)}, u32[]{:S(2)}) collective-permute-start(bf16[272,1152]{1,0:T(8,128)(2,1)} %fusion), channel_id=1, source_target_pairs={{0,124},{1,125},{2,126},{3,127},{4,0},{5,1},{6,2},{7,3},{8,4},{9,5... | collective-permute-start | bytes 1880072 | tf_op jit(solution)/shard_map/ppermute | solution.py:43
  40.6 11.9 %collective-permute-start.3 = (bf16[256,1152]{1,0:T(8,128)(2,1)}, bf16[256,1152]{1,0:T(8,128)(2,1)}, u32[]{:S(2)}, u32[]{:S(2)}) collective-permute-start(bf16[256,1152]{1,0:T(8,128)(2,1)} %collective-permute-done.2.first), channel_id=1, source_target_pairs={{12,124},{13,125},{14,126},{15,127},{28,12},{29,13},{30,14},{31,15... | collective-permute-start | bytes 1769480 | tf_op jit(solution)/shard_map/ppermute | solution.py:43
  42.1 1.7 %copy-start.1 = (f32[520,1152]{1,0:T(8,128)S(1)}, f32[520,1152]{1,0:T(8,128)}, u32[]{:S(2)}) copy-start(f32[520,1152]{1,0:T(8,128)} %copy-done) | copy-start | bytes 7188484
  52.5 2.9 %copy-start.2 = (f32[520,1152]{1,0:T(8,128)}, f32[520,1152]{1,0:T(8,128)S(1)}, u32[]{:S(2)}) copy-start(f32[520,1152]{1,0:T(8,128)S(1)} %get-tuple-element.27.mine) | copy-start | bytes 7188484
  55.5 3.2 %collective-permute-start.5 = (bf16[528,1152]{1,0:T(8,128)(2,1)S(1)}, bf16[528,1152]{1,0:T(8,128)(2,1)S(1)}, u32[]{:S(2)}, u32[]{:S(2)}) collective-permute-start(bf16[528,1152]{1,0:T(8,128)(2,1)S(1)} %shard_map.78.refs_0_), channel_id=1, source_target_pairs={{0,1},{1,0},{2,3},{3,2},{4,5},{5,4},{6,7},{7,6},{8,9},{9,8},{10,11... | collective-permute-start | bytes 3649544 | tf_op jit(solution)/shard_map/ppermute | solution.py:43
  65.8 1.4 %copy-start.6 = (f32[512,1152]{1,0:T(8,128)}, f32[512,1152]{1,0:T(8,128)S(1)}, u32[]{:S(2)}) copy-start(f32[512,1152]{1,0:T(8,128)S(1)} %get-tuple-element.45.two) | copy-start | bytes 7077892
  74.7 2.9 %collective-permute-start.6 = (bf16[528,1152]{1,0:T(8,128)(2,1)S(1)}, bf16[528,1152]{1,0:T(8,128)(2,1)S(1)}, u32[]{:S(2)}, u32[]{:S(2)}) collective-permute-start(bf16[528,1152]{1,0:T(8,128)(2,1)S(1)} %get-tuple-element.37), channel_id=1, source_target_pairs={{0,1},{1,0},{2,3},{3,2},{4,5},{5,4},{6,7},{7,6},{8,9},{9,8},{10,11... | collective-permute-start | bytes 3649544 | tf_op jit(solution)/shard_map/ppermute | solution.py:43
  77.6 20.5 %copy-start.5 = (f32[512,1152]{1,0:T(8,128)S(1)}, f32[512,1152]{1,0:T(8,128)}, u32[]{:S(2)}) copy-start(f32[512,1152]{1,0:T(8,128)} %copy-done.4) | copy-start | bytes 7077892
  78.6 48.8 %collective-permute-start.7 = (f32[520,1152]{1,0:T(8,128)}, f32[520,1152]{1,0:T(8,128)}, u32[]{:S(2)}, u32[]{:S(2)}) collective-permute-start(f32[520,1152]{1,0:T(8,128)} %get-tuple-element.39), channel_id=1, source_target_pairs={{0,1},{1,0},{2,3},{3,2},{4,5},{5,4},{6,7},{7,6},{8,9},{9,8},{10,11... | collective-permute-start | bytes 7188488 | tf_op jit(solution)/shard_map/ppermute | solution.py:43
  78.7 16.9 %collective-permute-start.8 = (bf16[256,1152]{1,0:T(8,128)(2,1)S(1)}, bf16[256,1152]{1,0:T(8,128)(2,1)}, u32[]{:S(2)}, u32[]{:S(2)}) collective-permute-start(bf16[256,1152]{1,0:T(8,128)(2,1)S(1)} %get-tuple-element.38), channel_id=1, source_target_pairs={{0,4},{1,5},{2,6},{3,7},{4,8},{5,9},{6,10},{7,11},{8,12},{9,13},{1... | collective-permute-start | bytes 1769480 | tf_op jit(solution)/shard_map/ppermute | solution.py:43
  78.7 30.5 %collective-permute-start.11 = (bf16[512,1152]{1,0:T(8,128)(2,1)}, bf16[512,1152]{1,0:T(8,128)(2,1)S(1)}, u32[]{:S(2)}, u32[]{:S(2)}) collective-permute-start(bf16[512,1152]{1,0:T(8,128)(2,1)} %get-tuple-element.46), channel_id=1, source_target_pairs={{0,2},{1,3},{2,0},{3,1},{4,6},{5,7},{6,4},{7,5},{8,10},{9,11},{10,... | collective-permute-start | bytes 3538952 | tf_op jit(solution)/shard_map/ppermute | solution.py:43
  95.6 31.8 %collective-permute-start.10 = (bf16[272,1152]{1,0:T(8,128)(2,1)}, bf16[272,1152]{1,0:T(8,128)(2,1)}, u32[]{:S(2)}, u32[]{:S(2)}) collective-permute-start(bf16[272,1152]{1,0:T(8,128)(2,1)} %get-tuple-element.41), channel_id=1, source_target_pairs={{0,4},{1,5},{2,6},{3,7},{4,8},{5,9},{6,10},{7,11},{8,12},{9,13},{1... | collective-permute-start | bytes 1880072 | tf_op jit(solution)/shard_map/ppermute | solution.py:43
  95.6 25.2 %collective-permute-start.9 = (bf16[256,1152]{1,0:T(8,128)(2,1)}, bf16[256,1152]{1,0:T(8,128)(2,1)}, u32[]{:S(2)}, u32[]{:S(2)}) collective-permute-start(bf16[256,1152]{1,0:T(8,128)(2,1)} %collective-permute-done.8.first), channel_id=1, source_target_pairs={{0,16},{1,17},{2,18},{3,19},{16,32},{17,33},{18,34},{19,35},{32,48... | collective-permute-start | bytes 1769480 | tf_op jit(solution)/shard_map/ppermute | solution.py:43
  98.1 1.7 %copy-start.7 = (f32[512,1152]{1,0:T(8,128)S(1)}, f32[512,1152]{1,0:T(8,128)}, u32[]{:S(2)}) copy-start(f32[512,1152]{1,0:T(8,128)} %copy-done.6) | copy-start | bytes 7077892
  100.2 27.2 %copy-start.3 = (f32[520,1152]{1,0:T(8,128)S(1)}, f32[520,1152]{1,0:T(8,128)}, u32[]{:S(2)}) copy-start(f32[520,1152]{1,0:T(8,128)} %copy-done.2) | copy-start | bytes 7188484

commit v3 on v2

--- a/solution.py
+++ b/solution.py
@@ -61,6 +61,7 @@
 SMEM = pl.BlockSpec(memory_space=pltpu.SMEM)
 VMEM = pl.BlockSpec(memory_space=pltpu.VMEM)
 ROWS, WIDTH, HALF = 512, 1152, 256
+FIRST = 256
 CARRY = 16
 
 
@@ -104,7 +105,7 @@
     return parts[0:1] + parts[1:2] + parts[2:3]
 
 
-def pair_body(gi_has, gt_has, start_ref, scale_ref, offset_ref, *refs):
+def pair_body(n, gi_has, gt_has, start_ref, scale_ref, offset_ref, *refs):
     refs = list(refs)
 
     def take(count):
@@ -112,15 +113,15 @@
         del refs[:count]
         return out
 
-    imgs, txt = take(2), take(1)[0]
-    gi_in = take(2) if gi_has else None
+    imgs, txt = take(n), take(1)[0]
+    gi_in = take(n) if gi_has else None
     gt_in = take(1)[0] if gt_has else None
-    gi, gt = take(2), take(1)[0]
+    gi, gt = take(n), take(1)[0]
     temper, shift = scale_ref[0], offset_ref[0]
     t = txt[...]
-    col = start_ref[0] + lax.broadcasted_iota(jnp.int32, (ROWS, ROWS), 0).astype(F32)
-    t_sum = gt_in[...] if gt_has else None
-    for m in range(2):
+    col = start_ref[0] + lax.broadcasted_iota(jnp.int32, (t.shape[0], ROWS), 0).astype(F32)
+    t_sum = None
+    for m in range(n):
         a = imgs[m][:ROWS, :]
         code = imgs[m][pl.ds(ROWS, CARRY), :ROWS].astype(F32)
         partner = code[0:1] * 256.0 + code[1:2]
@@ -135,6 +136,8 @@
         gi[m][:ROWS, :] = g.astype(gi[m].dtype)
         put_loss(gi[m], ROWS, loss)
         t_sum = d if t_sum is None else t_sum + d
+    if gt_has:
+        t_sum = t_sum + gt_in[...]
     gt[...] = t_sum.astype(gt.dtype)
 
 
@@ -142,18 +145,19 @@
     return pltpu.VMEM((ROWS + (8 if ty == F32 else CARRY), WIDTH), ty)
 
 
-def pairs(imgs, txt, start, scale, offset, gi=None, gt=None, gi_types=(F32, F32), gt_type=F32):
-    arrays = [*imgs, txt, *(gi or []), *([gt] if gt is not None else [])]
-    alias = {}
-    if gi is not None:
-        alias.update({6 + m: m for m in range(2) if gi_types[m] == F32})
-    if gt is not None and gt_type == F32:
-        alias[5 + len(arrays) - 3] = 2
-    outs = [grad_shape(ty) for ty in gi_types] + [pltpu.VMEM((ROWS, WIDTH), gt_type)]
+def pairs(imgs, txt, start, scale, offset, gi=None, gi_types=None, gt=None, gt_type=F32):
+    n = len(imgs)
+    gi_types = gi_types or [F32] * n
+    alias = {4 + n + m: m for m in range(n) if gi is not None and gi_types[m] == F32}
+    outs = [grad_shape(ty) for ty in gi_types] + [pltpu.VMEM(txt.shape, gt_type)]
     got = call(
-        functools.partial(pair_body, gi is not None, gt is not None), (start, scale, offset), arrays, outs, alias
-    )
-    return got[:2], got[2]
+        functools.partial(pair_body, n, gi is not None, gt is not None),
+        (start, scale, offset),
+        [*imgs, txt, *(gi or []), *([gt] if gt is not None else [])],
+        outs,
+        alias,
+    )
+    return got[:n], got[n]
 
 
 def assemble_body(flag_ref, first, turned, rest, out):
@@ -167,12 +171,11 @@
     put_loss(rest, HALF, get_loss(mine, ROWS) + get_loss(other, ROWS))
 
 
-def image_body(flag_ref, mine, other, first, turned, rest, grad, row_loss):
+def image_body(flag_ref, mine, first, turned, rest, grad, row_loss):
     top = jnp.where(flag_ref[0] == 1, turned[...], first[...]).astype(F32)
-    grad[:HALF, :] = (mine[:HALF, :] + other[:HALF, :] + top).astype(BF16)
-    below = rest[:HALF, :].astype(F32)
-    grad[HALF:, :] = (mine[HALF:ROWS, :] + other[HALF:ROWS, :] + below).astype(BF16)
-    loss = get_loss(mine, ROWS) + get_loss(other, ROWS) + get_loss(rest, HALF)
+    grad[:HALF, :] = (mine[:HALF, :] + top).astype(BF16)
+    grad[HALF:, :] = (mine[HALF:ROWS, :] + rest[:HALF, :].astype(F32)).astype(BF16)
+    loss = get_loss(mine, ROWS) + get_loss(rest, HALF)
     row_loss[...] = loss / (8.0 * ROWS)
 
 
@@ -180,8 +183,9 @@
     out[...] = one[...] + two[...]
 
 
-def text_body(mine, back, grad):
-    grad[...] = (mine[...] + back[...].astype(F32)).astype(BF16)
+def text_body(mine, back1, back2, grad):
+    grad[:FIRST, :] = (mine[:FIRST, :] + back1[...].astype(F32)).astype(BF16)
+    grad[FIRST:, :] = (mine[FIRST:, :] + back2[...].astype(F32)).astype(BF16)
 
 
 def body(images, texts, partner, scale, offset):
@@ -196,33 +200,40 @@
 
     code = jnp.stack([partner // 256, partner % 256]).astype(BF16)
     own = jnp.concatenate([images, jnp.pad(code, ((0, CARRY - 2), (0, WIDTH - ROWS)))])
-    far = send(texts, across)
+    far1 = send(texts[:FIRST], across)
     first = send(images[:HALF], moved(z=-1))
     own2 = send(own, swap)
     (ga, ga2), gs = pairs([own, own2], texts, start, scale, offset)
-    turned = send(after(first, gs), last_hop(-1))
-    rest = send(after(own[HALF:], far, gs), along_loop(-1))
-    (ga, ga2), gu = pairs([own, own2], far, far_start, scale, offset, [ga, ga2])
+    rest = send(after(own[HALF:], first, gs, far1), along_loop(-1))
+    turned = send(after(first, gs, far1), last_hop(-1))
+    (ga, ga2), gu = pairs([own, own2], far1, far_start, scale, offset, [ga, ga2])
+    far2 = send(after(texts[FIRST:], far1), across)
     visitor = call(
         assemble_body, (flag(3),), (after(first, gu), turned, rest), [pltpu.VMEM((ROWS + CARRY, WIDTH), BF16)]
     )[0]
     visitor2 = send(visitor, swap)
     (gb, gb2), gs2 = pairs([visitor, visitor2], texts, start, scale, offset)
-    (gb, gb2), gu = pairs([visitor, visitor2], far, far_start, scale, offset, [gb, gb2], gu, (F32, BF16), BF16)
-    gu_back = send(gu, across)
-    gb_got = send(gb2, swap)
+    (gb, gb2), gu = pairs([visitor, visitor2], far1, far_start, scale, offset, [gb, gb2], None, gu, BF16)
+    every = [own, own2, visitor, visitor2]
+    gu1_back = send(gu, across)
+    (ga, ga2, gb, gb2), gu2 = pairs(
+        every, far2, far_start + FIRST, scale, offset, [ga, ga2, gb, gb2], [F32, F32, F32, BF16], None, BF16
+    )
+    gu2_back = send(gu2, across)
+    gb_got = send(after(gb2, gu1_back), swap)
     top, bottom = call(
         fold_body, (), (gb, gb_got),
         [pltpu.VMEM((HALF, WIDTH), BF16), pltpu.VMEM((HALF + CARRY, WIDTH), BF16)],
     )
     back_first = send(top, moved(z=1))
-    back_rest = send(after(bottom, back_first), along_loop(1))
+    back_rest = send(after(bottom, back_first, gu2_back), along_loop(1))
     gs = call(add_body, (), (after(gs, top), gs2), [pltpu.VMEM((ROWS, WIDTH), F32)], {0: 0})[0]
-    back_turned = send(back_first, last_hop(1))
+    back_turned = send(after(back_first, gu2_back), last_hop(1))
     ga_got = send(after(ga2, top), swap)
-    grad_texts = call(text_body, (), (gs, gu_back), [jax.ShapeDtypeStruct((ROWS, WIDTH), BF16)])[0]
+    ga = call(add_body, (), (ga, ga_got), [grad_shape(F32)], {0: 0})[0]
+    grad_texts = call(text_body, (), (gs, gu1_back, gu2_back), [jax.ShapeDtypeStruct((ROWS, WIDTH), BF16)])[0]
     grad_images, row_loss = call(
-        image_body, (flag(0),), (ga, ga_got, back_first, back_turned, back_rest),
+        image_body, (flag(0),), (ga, back_first, back_turned, back_rest),
         [jax.ShapeDtypeStruct((ROWS, WIDTH), BF16), jax.ShapeDtypeStruct((1, ROWS), F32)],
     )
     return row_loss[0], grad_images, grad_texts

time: 132 us -> 121 us (0.917)
  waiting for transfers between devices: 56.1 us -> 33.9 us
  local copies, waits for them, and re-layouts: 8.52 us -> 19.1 us
    ppermute x12 -> x14, waiting for transfers between devices: 56.1 us -> 33.9 us  [send(): return lax.ppermute(block, AXES, route)]
    unnamed x18 -> x46, local copies, waits for them, and re-layouts: 7.65 us -> 16.9 us
    ppermute x12 -> x14, starting transfers between devices: 22.1 us -> 22.9 us  [send(): return lax.ppermute(block, AXES, route)]
    pallas_call x9 -> x11, Pallas kernels: 38 us -> 38.2 us  [call(): pl.pallas_call(kernel, in_specs=[SMEM] * len(smalls) + [VMEM] * len(array...]
  transfers between devices with their start and end apart: 12 -> 14, of which waited for: 8 -> 8; matrix products, arithmetic and copies ran while one was open for 2% -> 3% of each run, Pallas kernels for 13% -> 27%
where the time goes in v3:
time: 121 us; the launch traced here: 120 us
  Pallas kernels  38.2 us (32%)
  waiting for transfers between devices  33.9 us (28%)
  starting transfers between devices  22.9 us (19%)
  local copies, waits for them, and re-layouts  19.1 us (16%)
  other arithmetic  4.21 us (3%)
  between operations  2.22 us (2%)
    pallas_call x11, Pallas kernels, call(): pl.pallas_call(kernel, in_specs=[SMEM] * len(smalls) + [VMEM] * len(array...  38.2 us
    ppermute x14, waiting for transfers between devices, send(): return lax.ppermute(block, AXES, route)  33.9 us
    ppermute x14, starting transfers between devices, send(): return lax.ppermute(block, AXES, route)  22.9 us
    unnamed x46, local copies, waits for them, and re-layouts  16.9 us
    concatenate x2, other arithmetic, body(): jnp.concatenate([images, jnp.pad(code, ((0, CARRY - 2), (0, WIDTH - ROWS)...  3.4 us
  transfers between devices with their start and end apart: 14, of which 8 were waited for; matrix products, arithmetic and copies ran while one was open for 3% of the time, Pallas kernels for 27%

profile of v3, /device:TPU:0, one launch (start us, length us, event | category | flops | bytes accessed | tf_op | source)
XLA Modules:
  0.0 120.5 jit_solution(10055163603981459852)
XLA Ops:
  0.6 0.8 fusion.7
  1.5 1.5 %pad_maximum_fusion.refs_0_ = bf16[528,1152]{1,0:T(8,128)(2,1)S(1)} fusion(bf16[16,1152]{1,0:T(8,128)(2,1)S(1)} %fusion.6, bf16[512,1152]{1,0:T(8,128)(2,1)} %param.5), kind=kLoop, calls=%fused_computation.1 | loop fusion | flops 2433024 | bytes 2433024 | tf_op jit(solution)/shard_map/concatenate | solution.py:202
  3.0 0.1 collective-permute-start
  3.1 1.0 slice.12
  4.1 4.1 %collective-permute-start.1 = (bf16[256,1152]{1,0:T(8,128)(2,1)}, bf16[256,1152]{1,0:T(8,128)(2,1)}, u32[]{:S(2)}, u32[]{:S(2)}) collective-permute-start(bf16[256,1152]{1,0:T(8,128)(2,1)} %slice.12), channel_id=1, source_target_pairs={{0,12},{1,13},{2,14},{3,15},{4,0},{5,1},{6,2},{7,3},{8,4},{9,5},{1... | collective-permute-start | bytes 1769480 | tf_op jit(solution)/shard_map/ppermute | solution.py:43
  8.2 1.1 fusion.10
  9.3 3.0 %collective-permute-start.2 = (bf16[256,1152]{1,0:T(8,128)(2,1)}, bf16[256,1152]{1,0:T(8,128)(2,1)S(1)}, u32[]{:S(2)}, u32[]{:S(2)}) collective-permute-start(bf16[256,1152]{1,0:T(8,128)(2,1)} %get-tuple-element.64), channel_id=1, source_target_pairs={{0,2},{1,3},{2,0},{3,1},{4,6},{5,7},{6,4},{7,5},{8,10},{9,11},{10,... | collective-permute-start | bytes 1769480 | tf_op jit(solution)/shard_map/ppermute | solution.py:43
  13.7 1.9 %fusion = bf16[272,1152]{1,0:T(8,128)(2,1)} fusion(bf16[512,1152]{1,0:T(8,128)(2,1)} %param.5, bf16[16,1152]{1,0:T(8,128)(2,1)S(1)} %fusion.6), kind=kLoop, calls=%fused_computation.3 | loop fusion | flops 1253376 | bytes 1843200 | tf_op jit(solution)/shard_map/concatenate | solution.py:202
  15.7 1.0 copy-done.4
  16.7 1.3 %copy-done.5 = bf16[528,1152]{1,0:T(8,128)(2,1)S(1)} copy-done((bf16[528,1152]{1,0:T(8,128)(2,1)S(1)}, bf16[528,1152]{1,0:T(8,128)(2,1)}, u32[]{:S(2)}) %copy-start.5) | copy-done | bytes 1216536
  18.0 1.3 %copy-done.9 = bf16[512,1152]{1,0:T(8,128)(2,1)S(1)} copy-done((bf16[512,1152]{1,0:T(8,128)(2,1)S(1)}, bf16[512,1152]{1,0:T(8,128)(2,1)}, u32[]{:S(2)}) %copy-start.9) | copy-done | bytes 1179672
  19.3 6.0 %shard_map.76 = (f32[520,1152]{1,0:T(8,128)S(1)}, f32[520,1152]{1,0:T(8,128)}, f32[512,1152]{1,0:T(8,128)S(1)}) custom-call(f32[1]{0:T(128)} %bitcast.3.start_ref, f32[1]{0:T(128)S(6)} %copy.26.scale_ref, f32[1]{0:T(128)S(6)} %copy.27.offset_ref, bf16[528,1152]{1,0:T(8,128)(2,1)S(1)} %copy-done.1, bf16[528,1152]{1,0:T(8,128)(2,1)S(1)} %copy-done.5, ...), custom_call_target="tpu_custom_call" | custom-call | flops 1000 | bytes 1000 | tf_op jit(solution)/shard_map/pallas_call | solution.py:73
  25.3 1.4 %copy-done.11 = f32[512,1152]{1,0:T(8,128)} copy-done((f32[512,1152]{1,0:T(8,128)}, f32[512,1152]{1,0:T(8,128)S(1)}, u32[]{:S(2)}) %copy-start.11) | copy-done | bytes 2359320
  26.7 3.4 %collective-permute-start.4 = (bf16[272,1152]{1,0:T(8,128)(2,1)}, bf16[272,1152]{1,0:T(8,128)(2,1)}, u32[]{:S(2)}, u32[]{:S(2)}) collective-permute-start(bf16[272,1152]{1,0:T(8,128)(2,1)} %fusion), channel_id=1, source_target_pairs={{0,124},{1,125},{2,126},{3,127},{4,0},{5,1},{6,2},{7,3},{8,4},{9,5... | collective-permute-start | bytes 1880072 | tf_op jit(solution)/shard_map/ppermute | solution.py:43
  30.1 1.5 %collective-permute-start.3 = (bf16[256,1152]{1,0:T(8,128)(2,1)}, bf16[256,1152]{1,0:T(8,128)(2,1)}, u32[]{:S(2)}, u32[]{:S(2)}) collective-permute-start(bf16[256,1152]{1,0:T(8,128)(2,1)} %collective-permute-done.1.first), channel_id=1, source_target_pairs={{12,124},{13,125},{14,126},{15,127},{28,12},{29,13},{30,14},{31,15... | collective-permute-start | bytes 1769480 | tf_op jit(solution)/shard_map/ppermute | solution.py:43
  31.6 1.3 %copy-done.2 = bf16[528,1152]{1,0:T(8,128)(2,1)S(1)} copy-done((bf16[528,1152]{1,0:T(8,128)(2,1)S(1)}, bf16[528,1152]{1,0:T(8,128)(2,1)}, u32[]{:S(2)}) %copy-start.2) | copy-done | bytes 1216536
  32.9 1.3 %copy-done.6 = bf16[528,1152]{1,0:T(8,128)(2,1)S(1)} copy-done((bf16[528,1152]{1,0:T(8,128)(2,1)S(1)}, bf16[528,1152]{1,0:T(8,128)(2,1)}, u32[]{:S(2)}) %copy-start.6) | copy-done | bytes 1216536
  34.2 6.0 %shard_map.77 = (f32[520,1152]{1,0:T(8,128)S(1)}, f32[520,1152]{1,0:T(8,128)}, f32[256,1152]{1,0:T(8,128)S(1)}) custom-call(f32[1]{0:T(128)} %bitcast.1.start_ref, f32[1]{0:T(128)S(6)} %copy.26.scale_ref, f32[1]{0:T(128)S(6)} %copy.27.offset_ref, bf16[528,1152]{1,0:T(8,128)(2,1)S(1)} %copy-done.2, ...), custom_call_target="tpu_custom_call", output_to_operand_aliasing={{0}: (6, {}), {1}: (7, {})} | custom-call | flops 1000 | bytes 1000 | tf_op jit(solution)/shard_map/pallas_call | solution.py:73
  40.2 3.0 %collective-permute-done.4.rest = bf16[272,1152]{1,0:T(8,128)(2,1)} collective-permute-done((bf16[272,1152]{1,0:T(8,128)(2,1)}, bf16[272,1152]{1,0:T(8,128)(2,1)}, u32[]{:S(2)}, u32[]{:S(2)}) %collective-permute-start.4) | collective-permute-done | bytes 626720 | tf_op jit(solution)/shard_map/ppermute | solution.py:43
  43.2 1.7 %shard_map.78.refs_0_.refs_2_ = bf16[528,1152]{1,0:T(8,128)(2,1)S(1)} custom-call(s32[1]{0:T(128)} %bitcast.2.flag_ref, bf16[256,1152]{1,0:T(8,128)(2,1)} %collective-permute-done.1.first, bf16[256,1152]{1,0:T(8,128)(2,1)} %collective-permute-done.3.turned, bf16[272,1152]{1,0:T(8,128)(2,1)} %collective-permute-done.4.rest), custom_call_target="tpu_custom_call" | custom-call | flops 1000 | bytes 1000 | tf_op jit(solution)/shard_map/pallas_call | solution.py:73
  44.9 0.1 collective-permute-start.5
  45.0 3.0 %collective-permute-start.6 = (bf16[256,1152]{1,0:T(8,128)(2,1)S(1)}, bf16[256,1152]{1,0:T(8,128)(2,1)S(1)}, u32[]{:S(2)}, u32[]{:S(2)}) collective-permute-start(bf16[256,1152]{1,0:T(8,128)(2,1)S(1)} %copy-done.22), channel_id=1, source_target_pairs={{0,2},{1,3},{2,0},{3,1},{4,6},{5,7},{6,4},{7,5},{8,10},{9,11},{10,... | collective-permute-start | bytes 1769480 | tf_op jit(solution)/shard_map/ppermute | solution.py:43
  48.0 5.8 %shard_map.79 = (f32[520,1152]{1,0:T(8,128)S(1)}, f32[520,1152]{1,0:T(8,128)S(1)}, f32[512,1152]{1,0:T(8,128)S(1)}) custom-call(f32[1]{0:T(128)} %bitcast.3.start_ref, f32[1]{0:T(128)S(6)} %copy.26.scale_ref, f32[1]{0:T(128)S(6)} %copy.27.offset_ref, bf16[528,1152]{1,0:T(8,128)(2,1)S(1)} %shard_map.78.refs_0_.refs_2_, ...), custom_call_target="tpu_custom_call" | custom-call | flops 1000 | bytes 1000 | tf_op jit(solution)/shard_map/pallas_call | solution.py:73
  53.9 3.6 %shard_map.80 = (f32[520,1152]{1,0:T(8,128)S(1)}, f32[520,1152]{1,0:T(8,128)S(1)}, bf16[256,1152]{1,0:T(8,128)(2,1)S(1)}) custom-call(f32[1]{0:T(128)} %bitcast.1.start_ref, f32[1]{0:T(128)S(6)} %copy.26.scale_ref, f32[1]{0:T(128)S(6)} %copy.27.offset_ref, ...), custom_call_target="tpu_custom_call", output_to_operand_aliasing={{0}: (6, {}), {1}: (7, {})} | custom-call | flops 1000 | bytes 1000 | tf_op jit(solution)/shard_map/pallas_call | solution.py:73
  57.5 2.9 %collective-permute-start.7 = (bf16[256,1152]{1,0:T(8,128)(2,1)S(1)}, bf16[256,1152]{1,0:T(8,128)(2,1)S(1)}, u32[]{:S(2)}, u32[]{:S(2)}) collective-permute-start(bf16[256,1152]{1,0:T(8,128)(2,1)S(1)} %get-tuple-element.51), channel_id=1, source_target_pairs={{0,2},{1,3},{2,0},{3,1},{4,6},{5,7},{6,4},{7,5},{8,10},{9,11},{10,... | collective-permute-start | bytes 1769480 | tf_op jit(solution)/shard_map/ppermute | solution.py:43
  60.4 2.1 %collective-permute-done.6.refs_4_ = bf16[256,1152]{1,0:T(8,128)(2,1)S(1)} collective-permute-done((bf16[256,1152]{1,0:T(8,128)(2,1)S(1)}, bf16[256,1152]{1,0:T(8,128)(2,1)S(1)}, u32[]{:S(2)}, u32[]{:S(2)}) %collective-permute-start.6) | collective-permute-done | bytes 589856 | tf_op jit(solution)/shard_map/ppermute | solution.py:43
  62.5 7.8 %shard_map.81 = (f32[520,1152]{1,0:T(8,128)S(1)}, f32[520,1152]{1,0:T(8,128)}, f32[520,1152]{1,0:T(8,128)S(1)}, bf16[528,1152]{1,0:T(8,128)(2,1)S(1)}, bf16[256,1152]{1,0:T(8,128)(2,1)S(1)}) custom-call(f32[1]{0:T(128)S(6)} %add.25.start_ref, f32[1]{0:T(128)S(6)} %copy.26.scale_ref, ...), custom_call_target="tpu_custom_call", output_to_operand_aliasing={{0}: (8, {}), {1}: (9, {}), {2}: (10, {})} | custom-call | flops 1000 | bytes 1000 | tf_op jit(solution)/shard_map/pallas_call | solution.py:73
  70.3 4.6 %collective-permute-done.7.back1 = bf16[256,1152]{1,0:T(8,128)(2,1)S(1)} collective-permute-done((bf16[256,1152]{1,0:T(8,128)(2,1)S(1)}, bf16[256,1152]{1,0:T(8,128)(2,1)S(1)}, u32[]{:S(2)}, u32[]{:S(2)}) %collective-permute-start.7) | collective-permute-done | bytes 589856 | tf_op jit(solution)/shard_map/ppermute | solution.py:43
  74.9 2.9 %collective-permute-done.8.other = bf16[528,1152]{1,0:T(8,128)(2,1)S(1)} collective-permute-done((bf16[528,1152]{1,0:T(8,128)(2,1)S(1)}, bf16[528,1152]{1,0:T(8,128)(2,1)S(1)}, u32[]{:S(2)}, u32[]{:S(2)}) %collective-permute-start.8) | collective-permute-done | bytes 1216544 | tf_op jit(solution)/shard_map/ppermute | solution.py:43
  77.8 1.0 shard_map.82
  78.8 0.1 collective-permute-start.9
  78.9 2.7 %collective-permute-start.11 = (bf16[256,1152]{1,0:T(8,128)(2,1)S(1)}, bf16[256,1152]{1,0:T(8,128)(2,1)S(1)}, u32[]{:S(2)}, u32[]{:S(2)}) collective-permute-start(bf16[256,1152]{1,0:T(8,128)(2,1)S(1)} %get-tuple-element.55), channel_id=1, source_target_pairs={{0,2},{1,3},{2,0},{3,1},{4,6},{5,7},{6,4},{7,5},{8,10},{9,11},{10,... | collective-permute-start | bytes 1769480 | tf_op jit(solution)/shard_map/ppermute | solution.py:43
  81.7 14.4 %collective-permute-done.11.back2 = bf16[256,1152]{1,0:T(8,128)(2,1)S(1)} collective-permute-done((bf16[256,1152]{1,0:T(8,128)(2,1)S(1)}, bf16[256,1152]{1,0:T(8,128)(2,1)S(1)}, u32[]{:S(2)}, u32[]{:S(2)}) %collective-permute-start.11) | collective-permute-done | bytes 589856 | tf_op jit(solution)/shard_map/ppermute | solution.py:43
  96.1 0.8 copy-done.19
  96.9 1.4 %collective-permute-done.10.first = bf16[256,1152]{1,0:T(8,128)(2,1)} collective-permute-done((bf16[256,1152]{1,0:T(8,128)(2,1)S(1)}, bf16[256,1152]{1,0:T(8,128)(2,1)}, u32[]{:S(2)}, u32[]{:S(2)}) %collective-permute-start.10) | collective-permute-done | bytes 589856 | tf_op jit(solution)/shard_map/ppermute | solution.py:43
  98.3 1.9 %collective-permute-start.12 = (bf16[256,1152]{1,0:T(8,128)(2,1)}, bf16[256,1152]{1,0:T(8,128)(2,1)}, u32[]{:S(2)}, u32[]{:S(2)}) collective-permute-start(bf16[256,1152]{1,0:T(8,128)(2,1)} %collective-permute-done.10.first), channel_id=1, source_target_pairs={{0,16},{1,17},{2,18},{3,19},{16,32},{17,33},{18,34},{19,35},{32,48... | collective-permute-start | bytes 1769480 | tf_op jit(solution)/shard_map/ppermute | solution.py:43
  100.3 1.7 %copy-done.12 = f32[512,1152]{1,0:T(8,128)S(1)} copy-done((f32[512,1152]{1,0:T(8,128)S(1)}, f32[512,1152]{1,0:T(8,128)}, u32[]{:S(2)}) %copy-start.12) | copy-done | bytes 2359320
  101.9 1.7 %copy-done.16 = f32[512,1152]{1,0:T(8,128)S(1)} copy-done((f32[512,1152]{1,0:T(8,128)S(1)}, f32[512,1152]{1,0:T(8,128)}, u32[]{:S(2)}) %copy-start.16) | copy-done | bytes 2359320
  103.6 0.4 shard_map.85.mine
  104.0 1.4 %copy-done.13 = f32[512,1152]{1,0:T(8,128)} copy-done((f32[512,1152]{1,0:T(8,128)}, f32[512,1152]{1,0:T(8,128)S(1)}, u32[]{:S(2)}) %copy-start.13) | copy-done | bytes 2359320
  105.4 1.7 %copy-done.14 = f32[512,1152]{1,0:T(8,128)S(1)} copy-done((f32[512,1152]{1,0:T(8,128)S(1)}, f32[512,1152]{1,0:T(8,128)}, u32[]{:S(2)}) %copy-start.14) | copy-done | bytes 2359320
  107.1 1.1 copy-done.18
  108.1 1.1 copy-done.20
  109.2 1.2 %shard_map.86 = bf16[512,1152]{1,0:T(8,128)(2,1)} custom-call(f32[512,1152]{1,0:T(8,128)S(1)} %copy-done.14, bf16[256,1152]{1,0:T(8,128)(2,1)S(1)} %copy-done.18, bf16[256,1152]{1,0:T(8,128)(2,1)S(1)} %copy-done.20), custom_call_target="tpu_custom_call" | custom-call | flops 1000 | bytes 1000 | tf_op jit(solution)/shard_map/pallas_call | solution.py:73
  110.4 2.1 %shard_map.83.mine = f32[520,1152]{1,0:T(8,128)S(1)} custom-call(f32[520,1152]{1,0:T(8,128)S(1)} %get-tuple-element.47.one, f32[520,1152]{1,0:T(8,128)} %collective-permute-done.9.two), custom_call_target="tpu_custom_call", output_to_operand_aliasing={{}: (0, {})} | custom-call | flops 1000 | bytes 1000 | tf_op jit(solution)/shard_map/pallas_call | solution.py:73
  112.5 4.8 %collective-permute-done.12.turned = bf16[256,1152]{1,0:T(8,128)(2,1)} collective-permute-done((bf16[256,1152]{1,0:T(8,128)(2,1)}, bf16[256,1152]{1,0:T(8,128)(2,1)}, u32[]{:S(2)}, u32[]{:S(2)}) %collective-permute-start.12) | collective-permute-done | bytes 589856 | tf_op jit(solution)/shard_map/ppermute | solution.py:43
  117.3 0.7 collective-permute-done.13.rest
  118.0 2.5 %shard_map.84 = (bf16[512,1152]{1,0:T(8,128)(2,1)}, f32[1,512]{1,0:T(1,128)}) custom-call(s32[1]{0:T(128)} %bitcast.flag_ref, f32[520,1152]{1,0:T(8,128)S(1)} %shard_map.83.mine, bf16[256,1152]{1,0:T(8,128)(2,1)} %collective-permute-done.10.first, bf16[256,1152]{1,0:T(8,128)(2,1)} %collective-permute-done.12.turned, ...), custom_call_target="tpu_custom_call" | custom-call | flops 1000 | bytes 1000 | tf_op jit(solution)/shard_map/pallas_call | solution.py:73
  (45 shorter events, 0.1 us)
Async XLA Ops:
  0.6 2.4 %copy-start.21 = (bf16[512,1152]{1,0:T(8,128)(2,1)S(1)}, bf16[512,1152]{1,0:T(8,128)(2,1)}, u32[]{:S(2)}) copy-start(bf16[512,1152]{1,0:T(8,128)(2,1)} %param.5) | copy-start | bytes 3538948
  1.5 6.7 %copy-start.8 = (bf16[512,1152]{1,0:T(8,128)(2,1)S(1)}, bf16[512,1152]{1,0:T(8,128)(2,1)}, u32[]{:S(2)}) copy-start(bf16[512,1152]{1,0:T(8,128)(2,1)} %refs_2_.3) | copy-start | bytes 3538948
  2.9 6.4 %copy-start = (bf16[528,1152]{1,0:T(8,128)(2,1)}, bf16[528,1152]{1,0:T(8,128)(2,1)S(1)}, u32[]{:S(2)}) copy-start(bf16[528,1152]{1,0:T(8,128)(2,1)S(1)} %pad_maximum_fusion.refs_0_) | copy-start | bytes 3649540
  3.0 12.7 %collective-permute-start = (bf16[528,1152]{1,0:T(8,128)(2,1)S(1)}, bf16[528,1152]{1,0:T(8,128)(2,1)S(1)}, u32[]{:S(2)}, u32[]{:S(2)}) collective-permute-start(bf16[528,1152]{1,0:T(8,128)(2,1)S(1)} %pad_maximum_fusion.refs_0_), channel_id=1, source_target_pairs={{0,1},{1,0},{2,3},{3,2},{4,5},{5,4},{6,7},{7,6},{8,9},{9,8},{10,11... | collective-permute-start | bytes 3649544 | tf_op jit(solution)/shard_map/ppermute | solution.py:43
  4.1 22.6 %collective-permute-start.1 = (bf16[256,1152]{1,0:T(8,128)(2,1)}, bf16[256,1152]{1,0:T(8,128)(2,1)}, u32[]{:S(2)}, u32[]{:S(2)}) collective-permute-start(bf16[256,1152]{1,0:T(8,128)(2,1)} %slice.12), channel_id=1, source_target_pairs={{0,12},{1,13},{2,14},{3,15},{4,0},{5,1},{6,2},{7,3},{8,4},{9,5},{1... | collective-permute-start | bytes 1769480 | tf_op jit(solution)/shard_map/ppermute | solution.py:43
  9.3 17.4 %collective-permute-start.2 = (bf16[256,1152]{1,0:T(8,128)(2,1)}, bf16[256,1152]{1,0:T(8,128)(2,1)S(1)}, u32[]{:S(2)}, u32[]{:S(2)}) collective-permute-start(bf16[256,1152]{1,0:T(8,128)(2,1)} %get-tuple-element.64), channel_id=1, source_target_pairs={{0,2},{1,3},{2,0},{3,1},{4,6},{5,7},{6,4},{7,5},{8,10},{9,11},{10,... | collective-permute-start | bytes 1769480 | tf_op jit(solution)/shard_map/ppermute | solution.py:43
  12.3 4.4 %copy-start.1 = (bf16[528,1152]{1,0:T(8,128)(2,1)S(1)}, bf16[528,1152]{1,0:T(8,128)(2,1)}, u32[]{:S(2)}) copy-start(bf16[528,1152]{1,0:T(8,128)(2,1)} %copy-done) | copy-start | bytes 3649540
  15.7 1.0 copy-start.4
  16.7 1.3 %copy-start.5 = (bf16[528,1152]{1,0:T(8,128)(2,1)S(1)}, bf16[528,1152]{1,0:T(8,128)(2,1)}, u32[]{:S(2)}) copy-start(bf16[528,1152]{1,0:T(8,128)(2,1)} %copy-done.4) | copy-start | bytes 3649540
  18.0 1.3 %copy-start.9 = (bf16[512,1152]{1,0:T(8,128)(2,1)S(1)}, bf16[512,1152]{1,0:T(8,128)(2,1)}, u32[]{:S(2)}) copy-start(bf16[512,1152]{1,0:T(8,128)(2,1)} %refs_2_.3) | copy-start | bytes 3538948
  25.3 1.4 %copy-start.11 = (f32[512,1152]{1,0:T(8,128)}, f32[512,1152]{1,0:T(8,128)S(1)}, u32[]{:S(2)}) copy-start(f32[512,1152]{1,0:T(8,128)S(1)} %get-tuple-element.61.one) | copy-start | bytes 7077892
  26.7 16.5 %collective-permute-start.4 = (bf16[272,1152]{1,0:T(8,128)(2,1)}, bf16[272,1152]{1,0:T(8,128)(2,1)}, u32[]{:S(2)}, u32[]{:S(2)}) collective-permute-start(bf16[272,1152]{1,0:T(8,128)(2,1)} %fusion), channel_id=1, source_target_pairs={{0,124},{1,125},{2,126},{3,127},{4,0},{5,1},{6,2},{7,3},{8,4},{9,5... | collective-permute-start | bytes 1880072 | tf_op jit(solution)/shard_map/ppermute | solution.py:43
  30.1 10.1 %collective-permute-start.3 = (bf16[256,1152]{1,0:T(8,128)(2,1)}, bf16[256,1152]{1,0:T(8,128)(2,1)}, u32[]{:S(2)}, u32[]{:S(2)}) collective-permute-start(bf16[256,1152]{1,0:T(8,128)(2,1)} %collective-permute-done.1.first), channel_id=1, source_target_pairs={{12,124},{13,125},{14,126},{15,127},{28,12},{29,13},{30,14},{31,15... | collective-permute-start | bytes 1769480 | tf_op jit(solution)/shard_map/ppermute | solution.py:43
  31.6 1.3 %copy-start.2 = (bf16[528,1152]{1,0:T(8,128)(2,1)S(1)}, bf16[528,1152]{1,0:T(8,128)(2,1)}, u32[]{:S(2)}) copy-start(bf16[528,1152]{1,0:T(8,128)(2,1)} %copy-done) | copy-start | bytes 3649540
  32.9 1.3 %copy-start.6 = (bf16[528,1152]{1,0:T(8,128)(2,1)S(1)}, bf16[528,1152]{1,0:T(8,128)(2,1)}, u32[]{:S(2)}) copy-start(bf16[528,1152]{1,0:T(8,128)(2,1)} %copy-done.4) | copy-start | bytes 3649540
  43.2 1.8 %copy-start.22 = (bf16[256,1152]{1,0:T(8,128)(2,1)S(1)}, bf16[256,1152]{1,0:T(8,128)(2,1)}, u32[]{:S(2)}) copy-start(bf16[256,1152]{1,0:T(8,128)(2,1)} %get-tuple-element.40) | copy-start | bytes 1769476
  43.2 4.8 %copy-start.10 = (bf16[512,1152]{1,0:T(8,128)(2,1)S(1)}, bf16[512,1152]{1,0:T(8,128)(2,1)}, u32[]{:S(2)}) copy-start(bf16[512,1152]{1,0:T(8,128)(2,1)} %refs_2_.3) | copy-start | bytes 3538948
  44.9 3.1 %collective-permute-start.5 = (bf16[528,1152]{1,0:T(8,128)(2,1)S(1)}, bf16[528,1152]{1,0:T(8,128)(2,1)S(1)}, u32[]{:S(2)}, u32[]{:S(2)}) collective-permute-start(bf16[528,1152]{1,0:T(8,128)(2,1)S(1)} %shard_map.78.refs_0_.refs_2_), channel_id=1, source_target_pairs={{0,1},{1,0},{2,3},{3,2},{4,5},{5,4},{6,7},{7,6},{8,9},{9,8},{10,11... | collective-permute-start | bytes 3649544 | tf_op jit(solution)/shard_map/ppermute | solution.py:43
  45.0 17.5 %collective-permute-start.6 = (bf16[256,1152]{1,0:T(8,128)(2,1)S(1)}, bf16[256,1152]{1,0:T(8,128)(2,1)S(1)}, u32[]{:S(2)}, u32[]{:S(2)}) collective-permute-start(bf16[256,1152]{1,0:T(8,128)(2,1)S(1)} %copy-done.22), channel_id=1, source_target_pairs={{0,2},{1,3},{2,0},{3,1},{4,6},{5,7},{6,4},{7,5},{8,10},{9,11},{10,... | collective-permute-start | bytes 1769480 | tf_op jit(solution)/shard_map/ppermute | solution.py:43
  53.8 3.6 %copy-start.15 = (f32[512,1152]{1,0:T(8,128)}, f32[512,1152]{1,0:T(8,128)S(1)}, u32[]{:S(2)}) copy-start(f32[512,1152]{1,0:T(8,128)S(1)} %get-tuple-element.62.two) | copy-start | bytes 7077892
  53.8 8.6 %copy-start.3 = (bf16[528,1152]{1,0:T(8,128)(2,1)S(1)}, bf16[528,1152]{1,0:T(8,128)(2,1)}, u32[]{:S(2)}) copy-start(bf16[528,1152]{1,0:T(8,128)(2,1)} %copy-done) | copy-start | bytes 3649540
  53.8 8.6 %copy-start.7 = (bf16[528,1152]{1,0:T(8,128)(2,1)S(1)}, bf16[528,1152]{1,0:T(8,128)(2,1)}, u32[]{:S(2)}) copy-start(bf16[528,1152]{1,0:T(8,128)(2,1)} %copy-done.4) | copy-start | bytes 3649540
  57.5 17.4 %collective-permute-start.7 = (bf16[256,1152]{1,0:T(8,128)(2,1)S(1)}, bf16[256,1152]{1,0:T(8,128)(2,1)S(1)}, u32[]{:S(2)}, u32[]{:S(2)}) collective-permute-start(bf16[256,1152]{1,0:T(8,128)(2,1)S(1)} %get-tuple-element.51), channel_id=1, source_target_pairs={{0,2},{1,3},{2,0},{3,1},{4,6},{5,7},{6,4},{7,5},{8,10},{9,11},{10,... | collective-permute-start | bytes 1769480 | tf_op jit(solution)/shard_map/ppermute | solution.py:43
  74.9 3.9 %copy-start.17 = (bf16[256,1152]{1,0:T(8,128)(2,1)}, bf16[256,1152]{1,0:T(8,128)(2,1)S(1)}, u32[]{:S(2)}) copy-start(bf16[256,1152]{1,0:T(8,128)(2,1)S(1)} %collective-permute-done.7.back1) | copy-start | bytes 1769476
  74.9 2.9 %collective-permute-start.8 = (bf16[528,1152]{1,0:T(8,128)(2,1)S(1)}, bf16[528,1152]{1,0:T(8,128)(2,1)S(1)}, u32[]{:S(2)}, u32[]{:S(2)}) collective-permute-start(bf16[528,1152]{1,0:T(8,128)(2,1)S(1)} %get-tuple-element.52), channel_id=1, source_target_pairs={{0,1},{1,0},{2,3},{3,2},{4,5},{5,4},{6,7},{7,6},{8,9},{9,8},{10,11... | collective-permute-start | bytes 3649544 | tf_op jit(solution)/shard_map/ppermute | solution.py:43
  78.8 31.6 %collective-permute-start.9 = (f32[520,1152]{1,0:T(8,128)}, f32[520,1152]{1,0:T(8,128)}, u32[]{:S(2)}, u32[]{:S(2)}) collective-permute-start(f32[520,1152]{1,0:T(8,128)} %get-tuple-element.54), channel_id=1, source_target_pairs={{0,1},{1,0},{2,3},{3,2},{4,5},{5,4},{6,7},{7,6},{8,9},{9,8},{10,11... | collective-permute-start | bytes 7188488 | tf_op jit(solution)/shard_map/ppermute | solution.py:43
  78.9 17.1 %collective-permute-start.11 = (bf16[256,1152]{1,0:T(8,128)(2,1)S(1)}, bf16[256,1152]{1,0:T(8,128)(2,1)S(1)}, u32[]{:S(2)}, u32[]{:S(2)}) collective-permute-start(bf16[256,1152]{1,0:T(8,128)(2,1)S(1)} %get-tuple-element.55), channel_id=1, source_target_pairs={{0,2},{1,3},{2,0},{3,1},{4,6},{5,7},{6,4},{7,5},{8,10},{9,11},{10,... | collective-permute-start | bytes 1769480 | tf_op jit(solution)/shard_map/ppermute | solution.py:43
  81.7 16.6 %collective-permute-start.10 = (bf16[256,1152]{1,0:T(8,128)(2,1)S(1)}, bf16[256,1152]{1,0:T(8,128)(2,1)}, u32[]{:S(2)}, u32[]{:S(2)}) collective-permute-start(bf16[256,1152]{1,0:T(8,128)(2,1)S(1)} %get-tuple-element.53), channel_id=1, source_target_pairs={{0,4},{1,5},{2,6},{3,7},{4,8},{5,9},{6,10},{7,11},{8,12},{9,13},{1... | collective-permute-start | bytes 1769480 | tf_op jit(solution)/shard_map/ppermute | solution.py:43
  96.1 0.8 copy-start.19
  98.3 19.7 %collective-permute-start.13 = (bf16[272,1152]{1,0:T(8,128)(2,1)}, bf16[272,1152]{1,0:T(8,128)(2,1)S(1)}, u32[]{:S(2)}, u32[]{:S(2)}) collective-permute-start(bf16[272,1152]{1,0:T(8,128)(2,1)} %get-tuple-element.58), channel_id=1, source_target_pairs={{0,4},{1,5},{2,6},{3,7},{4,8},{5,9},{6,10},{7,11},{8,12},{9,13},{1... | collective-permute-start | bytes 1880072 | tf_op jit(solution)/shard_map/ppermute | solution.py:43
  98.3 19.0 %collective-permute-start.12 = (bf16[256,1152]{1,0:T(8,128)(2,1)}, bf16[256,1152]{1,0:T(8,128)(2,1)}, u32[]{:S(2)}, u32[]{:S(2)}) collective-permute-start(bf16[256,1152]{1,0:T(8,128)(2,1)} %collective-permute-done.10.first), channel_id=1, source_target_pairs={{0,16},{1,17},{2,18},{3,19},{16,32},{17,33},{18,34},{19,35},{32,48... | collective-permute-start | bytes 1769480 | tf_op jit(solution)/shard_map/ppermute | solution.py:43
  100.2 1.7 %copy-start.12 = (f32[512,1152]{1,0:T(8,128)S(1)}, f32[512,1152]{1,0:T(8,128)}, u32[]{:S(2)}) copy-start(f32[512,1152]{1,0:T(8,128)} %copy-done.11) | copy-start | bytes 7077892
  101.9 1.7 %copy-start.16 = (f32[512,1152]{1,0:T(8,128)S(1)}, f32[512,1152]{1,0:T(8,128)}, u32[]{:S(2)}) copy-start(f32[512,1152]{1,0:T(8,128)} %copy-done.15) | copy-start | bytes 7077892
  104.0 1.4 %copy-start.13 = (f32[512,1152]{1,0:T(8,128)}, f32[512,1152]{1,0:T(8,128)S(1)}, u32[]{:S(2)}) copy-start(f32[512,1152]{1,0:T(8,128)S(1)} %shard_map.85.mine) | copy-start | bytes 7077892
  105.4 1.7 %copy-start.14 = (f32[512,1152]{1,0:T(8,128)S(1)}, f32[512,1152]{1,0:T(8,128)}, u32[]{:S(2)}) copy-start(f32[512,1152]{1,0:T(8,128)} %copy-done.13) | copy-start | bytes 7077892
  107.1 1.1 copy-start.18
  108.1 1.1 copy-start.20

commit v4 on v3

--- a/solution.py
+++ b/solution.py
@@ -51,7 +51,7 @@
     logit = temper * dots + shift
     z = jnp.where(positive, -logit, logit)
     e = jnp.exp(-jnp.abs(z))
-    log_term = jnp.where(e < 1e-4, e, jnp.log(1.0 + e))
+    log_term = jnp.where(e < 1e-4, (1.0 - 0.5 * e) * e, jnp.log(1.0 + e))
     loss = jnp.maximum(z, 0.0) + log_term
     sigmoid = jnp.exp(jnp.minimum(z, 0.0) - log_term)
     coef = (jnp.where(positive, -temper, temper) * sigmoid).astype(BF16)

time: 121 us -> 121 us (level)
  transfers between devices with their start and end apart: 14 -> 14, of which waited for: 8 -> 9; matrix products, arithmetic and copies ran while one was open for 3% -> 3% of each run, Pallas kernels for 27% -> 28%
where the time goes in v4:
time: 121 us; the launch traced here: 120 us
  Pallas kernels  38.8 us (32%)
  waiting for transfers between devices  33.8 us (28%)
  starting transfers between devices  22.4 us (19%)
  local copies, waits for them, and re-layouts  19.1 us (16%)
  other arithmetic  4.21 us (3%)
  between operations  2.22 us (2%)
    pallas_call x11, Pallas kernels, call(): pl.pallas_call(kernel, in_specs=[SMEM] * len(smalls) + [VMEM] * len(array...  38.8 us
    ppermute x14, waiting for transfers between devices, send(): return lax.ppermute(block, AXES, route)  33.8 us
    ppermute x14, starting transfers between devices, send(): return lax.ppermute(block, AXES, route)  22.4 us
    unnamed x46, local copies, waits for them, and re-layouts  16.9 us
    concatenate x2, other arithmetic, body(): jnp.concatenate([images, jnp.pad(code, ((0, CARRY - 2), (0, WIDTH - ROWS)...  3.4 us
  transfers between devices with their start and end apart: 14, of which 9 were waited for; matrix products, arithmetic and copies ran while one was open for 3% of the time, Pallas kernels for 28%

profile of v4, /device:TPU:0, one launch (start us, length us, event | category | flops | bytes accessed | tf_op | source)
XLA Modules:
  0.0 120.5 jit_solution(8038643845994809356)
XLA Ops:
  0.6 0.8 fusion.7
  1.5 1.5 %pad_maximum_fusion.refs_0_ = bf16[528,1152]{1,0:T(8,128)(2,1)S(1)} fusion(bf16[16,1152]{1,0:T(8,128)(2,1)S(1)} %fusion.6, bf16[512,1152]{1,0:T(8,128)(2,1)} %param.5), kind=kLoop, calls=%fused_computation.1 | loop fusion | flops 2433024 | bytes 2433024 | tf_op jit(solution)/shard_map/concatenate | solution.py:202
  3.0 0.1 collective-permute-start
  3.1 1.0 slice.12
  4.1 4.1 %collective-permute-start.1 = (bf16[256,1152]{1,0:T(8,128)(2,1)}, bf16[256,1152]{1,0:T(8,128)(2,1)}, u32[]{:S(2)}, u32[]{:S(2)}) collective-permute-start(bf16[256,1152]{1,0:T(8,128)(2,1)} %slice.12), channel_id=1, source_target_pairs={{0,12},{1,13},{2,14},{3,15},{4,0},{5,1},{6,2},{7,3},{8,4},{9,5},{1... | collective-permute-start | bytes 1769480 | tf_op jit(solution)/shard_map/ppermute | solution.py:43
  8.2 1.1 fusion.10
  9.3 3.0 %collective-permute-start.2 = (bf16[256,1152]{1,0:T(8,128)(2,1)}, bf16[256,1152]{1,0:T(8,128)(2,1)S(1)}, u32[]{:S(2)}, u32[]{:S(2)}) collective-permute-start(bf16[256,1152]{1,0:T(8,128)(2,1)} %get-tuple-element.64), channel_id=1, source_target_pairs={{0,2},{1,3},{2,0},{3,1},{4,6},{5,7},{6,4},{7,5},{8,10},{9,11},{10,... | collective-permute-start | bytes 1769480 | tf_op jit(solution)/shard_map/ppermute | solution.py:43
  13.7 1.9 %fusion = bf16[272,1152]{1,0:T(8,128)(2,1)} fusion(bf16[512,1152]{1,0:T(8,128)(2,1)} %param.5, bf16[16,1152]{1,0:T(8,128)(2,1)S(1)} %fusion.6), kind=kLoop, calls=%fused_computation.3 | loop fusion | flops 1253376 | bytes 1843200 | tf_op jit(solution)/shard_map/concatenate | solution.py:202
  15.7 1.0 copy-done.4
  16.7 1.3 %copy-done.5 = bf16[528,1152]{1,0:T(8,128)(2,1)S(1)} copy-done((bf16[528,1152]{1,0:T(8,128)(2,1)S(1)}, bf16[528,1152]{1,0:T(8,128)(2,1)}, u32[]{:S(2)}) %copy-start.5) | copy-done | bytes 1216536
  18.0 1.3 %copy-done.9 = bf16[512,1152]{1,0:T(8,128)(2,1)S(1)} copy-done((bf16[512,1152]{1,0:T(8,128)(2,1)S(1)}, bf16[512,1152]{1,0:T(8,128)(2,1)}, u32[]{:S(2)}) %copy-start.9) | copy-done | bytes 1179672
  19.3 6.2 %shard_map.76 = (f32[520,1152]{1,0:T(8,128)S(1)}, f32[520,1152]{1,0:T(8,128)}, f32[512,1152]{1,0:T(8,128)S(1)}) custom-call(f32[1]{0:T(128)} %bitcast.3.start_ref, f32[1]{0:T(128)S(6)} %copy.26.scale_ref, f32[1]{0:T(128)S(6)} %copy.27.offset_ref, bf16[528,1152]{1,0:T(8,128)(2,1)S(1)} %copy-done.1, bf16[528,1152]{1,0:T(8,128)(2,1)S(1)} %copy-done.5, ...), custom_call_target="tpu_custom_call" | custom-call | flops 1000 | bytes 1000 | tf_op jit(solution)/shard_map/pallas_call | solution.py:73
  25.4 1.4 %copy-done.11 = f32[512,1152]{1,0:T(8,128)} copy-done((f32[512,1152]{1,0:T(8,128)}, f32[512,1152]{1,0:T(8,128)S(1)}, u32[]{:S(2)}) %copy-start.11) | copy-done | bytes 2359320
  26.9 3.3 %collective-permute-start.4 = (bf16[272,1152]{1,0:T(8,128)(2,1)}, bf16[272,1152]{1,0:T(8,128)(2,1)}, u32[]{:S(2)}, u32[]{:S(2)}) collective-permute-start(bf16[272,1152]{1,0:T(8,128)(2,1)} %fusion), channel_id=1, source_target_pairs={{0,124},{1,125},{2,126},{3,127},{4,0},{5,1},{6,2},{7,3},{8,4},{9,5... | collective-permute-start | bytes 1880072 | tf_op jit(solution)/shard_map/ppermute | solution.py:43
  30.1 1.5 %collective-permute-start.3 = (bf16[256,1152]{1,0:T(8,128)(2,1)}, bf16[256,1152]{1,0:T(8,128)(2,1)}, u32[]{:S(2)}, u32[]{:S(2)}) collective-permute-start(bf16[256,1152]{1,0:T(8,128)(2,1)} %collective-permute-done.1.first), channel_id=1, source_target_pairs={{12,124},{13,125},{14,126},{15,127},{28,12},{29,13},{30,14},{31,15... | collective-permute-start | bytes 1769480 | tf_op jit(solution)/shard_map/ppermute | solution.py:43
  31.6 1.3 %copy-done.2 = bf16[528,1152]{1,0:T(8,128)(2,1)S(1)} copy-done((bf16[528,1152]{1,0:T(8,128)(2,1)S(1)}, bf16[528,1152]{1,0:T(8,128)(2,1)}, u32[]{:S(2)}) %copy-start.2) | copy-done | bytes 1216536
  32.9 1.3 %copy-done.6 = bf16[528,1152]{1,0:T(8,128)(2,1)S(1)} copy-done((bf16[528,1152]{1,0:T(8,128)(2,1)S(1)}, bf16[528,1152]{1,0:T(8,128)(2,1)}, u32[]{:S(2)}) %copy-start.6) | copy-done | bytes 1216536
  34.2 6.1 %shard_map.77 = (f32[520,1152]{1,0:T(8,128)S(1)}, f32[520,1152]{1,0:T(8,128)}, f32[256,1152]{1,0:T(8,128)S(1)}) custom-call(f32[1]{0:T(128)} %bitcast.1.start_ref, f32[1]{0:T(128)S(6)} %copy.26.scale_ref, f32[1]{0:T(128)S(6)} %copy.27.offset_ref, bf16[528,1152]{1,0:T(8,128)(2,1)S(1)} %copy-done.2, ...), custom_call_target="tpu_custom_call", output_to_operand_aliasing={{0}: (6, {}), {1}: (7, {})} | custom-call | flops 1000 | bytes 1000 | tf_op jit(solution)/shard_map/pallas_call | solution.py:73
  40.3 3.0 %collective-permute-done.4.rest = bf16[272,1152]{1,0:T(8,128)(2,1)} collective-permute-done((bf16[272,1152]{1,0:T(8,128)(2,1)}, bf16[272,1152]{1,0:T(8,128)(2,1)}, u32[]{:S(2)}, u32[]{:S(2)}) %collective-permute-start.4) | collective-permute-done | bytes 626720 | tf_op jit(solution)/shard_map/ppermute | solution.py:43
  43.4 1.7 %shard_map.78.refs_0_.refs_2_ = bf16[528,1152]{1,0:T(8,128)(2,1)S(1)} custom-call(s32[1]{0:T(128)} %bitcast.2.flag_ref, bf16[256,1152]{1,0:T(8,128)(2,1)} %collective-permute-done.1.first, bf16[256,1152]{1,0:T(8,128)(2,1)} %collective-permute-done.3.turned, bf16[272,1152]{1,0:T(8,128)(2,1)} %collective-permute-done.4.rest), custom_call_target="tpu_custom_call" | custom-call | flops 1000 | bytes 1000 | tf_op jit(solution)/shard_map/pallas_call | solution.py:73
  45.1 0.1 collective-permute-start.5
  45.2 2.8 %collective-permute-start.6 = (bf16[256,1152]{1,0:T(8,128)(2,1)S(1)}, bf16[256,1152]{1,0:T(8,128)(2,1)S(1)}, u32[]{:S(2)}, u32[]{:S(2)}) collective-permute-start(bf16[256,1152]{1,0:T(8,128)(2,1)S(1)} %copy-done.22), channel_id=1, source_target_pairs={{0,2},{1,3},{2,0},{3,1},{4,6},{5,7},{6,4},{7,5},{8,10},{9,11},{10,... | collective-permute-start | bytes 1769480 | tf_op jit(solution)/shard_map/ppermute | solution.py:43
  48.0 6.0 %shard_map.79 = (f32[520,1152]{1,0:T(8,128)S(1)}, f32[520,1152]{1,0:T(8,128)S(1)}, f32[512,1152]{1,0:T(8,128)S(1)}) custom-call(f32[1]{0:T(128)} %bitcast.3.start_ref, f32[1]{0:T(128)S(6)} %copy.26.scale_ref, f32[1]{0:T(128)S(6)} %copy.27.offset_ref, bf16[528,1152]{1,0:T(8,128)(2,1)S(1)} %shard_map.78.refs_0_.refs_2_, ...), custom_call_target="tpu_custom_call" | custom-call | flops 1000 | bytes 1000 | tf_op jit(solution)/shard_map/pallas_call | solution.py:73
  54.1 3.7 %shard_map.80 = (f32[520,1152]{1,0:T(8,128)S(1)}, f32[520,1152]{1,0:T(8,128)S(1)}, bf16[256,1152]{1,0:T(8,128)(2,1)S(1)}) custom-call(f32[1]{0:T(128)} %bitcast.1.start_ref, f32[1]{0:T(128)S(6)} %copy.26.scale_ref, f32[1]{0:T(128)S(6)} %copy.27.offset_ref, ...), custom_call_target="tpu_custom_call", output_to_operand_aliasing={{0}: (6, {}), {1}: (7, {})} | custom-call | flops 1000 | bytes 1000 | tf_op jit(solution)/shard_map/pallas_call | solution.py:73
  57.9 2.8 %collective-permute-start.7 = (bf16[256,1152]{1,0:T(8,128)(2,1)S(1)}, bf16[256,1152]{1,0:T(8,128)(2,1)S(1)}, u32[]{:S(2)}, u32[]{:S(2)}) collective-permute-start(bf16[256,1152]{1,0:T(8,128)(2,1)S(1)} %get-tuple-element.51), channel_id=1, source_target_pairs={{0,2},{1,3},{2,0},{3,1},{4,6},{5,7},{6,4},{7,5},{8,10},{9,11},{10,... | collective-permute-start | bytes 1769480 | tf_op jit(solution)/shard_map/ppermute | solution.py:43
  60.7 1.7 %collective-permute-done.6.refs_4_ = bf16[256,1152]{1,0:T(8,128)(2,1)S(1)} collective-permute-done((bf16[256,1152]{1,0:T(8,128)(2,1)S(1)}, bf16[256,1152]{1,0:T(8,128)(2,1)S(1)}, u32[]{:S(2)}, u32[]{:S(2)}) %collective-permute-start.6) | collective-permute-done | bytes 589856 | tf_op jit(solution)/shard_map/ppermute | solution.py:43
  62.4 7.8 %shard_map.81 = (f32[520,1152]{1,0:T(8,128)S(1)}, f32[520,1152]{1,0:T(8,128)}, f32[520,1152]{1,0:T(8,128)S(1)}, bf16[528,1152]{1,0:T(8,128)(2,1)S(1)}, bf16[256,1152]{1,0:T(8,128)(2,1)S(1)}) custom-call(f32[1]{0:T(128)S(6)} %add.25.start_ref, f32[1]{0:T(128)S(6)} %copy.26.scale_ref, ...), custom_call_target="tpu_custom_call", output_to_operand_aliasing={{0}: (8, {}), {1}: (9, {}), {2}: (10, {})} | custom-call | flops 1000 | bytes 1000 | tf_op jit(solution)/shard_map/pallas_call | solution.py:73
  70.2 4.8 %collective-permute-done.7.back1 = bf16[256,1152]{1,0:T(8,128)(2,1)S(1)} collective-permute-done((bf16[256,1152]{1,0:T(8,128)(2,1)S(1)}, bf16[256,1152]{1,0:T(8,128)(2,1)S(1)}, u32[]{:S(2)}, u32[]{:S(2)}) %collective-permute-start.7) | collective-permute-done | bytes 589856 | tf_op jit(solution)/shard_map/ppermute | solution.py:43
  75.0 2.9 %collective-permute-done.8.other = bf16[528,1152]{1,0:T(8,128)(2,1)S(1)} collective-permute-done((bf16[528,1152]{1,0:T(8,128)(2,1)S(1)}, bf16[528,1152]{1,0:T(8,128)(2,1)S(1)}, u32[]{:S(2)}, u32[]{:S(2)}) %collective-permute-start.8) | collective-permute-done | bytes 1216544 | tf_op jit(solution)/shard_map/ppermute | solution.py:43
  77.9 1.0 shard_map.82
  79.0 0.1 collective-permute-start.9
  79.1 2.5 %collective-permute-start.11 = (bf16[256,1152]{1,0:T(8,128)(2,1)S(1)}, bf16[256,1152]{1,0:T(8,128)(2,1)S(1)}, u32[]{:S(2)}, u32[]{:S(2)}) collective-permute-start(bf16[256,1152]{1,0:T(8,128)(2,1)S(1)} %get-tuple-element.55), channel_id=1, source_target_pairs={{0,2},{1,3},{2,0},{3,1},{4,6},{5,7},{6,4},{7,5},{8,10},{9,11},{10,... | collective-permute-start | bytes 1769480 | tf_op jit(solution)/shard_map/ppermute | solution.py:43
  81.7 14.6 %collective-permute-done.11.back2 = bf16[256,1152]{1,0:T(8,128)(2,1)S(1)} collective-permute-done((bf16[256,1152]{1,0:T(8,128)(2,1)S(1)}, bf16[256,1152]{1,0:T(8,128)(2,1)S(1)}, u32[]{:S(2)}, u32[]{:S(2)}) %collective-permute-start.11) | collective-permute-done | bytes 589856 | tf_op jit(solution)/shard_map/ppermute | solution.py:43
  96.2 0.8 copy-done.19
  97.0 1.3 %collective-permute-done.10.first = bf16[256,1152]{1,0:T(8,128)(2,1)} collective-permute-done((bf16[256,1152]{1,0:T(8,128)(2,1)S(1)}, bf16[256,1152]{1,0:T(8,128)(2,1)}, u32[]{:S(2)}, u32[]{:S(2)}) %collective-permute-start.10) | collective-permute-done | bytes 589856 | tf_op jit(solution)/shard_map/ppermute | solution.py:43
  98.3 1.9 %collective-permute-start.12 = (bf16[256,1152]{1,0:T(8,128)(2,1)}, bf16[256,1152]{1,0:T(8,128)(2,1)}, u32[]{:S(2)}, u32[]{:S(2)}) collective-permute-start(bf16[256,1152]{1,0:T(8,128)(2,1)} %collective-permute-done.10.first), channel_id=1, source_target_pairs={{0,16},{1,17},{2,18},{3,19},{16,32},{17,33},{18,34},{19,35},{32,48... | collective-permute-start | bytes 1769480 | tf_op jit(solution)/shard_map/ppermute | solution.py:43
  100.3 1.7 %copy-done.12 = f32[512,1152]{1,0:T(8,128)S(1)} copy-done((f32[512,1152]{1,0:T(8,128)S(1)}, f32[512,1152]{1,0:T(8,128)}, u32[]{:S(2)}) %copy-start.12) | copy-done | bytes 2359320
  101.9 1.7 %copy-done.16 = f32[512,1152]{1,0:T(8,128)S(1)} copy-done((f32[512,1152]{1,0:T(8,128)S(1)}, f32[512,1152]{1,0:T(8,128)}, u32[]{:S(2)}) %copy-start.16) | copy-done | bytes 2359320
  103.6 0.4 shard_map.85.mine
  104.0 1.4 %copy-done.13 = f32[512,1152]{1,0:T(8,128)} copy-done((f32[512,1152]{1,0:T(8,128)}, f32[512,1152]{1,0:T(8,128)S(1)}, u32[]{:S(2)}) %copy-start.13) | copy-done | bytes 2359320
  105.4 1.7 %copy-done.14 = f32[512,1152]{1,0:T(8,128)S(1)} copy-done((f32[512,1152]{1,0:T(8,128)S(1)}, f32[512,1152]{1,0:T(8,128)}, u32[]{:S(2)}) %copy-start.14) | copy-done | bytes 2359320
  107.1 1.1 copy-done.18
  108.1 1.1 copy-done.20
  109.2 1.2 %shard_map.86 = bf16[512,1152]{1,0:T(8,128)(2,1)} custom-call(f32[512,1152]{1,0:T(8,128)S(1)} %copy-done.14, bf16[256,1152]{1,0:T(8,128)(2,1)S(1)} %copy-done.18, bf16[256,1152]{1,0:T(8,128)(2,1)S(1)} %copy-done.20), custom_call_target="tpu_custom_call" | custom-call | flops 1000 | bytes 1000 | tf_op jit(solution)/shard_map/pallas_call | solution.py:73
  110.4 2.1 %shard_map.83.mine = f32[520,1152]{1,0:T(8,128)S(1)} custom-call(f32[520,1152]{1,0:T(8,128)S(1)} %get-tuple-element.47.one, f32[520,1152]{1,0:T(8,128)} %collective-permute-done.9.two), custom_call_target="tpu_custom_call", output_to_operand_aliasing={{}: (0, {})} | custom-call | flops 1000 | bytes 1000 | tf_op jit(solution)/shard_map/pallas_call | solution.py:73
  112.5 4.8 %collective-permute-done.12.turned = bf16[256,1152]{1,0:T(8,128)(2,1)} collective-permute-done((bf16[256,1152]{1,0:T(8,128)(2,1)}, bf16[256,1152]{1,0:T(8,128)(2,1)}, u32[]{:S(2)}, u32[]{:S(2)}) %collective-permute-start.12) | collective-permute-done | bytes 589856 | tf_op jit(solution)/shard_map/ppermute | solution.py:43
  117.3 0.7 collective-permute-done.13.rest
  118.0 2.5 %shard_map.84 = (bf16[512,1152]{1,0:T(8,128)(2,1)}, f32[1,512]{1,0:T(1,128)}) custom-call(s32[1]{0:T(128)} %bitcast.flag_ref, f32[520,1152]{1,0:T(8,128)S(1)} %shard_map.83.mine, bf16[256,1152]{1,0:T(8,128)(2,1)} %collective-permute-done.10.first, bf16[256,1152]{1,0:T(8,128)(2,1)} %collective-permute-done.12.turned, ...), custom_call_target="tpu_custom_call" | custom-call | flops 1000 | bytes 1000 | tf_op jit(solution)/shard_map/pallas_call | solution.py:73
  (45 shorter events, 0.2 us)
Async XLA Ops:
  0.6 2.4 %copy-start.21 = (bf16[512,1152]{1,0:T(8,128)(2,1)S(1)}, bf16[512,1152]{1,0:T(8,128)(2,1)}, u32[]{:S(2)}) copy-start(bf16[512,1152]{1,0:T(8,128)(2,1)} %param.5) | copy-start | bytes 3538948
  1.5 6.7 %copy-start.8 = (bf16[512,1152]{1,0:T(8,128)(2,1)S(1)}, bf16[512,1152]{1,0:T(8,128)(2,1)}, u32[]{:S(2)}) copy-start(bf16[512,1152]{1,0:T(8,128)(2,1)} %refs_2_.3) | copy-start | bytes 3538948
  2.9 6.4 %copy-start = (bf16[528,1152]{1,0:T(8,128)(2,1)}, bf16[528,1152]{1,0:T(8,128)(2,1)S(1)}, u32[]{:S(2)}) copy-start(bf16[528,1152]{1,0:T(8,128)(2,1)S(1)} %pad_maximum_fusion.refs_0_) | copy-start | bytes 3649540
  3.0 12.7 %collective-permute-start = (bf16[528,1152]{1,0:T(8,128)(2,1)S(1)}, bf16[528,1152]{1,0:T(8,128)(2,1)S(1)}, u32[]{:S(2)}, u32[]{:S(2)}) collective-permute-start(bf16[528,1152]{1,0:T(8,128)(2,1)S(1)} %pad_maximum_fusion.refs_0_), channel_id=1, source_target_pairs={{0,1},{1,0},{2,3},{3,2},{4,5},{5,4},{6,7},{7,6},{8,9},{9,8},{10,11... | collective-permute-start | bytes 3649544 | tf_op jit(solution)/shard_map/ppermute | solution.py:43
  4.1 22.8 %collective-permute-start.1 = (bf16[256,1152]{1,0:T(8,128)(2,1)}, bf16[256,1152]{1,0:T(8,128)(2,1)}, u32[]{:S(2)}, u32[]{:S(2)}) collective-permute-start(bf16[256,1152]{1,0:T(8,128)(2,1)} %slice.12), channel_id=1, source_target_pairs={{0,12},{1,13},{2,14},{3,15},{4,0},{5,1},{6,2},{7,3},{8,4},{9,5},{1... | collective-permute-start | bytes 1769480 | tf_op jit(solution)/shard_map/ppermute | solution.py:43
  9.3 17.5 %collective-permute-start.2 = (bf16[256,1152]{1,0:T(8,128)(2,1)}, bf16[256,1152]{1,0:T(8,128)(2,1)S(1)}, u32[]{:S(2)}, u32[]{:S(2)}) collective-permute-start(bf16[256,1152]{1,0:T(8,128)(2,1)} %get-tuple-element.64), channel_id=1, source_target_pairs={{0,2},{1,3},{2,0},{3,1},{4,6},{5,7},{6,4},{7,5},{8,10},{9,11},{10,... | collective-permute-start | bytes 1769480 | tf_op jit(solution)/shard_map/ppermute | solution.py:43
  12.3 4.4 %copy-start.1 = (bf16[528,1152]{1,0:T(8,128)(2,1)S(1)}, bf16[528,1152]{1,0:T(8,128)(2,1)}, u32[]{:S(2)}) copy-start(bf16[528,1152]{1,0:T(8,128)(2,1)} %copy-done) | copy-start | bytes 3649540
  15.7 1.0 copy-start.4
  16.7 1.3 %copy-start.5 = (bf16[528,1152]{1,0:T(8,128)(2,1)S(1)}, bf16[528,1152]{1,0:T(8,128)(2,1)}, u32[]{:S(2)}) copy-start(bf16[528,1152]{1,0:T(8,128)(2,1)} %copy-done.4) | copy-start | bytes 3649540
  18.0 1.3 %copy-start.9 = (bf16[512,1152]{1,0:T(8,128)(2,1)S(1)}, bf16[512,1152]{1,0:T(8,128)(2,1)}, u32[]{:S(2)}) copy-start(bf16[512,1152]{1,0:T(8,128)(2,1)} %refs_2_.3) | copy-start | bytes 3538948
  25.4 1.4 %copy-start.11 = (f32[512,1152]{1,0:T(8,128)}, f32[512,1152]{1,0:T(8,128)S(1)}, u32[]{:S(2)}) copy-start(f32[512,1152]{1,0:T(8,128)S(1)} %get-tuple-element.61.one) | copy-start | bytes 7077892
  26.9 16.5 %collective-permute-start.4 = (bf16[272,1152]{1,0:T(8,128)(2,1)}, bf16[272,1152]{1,0:T(8,128)(2,1)}, u32[]{:S(2)}, u32[]{:S(2)}) collective-permute-start(bf16[272,1152]{1,0:T(8,128)(2,1)} %fusion), channel_id=1, source_target_pairs={{0,124},{1,125},{2,126},{3,127},{4,0},{5,1},{6,2},{7,3},{8,4},{9,5... | collective-permute-start | bytes 1880072 | tf_op jit(solution)/shard_map/ppermute | solution.py:43
  30.1 10.2 %collective-permute-start.3 = (bf16[256,1152]{1,0:T(8,128)(2,1)}, bf16[256,1152]{1,0:T(8,128)(2,1)}, u32[]{:S(2)}, u32[]{:S(2)}) collective-permute-start(bf16[256,1152]{1,0:T(8,128)(2,1)} %collective-permute-done.1.first), channel_id=1, source_target_pairs={{12,124},{13,125},{14,126},{15,127},{28,12},{29,13},{30,14},{31,15... | collective-permute-start | bytes 1769480 | tf_op jit(solution)/shard_map/ppermute | solution.py:43
  31.6 1.3 %copy-start.2 = (bf16[528,1152]{1,0:T(8,128)(2,1)S(1)}, bf16[528,1152]{1,0:T(8,128)(2,1)}, u32[]{:S(2)}) copy-start(bf16[528,1152]{1,0:T(8,128)(2,1)} %copy-done) | copy-start | bytes 3649540
  32.9 1.3 %copy-start.6 = (bf16[528,1152]{1,0:T(8,128)(2,1)S(1)}, bf16[528,1152]{1,0:T(8,128)(2,1)}, u32[]{:S(2)}) copy-start(bf16[528,1152]{1,0:T(8,128)(2,1)} %copy-done.4) | copy-start | bytes 3649540
  43.4 1.8 %copy-start.22 = (bf16[256,1152]{1,0:T(8,128)(2,1)S(1)}, bf16[256,1152]{1,0:T(8,128)(2,1)}, u32[]{:S(2)}) copy-start(bf16[256,1152]{1,0:T(8,128)(2,1)} %get-tuple-element.40) | copy-start | bytes 1769476
  43.4 4.7 %copy-start.10 = (bf16[512,1152]{1,0:T(8,128)(2,1)S(1)}, bf16[512,1152]{1,0:T(8,128)(2,1)}, u32[]{:S(2)}) copy-start(bf16[512,1152]{1,0:T(8,128)(2,1)} %refs_2_.3) | copy-start | bytes 3538948
  45.1 3.0 %collective-permute-start.5 = (bf16[528,1152]{1,0:T(8,128)(2,1)S(1)}, bf16[528,1152]{1,0:T(8,128)(2,1)S(1)}, u32[]{:S(2)}, u32[]{:S(2)}) collective-permute-start(bf16[528,1152]{1,0:T(8,128)(2,1)S(1)} %shard_map.78.refs_0_.refs_2_), channel_id=1, source_target_pairs={{0,1},{1,0},{2,3},{3,2},{4,5},{5,4},{6,7},{7,6},{8,9},{9,8},{10,11... | collective-permute-start | bytes 3649544 | tf_op jit(solution)/shard_map/ppermute | solution.py:43
  45.2 17.2 %collective-permute-start.6 = (bf16[256,1152]{1,0:T(8,128)(2,1)S(1)}, bf16[256,1152]{1,0:T(8,128)(2,1)S(1)}, u32[]{:S(2)}, u32[]{:S(2)}) collective-permute-start(bf16[256,1152]{1,0:T(8,128)(2,1)S(1)} %copy-done.22), channel_id=1, source_target_pairs={{0,2},{1,3},{2,0},{3,1},{4,6},{5,7},{6,4},{7,5},{8,10},{9,11},{10,... | collective-permute-start | bytes 1769480 | tf_op jit(solution)/shard_map/ppermute | solution.py:43
  54.1 3.8 %copy-start.15 = (f32[512,1152]{1,0:T(8,128)}, f32[512,1152]{1,0:T(8,128)S(1)}, u32[]{:S(2)}) copy-start(f32[512,1152]{1,0:T(8,128)S(1)} %get-tuple-element.62.two) | copy-start | bytes 7077892
  54.1 8.3 %copy-start.3 = (bf16[528,1152]{1,0:T(8,128)(2,1)S(1)}, bf16[528,1152]{1,0:T(8,128)(2,1)}, u32[]{:S(2)}) copy-start(bf16[528,1152]{1,0:T(8,128)(2,1)} %copy-done) | copy-start | bytes 3649540
  54.1 8.3 %copy-start.7 = (bf16[528,1152]{1,0:T(8,128)(2,1)S(1)}, bf16[528,1152]{1,0:T(8,128)(2,1)}, u32[]{:S(2)}) copy-start(bf16[528,1152]{1,0:T(8,128)(2,1)} %copy-done.4) | copy-start | bytes 3649540
  57.9 17.2 %collective-permute-start.7 = (bf16[256,1152]{1,0:T(8,128)(2,1)S(1)}, bf16[256,1152]{1,0:T(8,128)(2,1)S(1)}, u32[]{:S(2)}, u32[]{:S(2)}) collective-permute-start(bf16[256,1152]{1,0:T(8,128)(2,1)S(1)} %get-tuple-element.51), channel_id=1, source_target_pairs={{0,2},{1,3},{2,0},{3,1},{4,6},{5,7},{6,4},{7,5},{8,10},{9,11},{10,... | collective-permute-start | bytes 1769480 | tf_op jit(solution)/shard_map/ppermute | solution.py:43
  75.0 3.9 %copy-start.17 = (bf16[256,1152]{1,0:T(8,128)(2,1)}, bf16[256,1152]{1,0:T(8,128)(2,1)S(1)}, u32[]{:S(2)}) copy-start(bf16[256,1152]{1,0:T(8,128)(2,1)S(1)} %collective-permute-done.7.back1) | copy-start | bytes 1769476
  75.0 2.9 %collective-permute-start.8 = (bf16[528,1152]{1,0:T(8,128)(2,1)S(1)}, bf16[528,1152]{1,0:T(8,128)(2,1)S(1)}, u32[]{:S(2)}, u32[]{:S(2)}) collective-permute-start(bf16[528,1152]{1,0:T(8,128)(2,1)S(1)} %get-tuple-element.52), channel_id=1, source_target_pairs={{0,1},{1,0},{2,3},{3,2},{4,5},{5,4},{6,7},{7,6},{8,9},{9,8},{10,11... | collective-permute-start | bytes 3649544 | tf_op jit(solution)/shard_map/ppermute | solution.py:43
  79.0 31.4 %collective-permute-start.9 = (f32[520,1152]{1,0:T(8,128)}, f32[520,1152]{1,0:T(8,128)}, u32[]{:S(2)}, u32[]{:S(2)}) collective-permute-start(f32[520,1152]{1,0:T(8,128)} %get-tuple-element.54), channel_id=1, source_target_pairs={{0,1},{1,0},{2,3},{3,2},{4,5},{5,4},{6,7},{7,6},{8,9},{9,8},{10,11... | collective-permute-start | bytes 7188488 | tf_op jit(solution)/shard_map/ppermute | solution.py:43
  79.1 17.1 %collective-permute-start.11 = (bf16[256,1152]{1,0:T(8,128)(2,1)S(1)}, bf16[256,1152]{1,0:T(8,128)(2,1)S(1)}, u32[]{:S(2)}, u32[]{:S(2)}) collective-permute-start(bf16[256,1152]{1,0:T(8,128)(2,1)S(1)} %get-tuple-element.55), channel_id=1, source_target_pairs={{0,2},{1,3},{2,0},{3,1},{4,6},{5,7},{6,4},{7,5},{8,10},{9,11},{10,... | collective-permute-start | bytes 1769480 | tf_op jit(solution)/shard_map/ppermute | solution.py:43
  81.7 16.6 %collective-permute-start.10 = (bf16[256,1152]{1,0:T(8,128)(2,1)S(1)}, bf16[256,1152]{1,0:T(8,128)(2,1)}, u32[]{:S(2)}, u32[]{:S(2)}) collective-permute-start(bf16[256,1152]{1,0:T(8,128)(2,1)S(1)} %get-tuple-element.53), channel_id=1, source_target_pairs={{0,4},{1,5},{2,6},{3,7},{4,8},{5,9},{6,10},{7,11},{8,12},{9,13},{1... | collective-permute-start | bytes 1769480 | tf_op jit(solution)/shard_map/ppermute | solution.py:43
  96.2 0.8 copy-start.19
  98.3 19.7 %collective-permute-start.13 = (bf16[272,1152]{1,0:T(8,128)(2,1)}, bf16[272,1152]{1,0:T(8,128)(2,1)S(1)}, u32[]{:S(2)}, u32[]{:S(2)}) collective-permute-start(bf16[272,1152]{1,0:T(8,128)(2,1)} %get-tuple-element.58), channel_id=1, source_target_pairs={{0,4},{1,5},{2,6},{3,7},{4,8},{5,9},{6,10},{7,11},{8,12},{9,13},{1... | collective-permute-start | bytes 1880072 | tf_op jit(solution)/shard_map/ppermute | solution.py:43
  98.3 19.0 %collective-permute-start.12 = (bf16[256,1152]{1,0:T(8,128)(2,1)}, bf16[256,1152]{1,0:T(8,128)(2,1)}, u32[]{:S(2)}, u32[]{:S(2)}) collective-permute-start(bf16[256,1152]{1,0:T(8,128)(2,1)} %collective-permute-done.10.first), channel_id=1, source_target_pairs={{0,16},{1,17},{2,18},{3,19},{16,32},{17,33},{18,34},{19,35},{32,48... | collective-permute-start | bytes 1769480 | tf_op jit(solution)/shard_map/ppermute | solution.py:43
  100.2 1.7 %copy-start.12 = (f32[512,1152]{1,0:T(8,128)S(1)}, f32[512,1152]{1,0:T(8,128)}, u32[]{:S(2)}) copy-start(f32[512,1152]{1,0:T(8,128)} %copy-done.11) | copy-start | bytes 7077892
  101.9 1.7 %copy-start.16 = (f32[512,1152]{1,0:T(8,128)S(1)}, f32[512,1152]{1,0:T(8,128)}, u32[]{:S(2)}) copy-start(f32[512,1152]{1,0:T(8,128)} %copy-done.15) | copy-start | bytes 7077892
  104.0 1.4 %copy-start.13 = (f32[512,1152]{1,0:T(8,128)}, f32[512,1152]{1,0:T(8,128)S(1)}, u32[]{:S(2)}) copy-start(f32[512,1152]{1,0:T(8,128)S(1)} %shard_map.85.mine) | copy-start | bytes 7077892
  105.4 1.7 %copy-start.14 = (f32[512,1152]{1,0:T(8,128)S(1)}, f32[512,1152]{1,0:T(8,128)}, u32[]{:S(2)}) copy-start(f32[512,1152]{1,0:T(8,128)} %copy-done.13) | copy-start | bytes 7077892
  107.1 1.1 copy-start.18
  108.1 1.1 copy-start.20

commit v5 on v4

--- a/solution.py
+++ b/solution.py
@@ -204,8 +204,8 @@
     first = send(images[:HALF], moved(z=-1))
     own2 = send(own, swap)
     (ga, ga2), gs = pairs([own, own2], texts, start, scale, offset)
-    rest = send(after(own[HALF:], first, gs, far1), along_loop(-1))
-    turned = send(after(first, gs, far1), last_hop(-1))
+    rest = send(after(own[HALF:], first, ga2, far1), along_loop(-1))
+    turned = send(after(first, ga2, far1), last_hop(-1))
     (ga, ga2), gu = pairs([own, own2], far1, far_start, scale, offset, [ga, ga2])
     far2 = send(after(texts[FIRST:], far1), across)
     visitor = call(

time: 121 us -> 121 us (level)
  no operation moved by 1% of the time
where the time goes in v5:
time: 121 us; the launch traced here: 120 us
  Pallas kernels  38.8 us (32%)
  waiting for transfers between devices  33.8 us (28%)
  starting transfers between devices  22.4 us (19%)
  local copies, waits for them, and re-layouts  19.1 us (16%)
  other arithmetic  4.21 us (3%)
  between operations  2.22 us (2%)
    pallas_call x11, Pallas kernels, call(): pl.pallas_call(kernel, in_specs=[SMEM] * len(smalls) + [VMEM] * len(array...  38.8 us
    ppermute x14, waiting for transfers between devices, send(): return lax.ppermute(block, AXES, route)  33.8 us
    ppermute x14, starting transfers between devices, send(): return lax.ppermute(block, AXES, route)  22.4 us
    unnamed x46, local copies, waits for them, and re-layouts  16.9 us
    concatenate x2, other arithmetic, body(): jnp.concatenate([images, jnp.pad(code, ((0, CARRY - 2), (0, WIDTH - ROWS)...  3.4 us
  transfers between devices with their start and end apart: 14, of which 9 were waited for; matrix products, arithmetic and copies ran while one was open for 3% of the time, Pallas kernels for 28%

profile of v5, /device:TPU:0, one launch (start us, length us, event | category | flops | bytes accessed | tf_op | source)
XLA Modules:
  0.0 120.5 jit_solution(8038643845994809356)
XLA Ops:
  0.6 0.8 fusion.7
  1.5 1.5 %pad_maximum_fusion.refs_0_ = bf16[528,1152]{1,0:T(8,128)(2,1)S(1)} fusion(bf16[16,1152]{1,0:T(8,128)(2,1)S(1)} %fusion.6, bf16[512,1152]{1,0:T(8,128)(2,1)} %param.5), kind=kLoop, calls=%fused_computation.1 | loop fusion | flops 2433024 | bytes 2433024 | tf_op jit(solution)/shard_map/concatenate | solution.py:202
  3.0 0.1 collective-permute-start
  3.1 1.0 slice.12
  4.1 4.1 %collective-permute-start.1 = (bf16[256,1152]{1,0:T(8,128)(2,1)}, bf16[256,1152]{1,0:T(8,128)(2,1)}, u32[]{:S(2)}, u32[]{:S(2)}) collective-permute-start(bf16[256,1152]{1,0:T(8,128)(2,1)} %slice.12), channel_id=1, source_target_pairs={{0,12},{1,13},{2,14},{3,15},{4,0},{5,1},{6,2},{7,3},{8,4},{9,5},{1... | collective-permute-start | bytes 1769480 | tf_op jit(solution)/shard_map/ppermute | solution.py:43
  8.2 1.1 fusion.10
  9.3 3.0 %collective-permute-start.2 = (bf16[256,1152]{1,0:T(8,128)(2,1)}, bf16[256,1152]{1,0:T(8,128)(2,1)S(1)}, u32[]{:S(2)}, u32[]{:S(2)}) collective-permute-start(bf16[256,1152]{1,0:T(8,128)(2,1)} %get-tuple-element.64), channel_id=1, source_target_pairs={{0,2},{1,3},{2,0},{3,1},{4,6},{5,7},{6,4},{7,5},{8,10},{9,11},{10,... | collective-permute-start | bytes 1769480 | tf_op jit(solution)/shard_map/ppermute | solution.py:43
  13.7 1.9 %fusion = bf16[272,1152]{1,0:T(8,128)(2,1)} fusion(bf16[512,1152]{1,0:T(8,128)(2,1)} %param.5, bf16[16,1152]{1,0:T(8,128)(2,1)S(1)} %fusion.6), kind=kLoop, calls=%fused_computation.3 | loop fusion | flops 1253376 | bytes 1843200 | tf_op jit(solution)/shard_map/concatenate | solution.py:202
  15.7 1.0 copy-done.4
  16.7 1.3 %copy-done.5 = bf16[528,1152]{1,0:T(8,128)(2,1)S(1)} copy-done((bf16[528,1152]{1,0:T(8,128)(2,1)S(1)}, bf16[528,1152]{1,0:T(8,128)(2,1)}, u32[]{:S(2)}) %copy-start.5) | copy-done | bytes 1216536
  18.0 1.3 %copy-done.9 = bf16[512,1152]{1,0:T(8,128)(2,1)S(1)} copy-done((bf16[512,1152]{1,0:T(8,128)(2,1)S(1)}, bf16[512,1152]{1,0:T(8,128)(2,1)}, u32[]{:S(2)}) %copy-start.9) | copy-done | bytes 1179672
  19.3 6.2 %shard_map.76 = (f32[520,1152]{1,0:T(8,128)S(1)}, f32[520,1152]{1,0:T(8,128)}, f32[512,1152]{1,0:T(8,128)S(1)}) custom-call(f32[1]{0:T(128)} %bitcast.3.start_ref, f32[1]{0:T(128)S(6)} %copy.26.scale_ref, f32[1]{0:T(128)S(6)} %copy.27.offset_ref, bf16[528,1152]{1,0:T(8,128)(2,1)S(1)} %copy-done.1, bf16[528,1152]{1,0:T(8,128)(2,1)S(1)} %copy-done.5, ...), custom_call_target="tpu_custom_call" | custom-call | flops 1000 | bytes 1000 | tf_op jit(solution)/shard_map/pallas_call | solution.py:73
  25.4 1.4 %copy-done.11 = f32[512,1152]{1,0:T(8,128)} copy-done((f32[512,1152]{1,0:T(8,128)}, f32[512,1152]{1,0:T(8,128)S(1)}, u32[]{:S(2)}) %copy-start.11) | copy-done | bytes 2359320
  26.9 3.3 %collective-permute-start.4 = (bf16[272,1152]{1,0:T(8,128)(2,1)}, bf16[272,1152]{1,0:T(8,128)(2,1)}, u32[]{:S(2)}, u32[]{:S(2)}) collective-permute-start(bf16[272,1152]{1,0:T(8,128)(2,1)} %fusion), channel_id=1, source_target_pairs={{0,124},{1,125},{2,126},{3,127},{4,0},{5,1},{6,2},{7,3},{8,4},{9,5... | collective-permute-start | bytes 1880072 | tf_op jit(solution)/shard_map/ppermute | solution.py:43
  30.1 1.5 %collective-permute-start.3 = (bf16[256,1152]{1,0:T(8,128)(2,1)}, bf16[256,1152]{1,0:T(8,128)(2,1)}, u32[]{:S(2)}, u32[]{:S(2)}) collective-permute-start(bf16[256,1152]{1,0:T(8,128)(2,1)} %collective-permute-done.1.first), channel_id=1, source_target_pairs={{12,124},{13,125},{14,126},{15,127},{28,12},{29,13},{30,14},{31,15... | collective-permute-start | bytes 1769480 | tf_op jit(solution)/shard_map/ppermute | solution.py:43
  31.6 1.3 %copy-done.2 = bf16[528,1152]{1,0:T(8,128)(2,1)S(1)} copy-done((bf16[528,1152]{1,0:T(8,128)(2,1)S(1)}, bf16[528,1152]{1,0:T(8,128)(2,1)}, u32[]{:S(2)}) %copy-start.2) | copy-done | bytes 1216536
  32.9 1.3 %copy-done.6 = bf16[528,1152]{1,0:T(8,128)(2,1)S(1)} copy-done((bf16[528,1152]{1,0:T(8,128)(2,1)S(1)}, bf16[528,1152]{1,0:T(8,128)(2,1)}, u32[]{:S(2)}) %copy-start.6) | copy-done | bytes 1216536
  34.2 6.1 %shard_map.77 = (f32[520,1152]{1,0:T(8,128)S(1)}, f32[520,1152]{1,0:T(8,128)}, f32[256,1152]{1,0:T(8,128)S(1)}) custom-call(f32[1]{0:T(128)} %bitcast.1.start_ref, f32[1]{0:T(128)S(6)} %copy.26.scale_ref, f32[1]{0:T(128)S(6)} %copy.27.offset_ref, bf16[528,1152]{1,0:T(8,128)(2,1)S(1)} %copy-done.2, ...), custom_call_target="tpu_custom_call", output_to_operand_aliasing={{0}: (6, {}), {1}: (7, {})} | custom-call | flops 1000 | bytes 1000 | tf_op jit(solution)/shard_map/pallas_call | solution.py:73
  40.3 3.0 %collective-permute-done.4.rest = bf16[272,1152]{1,0:T(8,128)(2,1)} collective-permute-done((bf16[272,1152]{1,0:T(8,128)(2,1)}, bf16[272,1152]{1,0:T(8,128)(2,1)}, u32[]{:S(2)}, u32[]{:S(2)}) %collective-permute-start.4) | collective-permute-done | bytes 626720 | tf_op jit(solution)/shard_map/ppermute | solution.py:43
  43.4 1.7 %shard_map.78.refs_0_.refs_2_ = bf16[528,1152]{1,0:T(8,128)(2,1)S(1)} custom-call(s32[1]{0:T(128)} %bitcast.2.flag_ref, bf16[256,1152]{1,0:T(8,128)(2,1)} %collective-permute-done.1.first, bf16[256,1152]{1,0:T(8,128)(2,1)} %collective-permute-done.3.turned, bf16[272,1152]{1,0:T(8,128)(2,1)} %collective-permute-done.4.rest), custom_call_target="tpu_custom_call" | custom-call | flops 1000 | bytes 1000 | tf_op jit(solution)/shard_map/pallas_call | solution.py:73
  45.1 0.1 collective-permute-start.5
  45.2 2.8 %collective-permute-start.6 = (bf16[256,1152]{1,0:T(8,128)(2,1)S(1)}, bf16[256,1152]{1,0:T(8,128)(2,1)S(1)}, u32[]{:S(2)}, u32[]{:S(2)}) collective-permute-start(bf16[256,1152]{1,0:T(8,128)(2,1)S(1)} %copy-done.22), channel_id=1, source_target_pairs={{0,2},{1,3},{2,0},{3,1},{4,6},{5,7},{6,4},{7,5},{8,10},{9,11},{10,... | collective-permute-start | bytes 1769480 | tf_op jit(solution)/shard_map/ppermute | solution.py:43
  48.0 6.0 %shard_map.79 = (f32[520,1152]{1,0:T(8,128)S(1)}, f32[520,1152]{1,0:T(8,128)S(1)}, f32[512,1152]{1,0:T(8,128)S(1)}) custom-call(f32[1]{0:T(128)} %bitcast.3.start_ref, f32[1]{0:T(128)S(6)} %copy.26.scale_ref, f32[1]{0:T(128)S(6)} %copy.27.offset_ref, bf16[528,1152]{1,0:T(8,128)(2,1)S(1)} %shard_map.78.refs_0_.refs_2_, ...), custom_call_target="tpu_custom_call" | custom-call | flops 1000 | bytes 1000 | tf_op jit(solution)/shard_map/pallas_call | solution.py:73
  54.1 3.7 %shard_map.80 = (f32[520,1152]{1,0:T(8,128)S(1)}, f32[520,1152]{1,0:T(8,128)S(1)}, bf16[256,1152]{1,0:T(8,128)(2,1)S(1)}) custom-call(f32[1]{0:T(128)} %bitcast.1.start_ref, f32[1]{0:T(128)S(6)} %copy.26.scale_ref, f32[1]{0:T(128)S(6)} %copy.27.offset_ref, ...), custom_call_target="tpu_custom_call", output_to_operand_aliasing={{0}: (6, {}), {1}: (7, {})} | custom-call | flops 1000 | bytes 1000 | tf_op jit(solution)/shard_map/pallas_call | solution.py:73
  57.9 2.8 %collective-permute-start.7 = (bf16[256,1152]{1,0:T(8,128)(2,1)S(1)}, bf16[256,1152]{1,0:T(8,128)(2,1)S(1)}, u32[]{:S(2)}, u32[]{:S(2)}) collective-permute-start(bf16[256,1152]{1,0:T(8,128)(2,1)S(1)} %get-tuple-element.50), channel_id=1, source_target_pairs={{0,2},{1,3},{2,0},{3,1},{4,6},{5,7},{6,4},{7,5},{8,10},{9,11},{10,... | collective-permute-start | bytes 1769480 | tf_op jit(solution)/shard_map/ppermute | solution.py:43
  60.7 1.7 %collective-permute-done.6.refs_4_ = bf16[256,1152]{1,0:T(8,128)(2,1)S(1)} collective-permute-done((bf16[256,1152]{1,0:T(8,128)(2,1)S(1)}, bf16[256,1152]{1,0:T(8,128)(2,1)S(1)}, u32[]{:S(2)}, u32[]{:S(2)}) %collective-permute-start.6) | collective-permute-done | bytes 589856 | tf_op jit(solution)/shard_map/ppermute | solution.py:43
  62.4 7.8 %shard_map.81 = (f32[520,1152]{1,0:T(8,128)S(1)}, f32[520,1152]{1,0:T(8,128)}, f32[520,1152]{1,0:T(8,128)S(1)}, bf16[528,1152]{1,0:T(8,128)(2,1)S(1)}, bf16[256,1152]{1,0:T(8,128)(2,1)S(1)}) custom-call(f32[1]{0:T(128)S(6)} %add.25.start_ref, f32[1]{0:T(128)S(6)} %copy.26.scale_ref, ...), custom_call_target="tpu_custom_call", output_to_operand_aliasing={{0}: (8, {}), {1}: (9, {}), {2}: (10, {})} | custom-call | flops 1000 | bytes 1000 | tf_op jit(solution)/shard_map/pallas_call | solution.py:73
  70.2 4.8 %collective-permute-done.7.back1 = bf16[256,1152]{1,0:T(8,128)(2,1)S(1)} collective-permute-done((bf16[256,1152]{1,0:T(8,128)(2,1)S(1)}, bf16[256,1152]{1,0:T(8,128)(2,1)S(1)}, u32[]{:S(2)}, u32[]{:S(2)}) %collective-permute-start.7) | collective-permute-done | bytes 589856 | tf_op jit(solution)/shard_map/ppermute | solution.py:43
  75.0 2.9 %collective-permute-done.8.other = bf16[528,1152]{1,0:T(8,128)(2,1)S(1)} collective-permute-done((bf16[528,1152]{1,0:T(8,128)(2,1)S(1)}, bf16[528,1152]{1,0:T(8,128)(2,1)S(1)}, u32[]{:S(2)}, u32[]{:S(2)}) %collective-permute-start.8) | collective-permute-done | bytes 1216544 | tf_op jit(solution)/shard_map/ppermute | solution.py:43
  77.9 1.0 shard_map.82
  79.0 0.1 collective-permute-start.9
  79.1 2.5 %collective-permute-start.11 = (bf16[256,1152]{1,0:T(8,128)(2,1)S(1)}, bf16[256,1152]{1,0:T(8,128)(2,1)S(1)}, u32[]{:S(2)}, u32[]{:S(2)}) collective-permute-start(bf16[256,1152]{1,0:T(8,128)(2,1)S(1)} %get-tuple-element.54), channel_id=1, source_target_pairs={{0,2},{1,3},{2,0},{3,1},{4,6},{5,7},{6,4},{7,5},{8,10},{9,11},{10,... | collective-permute-start | bytes 1769480 | tf_op jit(solution)/shard_map/ppermute | solution.py:43
  81.7 14.6 %collective-permute-done.11.back2 = bf16[256,1152]{1,0:T(8,128)(2,1)S(1)} collective-permute-done((bf16[256,1152]{1,0:T(8,128)(2,1)S(1)}, bf16[256,1152]{1,0:T(8,128)(2,1)S(1)}, u32[]{:S(2)}, u32[]{:S(2)}) %collective-permute-start.11) | collective-permute-done | bytes 589856 | tf_op jit(solution)/shard_map/ppermute | solution.py:43
  96.2 0.8 copy-done.19
  97.0 1.3 %collective-permute-done.10.first = bf16[256,1152]{1,0:T(8,128)(2,1)} collective-permute-done((bf16[256,1152]{1,0:T(8,128)(2,1)S(1)}, bf16[256,1152]{1,0:T(8,128)(2,1)}, u32[]{:S(2)}, u32[]{:S(2)}) %collective-permute-start.10) | collective-permute-done | bytes 589856 | tf_op jit(solution)/shard_map/ppermute | solution.py:43
  98.3 1.9 %collective-permute-start.12 = (bf16[256,1152]{1,0:T(8,128)(2,1)}, bf16[256,1152]{1,0:T(8,128)(2,1)}, u32[]{:S(2)}, u32[]{:S(2)}) collective-permute-start(bf16[256,1152]{1,0:T(8,128)(2,1)} %collective-permute-done.10.first), channel_id=1, source_target_pairs={{0,16},{1,17},{2,18},{3,19},{16,32},{17,33},{18,34},{19,35},{32,48... | collective-permute-start | bytes 1769480 | tf_op jit(solution)/shard_map/ppermute | solution.py:43
  100.3 1.7 %copy-done.12 = f32[512,1152]{1,0:T(8,128)S(1)} copy-done((f32[512,1152]{1,0:T(8,128)S(1)}, f32[512,1152]{1,0:T(8,128)}, u32[]{:S(2)}) %copy-start.12) | copy-done | bytes 2359320
  101.9 1.7 %copy-done.16 = f32[512,1152]{1,0:T(8,128)S(1)} copy-done((f32[512,1152]{1,0:T(8,128)S(1)}, f32[512,1152]{1,0:T(8,128)}, u32[]{:S(2)}) %copy-start.16) | copy-done | bytes 2359320
  103.6 0.4 shard_map.85.mine
  104.0 1.4 %copy-done.13 = f32[512,1152]{1,0:T(8,128)} copy-done((f32[512,1152]{1,0:T(8,128)}, f32[512,1152]{1,0:T(8,128)S(1)}, u32[]{:S(2)}) %copy-start.13) | copy-done | bytes 2359320
  105.4 1.7 %copy-done.14 = f32[512,1152]{1,0:T(8,128)S(1)} copy-done((f32[512,1152]{1,0:T(8,128)S(1)}, f32[512,1152]{1,0:T(8,128)}, u32[]{:S(2)}) %copy-start.14) | copy-done | bytes 2359320
  107.1 1.1 copy-done.18
  108.1 1.1 copy-done.20
  109.2 1.2 %shard_map.86 = bf16[512,1152]{1,0:T(8,128)(2,1)} custom-call(f32[512,1152]{1,0:T(8,128)S(1)} %copy-done.14, bf16[256,1152]{1,0:T(8,128)(2,1)S(1)} %copy-done.18, bf16[256,1152]{1,0:T(8,128)(2,1)S(1)} %copy-done.20), custom_call_target="tpu_custom_call" | custom-call | flops 1000 | bytes 1000 | tf_op jit(solution)/shard_map/pallas_call | solution.py:73
  110.4 2.1 %shard_map.83.mine = f32[520,1152]{1,0:T(8,128)S(1)} custom-call(f32[520,1152]{1,0:T(8,128)S(1)} %get-tuple-element.46.one, f32[520,1152]{1,0:T(8,128)} %collective-permute-done.9.two), custom_call_target="tpu_custom_call", output_to_operand_aliasing={{}: (0, {})} | custom-call | flops 1000 | bytes 1000 | tf_op jit(solution)/shard_map/pallas_call | solution.py:73
  112.5 4.8 %collective-permute-done.12.turned = bf16[256,1152]{1,0:T(8,128)(2,1)} collective-permute-done((bf16[256,1152]{1,0:T(8,128)(2,1)}, bf16[256,1152]{1,0:T(8,128)(2,1)}, u32[]{:S(2)}, u32[]{:S(2)}) %collective-permute-start.12) | collective-permute-done | bytes 589856 | tf_op jit(solution)/shard_map/ppermute | solution.py:43
  117.3 0.7 collective-permute-done.13.rest
  118.0 2.5 %shard_map.84 = (bf16[512,1152]{1,0:T(8,128)(2,1)}, f32[1,512]{1,0:T(1,128)}) custom-call(s32[1]{0:T(128)} %bitcast.flag_ref, f32[520,1152]{1,0:T(8,128)S(1)} %shard_map.83.mine, bf16[256,1152]{1,0:T(8,128)(2,1)} %collective-permute-done.10.first, bf16[256,1152]{1,0:T(8,128)(2,1)} %collective-permute-done.12.turned, ...), custom_call_target="tpu_custom_call" | custom-call | flops 1000 | bytes 1000 | tf_op jit(solution)/shard_map/pallas_call | solution.py:73
  (45 shorter events, 0.2 us)
Async XLA Ops:
  0.6 2.4 %copy-start.21 = (bf16[512,1152]{1,0:T(8,128)(2,1)S(1)}, bf16[512,1152]{1,0:T(8,128)(2,1)}, u32[]{:S(2)}) copy-start(bf16[512,1152]{1,0:T(8,128)(2,1)} %param.5) | copy-start | bytes 3538948
  1.5 6.7 %copy-start.8 = (bf16[512,1152]{1,0:T(8,128)(2,1)S(1)}, bf16[512,1152]{1,0:T(8,128)(2,1)}, u32[]{:S(2)}) copy-start(bf16[512,1152]{1,0:T(8,128)(2,1)} %refs_2_.3) | copy-start | bytes 3538948
  2.9 6.4 %copy-start = (bf16[528,1152]{1,0:T(8,128)(2,1)}, bf16[528,1152]{1,0:T(8,128)(2,1)S(1)}, u32[]{:S(2)}) copy-start(bf16[528,1152]{1,0:T(8,128)(2,1)S(1)} %pad_maximum_fusion.refs_0_) | copy-start | bytes 3649540
  3.0 12.7 %collective-permute-start = (bf16[528,1152]{1,0:T(8,128)(2,1)S(1)}, bf16[528,1152]{1,0:T(8,128)(2,1)S(1)}, u32[]{:S(2)}, u32[]{:S(2)}) collective-permute-start(bf16[528,1152]{1,0:T(8,128)(2,1)S(1)} %pad_maximum_fusion.refs_0_), channel_id=1, source_target_pairs={{0,1},{1,0},{2,3},{3,2},{4,5},{5,4},{6,7},{7,6},{8,9},{9,8},{10,11... | collective-permute-start | bytes 3649544 | tf_op jit(solution)/shard_map/ppermute | solution.py:43
  4.1 22.8 %collective-permute-start.1 = (bf16[256,1152]{1,0:T(8,128)(2,1)}, bf16[256,1152]{1,0:T(8,128)(2,1)}, u32[]{:S(2)}, u32[]{:S(2)}) collective-permute-start(bf16[256,1152]{1,0:T(8,128)(2,1)} %slice.12), channel_id=1, source_target_pairs={{0,12},{1,13},{2,14},{3,15},{4,0},{5,1},{6,2},{7,3},{8,4},{9,5},{1... | collective-permute-start | bytes 1769480 | tf_op jit(solution)/shard_map/ppermute | solution.py:43
  9.3 17.5 %collective-permute-start.2 = (bf16[256,1152]{1,0:T(8,128)(2,1)}, bf16[256,1152]{1,0:T(8,128)(2,1)S(1)}, u32[]{:S(2)}, u32[]{:S(2)}) collective-permute-start(bf16[256,1152]{1,0:T(8,128)(2,1)} %get-tuple-element.64), channel_id=1, source_target_pairs={{0,2},{1,3},{2,0},{3,1},{4,6},{5,7},{6,4},{7,5},{8,10},{9,11},{10,... | collective-permute-start | bytes 1769480 | tf_op jit(solution)/shard_map/ppermute | solution.py:43
  12.3 4.4 %copy-start.1 = (bf16[528,1152]{1,0:T(8,128)(2,1)S(1)}, bf16[528,1152]{1,0:T(8,128)(2,1)}, u32[]{:S(2)}) copy-start(bf16[528,1152]{1,0:T(8,128)(2,1)} %copy-done) | copy-start | bytes 3649540
  15.7 1.0 copy-start.4
  16.7 1.3 %copy-start.5 = (bf16[528,1152]{1,0:T(8,128)(2,1)S(1)}, bf16[528,1152]{1,0:T(8,128)(2,1)}, u32[]{:S(2)}) copy-start(bf16[528,1152]{1,0:T(8,128)(2,1)} %copy-done.4) | copy-start | bytes 3649540
  18.0 1.3 %copy-start.9 = (bf16[512,1152]{1,0:T(8,128)(2,1)S(1)}, bf16[512,1152]{1,0:T(8,128)(2,1)}, u32[]{:S(2)}) copy-start(bf16[512,1152]{1,0:T(8,128)(2,1)} %refs_2_.3) | copy-start | bytes 3538948
  25.4 1.4 %copy-start.11 = (f32[512,1152]{1,0:T(8,128)}, f32[512,1152]{1,0:T(8,128)S(1)}, u32[]{:S(2)}) copy-start(f32[512,1152]{1,0:T(8,128)S(1)} %get-tuple-element.61.one) | copy-start | bytes 7077892
  26.9 16.5 %collective-permute-start.4 = (bf16[272,1152]{1,0:T(8,128)(2,1)}, bf16[272,1152]{1,0:T(8,128)(2,1)}, u32[]{:S(2)}, u32[]{:S(2)}) collective-permute-start(bf16[272,1152]{1,0:T(8,128)(2,1)} %fusion), channel_id=1, source_target_pairs={{0,124},{1,125},{2,126},{3,127},{4,0},{5,1},{6,2},{7,3},{8,4},{9,5... | collective-permute-start | bytes 1880072 | tf_op jit(solution)/shard_map/ppermute | solution.py:43
  30.1 10.2 %collective-permute-start.3 = (bf16[256,1152]{1,0:T(8,128)(2,1)}, bf16[256,1152]{1,0:T(8,128)(2,1)}, u32[]{:S(2)}, u32[]{:S(2)}) collective-permute-start(bf16[256,1152]{1,0:T(8,128)(2,1)} %collective-permute-done.1.first), channel_id=1, source_target_pairs={{12,124},{13,125},{14,126},{15,127},{28,12},{29,13},{30,14},{31,15... | collective-permute-start | bytes 1769480 | tf_op jit(solution)/shard_map/ppermute | solution.py:43
  31.6 1.3 %copy-start.2 = (bf16[528,1152]{1,0:T(8,128)(2,1)S(1)}, bf16[528,1152]{1,0:T(8,128)(2,1)}, u32[]{:S(2)}) copy-start(bf16[528,1152]{1,0:T(8,128)(2,1)} %copy-done) | copy-start | bytes 3649540
  32.9 1.3 %copy-start.6 = (bf16[528,1152]{1,0:T(8,128)(2,1)S(1)}, bf16[528,1152]{1,0:T(8,128)(2,1)}, u32[]{:S(2)}) copy-start(bf16[528,1152]{1,0:T(8,128)(2,1)} %copy-done.4) | copy-start | bytes 3649540
  43.4 1.8 %copy-start.22 = (bf16[256,1152]{1,0:T(8,128)(2,1)S(1)}, bf16[256,1152]{1,0:T(8,128)(2,1)}, u32[]{:S(2)}) copy-start(bf16[256,1152]{1,0:T(8,128)(2,1)} %get-tuple-element.39) | copy-start | bytes 1769476
  43.4 4.7 %copy-start.10 = (bf16[512,1152]{1,0:T(8,128)(2,1)S(1)}, bf16[512,1152]{1,0:T(8,128)(2,1)}, u32[]{:S(2)}) copy-start(bf16[512,1152]{1,0:T(8,128)(2,1)} %refs_2_.3) | copy-start | bytes 3538948
  45.1 3.0 %collective-permute-start.5 = (bf16[528,1152]{1,0:T(8,128)(2,1)S(1)}, bf16[528,1152]{1,0:T(8,128)(2,1)S(1)}, u32[]{:S(2)}, u32[]{:S(2)}) collective-permute-start(bf16[528,1152]{1,0:T(8,128)(2,1)S(1)} %shard_map.78.refs_0_.refs_2_), channel_id=1, source_target_pairs={{0,1},{1,0},{2,3},{3,2},{4,5},{5,4},{6,7},{7,6},{8,9},{9,8},{10,11... | collective-permute-start | bytes 3649544 | tf_op jit(solution)/shard_map/ppermute | solution.py:43
  45.2 17.2 %collective-permute-start.6 = (bf16[256,1152]{1,0:T(8,128)(2,1)S(1)}, bf16[256,1152]{1,0:T(8,128)(2,1)S(1)}, u32[]{:S(2)}, u32[]{:S(2)}) collective-permute-start(bf16[256,1152]{1,0:T(8,128)(2,1)S(1)} %copy-done.22), channel_id=1, source_target_pairs={{0,2},{1,3},{2,0},{3,1},{4,6},{5,7},{6,4},{7,5},{8,10},{9,11},{10,... | collective-permute-start | bytes 1769480 | tf_op jit(solution)/shard_map/ppermute | solution.py:43
  54.1 3.8 %copy-start.15 = (f32[512,1152]{1,0:T(8,128)}, f32[512,1152]{1,0:T(8,128)S(1)}, u32[]{:S(2)}) copy-start(f32[512,1152]{1,0:T(8,128)S(1)} %get-tuple-element.62.two) | copy-start | bytes 7077892
  54.1 8.3 %copy-start.3 = (bf16[528,1152]{1,0:T(8,128)(2,1)S(1)}, bf16[528,1152]{1,0:T(8,128)(2,1)}, u32[]{:S(2)}) copy-start(bf16[528,1152]{1,0:T(8,128)(2,1)} %copy-done) | copy-start | bytes 3649540
  54.1 8.3 %copy-start.7 = (bf16[528,1152]{1,0:T(8,128)(2,1)S(1)}, bf16[528,1152]{1,0:T(8,128)(2,1)}, u32[]{:S(2)}) copy-start(bf16[528,1152]{1,0:T(8,128)(2,1)} %copy-done.4) | copy-start | bytes 3649540
  57.9 17.2 %collective-permute-start.7 = (bf16[256,1152]{1,0:T(8,128)(2,1)S(1)}, bf16[256,1152]{1,0:T(8,128)(2,1)S(1)}, u32[]{:S(2)}, u32[]{:S(2)}) collective-permute-start(bf16[256,1152]{1,0:T(8,128)(2,1)S(1)} %get-tuple-element.50), channel_id=1, source_target_pairs={{0,2},{1,3},{2,0},{3,1},{4,6},{5,7},{6,4},{7,5},{8,10},{9,11},{10,... | collective-permute-start | bytes 1769480 | tf_op jit(solution)/shard_map/ppermute | solution.py:43
  75.0 3.9 %copy-start.17 = (bf16[256,1152]{1,0:T(8,128)(2,1)}, bf16[256,1152]{1,0:T(8,128)(2,1)S(1)}, u32[]{:S(2)}) copy-start(bf16[256,1152]{1,0:T(8,128)(2,1)S(1)} %collective-permute-done.7.back1) | copy-start | bytes 1769476
  75.0 2.9 %collective-permute-start.8 = (bf16[528,1152]{1,0:T(8,128)(2,1)S(1)}, bf16[528,1152]{1,0:T(8,128)(2,1)S(1)}, u32[]{:S(2)}, u32[]{:S(2)}) collective-permute-start(bf16[528,1152]{1,0:T(8,128)(2,1)S(1)} %get-tuple-element.51), channel_id=1, source_target_pairs={{0,1},{1,0},{2,3},{3,2},{4,5},{5,4},{6,7},{7,6},{8,9},{9,8},{10,11... | collective-permute-start | bytes 3649544 | tf_op jit(solution)/shard_map/ppermute | solution.py:43
  79.0 31.4 %collective-permute-start.9 = (f32[520,1152]{1,0:T(8,128)}, f32[520,1152]{1,0:T(8,128)}, u32[]{:S(2)}, u32[]{:S(2)}) collective-permute-start(f32[520,1152]{1,0:T(8,128)} %get-tuple-element.53), channel_id=1, source_target_pairs={{0,1},{1,0},{2,3},{3,2},{4,5},{5,4},{6,7},{7,6},{8,9},{9,8},{10,11... | collective-permute-start | bytes 7188488 | tf_op jit(solution)/shard_map/ppermute | solution.py:43
  79.1 17.1 %collective-permute-start.11 = (bf16[256,1152]{1,0:T(8,128)(2,1)S(1)}, bf16[256,1152]{1,0:T(8,128)(2,1)S(1)}, u32[]{:S(2)}, u32[]{:S(2)}) collective-permute-start(bf16[256,1152]{1,0:T(8,128)(2,1)S(1)} %get-tuple-element.54), channel_id=1, source_target_pairs={{0,2},{1,3},{2,0},{3,1},{4,6},{5,7},{6,4},{7,5},{8,10},{9,11},{10,... | collective-permute-start | bytes 1769480 | tf_op jit(solution)/shard_map/ppermute | solution.py:43
  81.7 16.6 %collective-permute-start.10 = (bf16[256,1152]{1,0:T(8,128)(2,1)S(1)}, bf16[256,1152]{1,0:T(8,128)(2,1)}, u32[]{:S(2)}, u32[]{:S(2)}) collective-permute-start(bf16[256,1152]{1,0:T(8,128)(2,1)S(1)} %get-tuple-element.52), channel_id=1, source_target_pairs={{0,4},{1,5},{2,6},{3,7},{4,8},{5,9},{6,10},{7,11},{8,12},{9,13},{1... | collective-permute-start | bytes 1769480 | tf_op jit(solution)/shard_map/ppermute | solution.py:43
  96.2 0.8 copy-start.19
  98.3 19.7 %collective-permute-start.13 = (bf16[272,1152]{1,0:T(8,128)(2,1)}, bf16[272,1152]{1,0:T(8,128)(2,1)S(1)}, u32[]{:S(2)}, u32[]{:S(2)}) collective-permute-start(bf16[272,1152]{1,0:T(8,128)(2,1)} %get-tuple-element.57), channel_id=1, source_target_pairs={{0,4},{1,5},{2,6},{3,7},{4,8},{5,9},{6,10},{7,11},{8,12},{9,13},{1... | collective-permute-start | bytes 1880072 | tf_op jit(solution)/shard_map/ppermute | solution.py:43
  98.3 19.0 %collective-permute-start.12 = (bf16[256,1152]{1,0:T(8,128)(2,1)}, bf16[256,1152]{1,0:T(8,128)(2,1)}, u32[]{:S(2)}, u32[]{:S(2)}) collective-permute-start(bf16[256,1152]{1,0:T(8,128)(2,1)} %collective-permute-done.10.first), channel_id=1, source_target_pairs={{0,16},{1,17},{2,18},{3,19},{16,32},{17,33},{18,34},{19,35},{32,48... | collective-permute-start | bytes 1769480 | tf_op jit(solution)/shard_map/ppermute | solution.py:43
  100.2 1.7 %copy-start.12 = (f32[512,1152]{1,0:T(8,128)S(1)}, f32[512,1152]{1,0:T(8,128)}, u32[]{:S(2)}) copy-start(f32[512,1152]{1,0:T(8,128)} %copy-done.11) | copy-start | bytes 7077892
  101.9 1.7 %copy-start.16 = (f32[512,1152]{1,0:T(8,128)S(1)}, f32[512,1152]{1,0:T(8,128)}, u32[]{:S(2)}) copy-start(f32[512,1152]{1,0:T(8,128)} %copy-done.15) | copy-start | bytes 7077892
  104.0 1.4 %copy-start.13 = (f32[512,1152]{1,0:T(8,128)}, f32[512,1152]{1,0:T(8,128)S(1)}, u32[]{:S(2)}) copy-start(f32[512,1152]{1,0:T(8,128)S(1)} %shard_map.85.mine) | copy-start | bytes 7077892
  105.4 1.7 %copy-start.14 = (f32[512,1152]{1,0:T(8,128)S(1)}, f32[512,1152]{1,0:T(8,128)}, u32[]{:S(2)}) copy-start(f32[512,1152]{1,0:T(8,128)} %copy-done.13) | copy-start | bytes 7077892
  107.1 1.1 copy-start.18
  108.1 1.1 copy-start.20
